TPU v7x, 32 devices: a whole 2x2x4 slice. The times are simulated.
32 devices in a mesh: dp: 4 (over x, core), ctx: 8 (over z, y).
Axes of the slice: x: 2, y: 2, z: 4, core: 2. Of those that a mesh axis runs over, the one named last changes fastest.
Arguments:
- tile_embed: bfloat16 [4, 8, 512, 1536], P(None, 'ctx', 'dp'), may hold values from -8 to 8
- tile_counts: int32 [4], replicated, may hold values from 1024 to 4096
- w_in: bfloat16 [1536, 768], replicated, may hold values from -1 to 1
- w_qkv: bfloat16 [768, 2304], replicated, may hold values from -1 to 1
- w_out: bfloat16 [768, 768], replicated, may hold values from -0.21875 to 0.21875
Outputs:
- mixed: bfloat16 [4, 4096, 768], P('dp', 'ctx')
Inputs may be any that keep to these rules, and one draw needn't show every extreme that they name: The tissue tiles of slide s fill its first tile_counts[s] positions; the rest are padding.
All inputs are finite; a program needn't handle non-finite values.
Results may differ from a plain program's by a relative error of at most 0.017.
Values may be sent and summed in bfloat16 or wider, within the bound.
No kernel may reach another device: no remote copies, remote signals or barrier semaphores. Data moves between devices by JAX's collectives and lax.ppermute only.
A program may use at most 128 MiB of HBM per device.

v0:
```python
import math

import jax
import jax.numpy as jnp
from jax import lax
from jax.sharding import PartitionSpec as P

HEAD_TOTAL = 12


epsilon = 1e-05


def normalize(values):
    average = jnp.mean(values, axis=-1, keepdims=True)
    centered = values - average
    variance = jnp.mean(centered * centered, axis=-1, keepdims=True)
    return (centered * lax.rsqrt(variance + epsilon)).astype(jnp.bfloat16)


def attend_rows(qkv, is_valid):
    length = qkv.shape[0]
    model_features = qkv.shape[1] // 3
    head_width = model_features // HEAD_TOTAL
    key_rows = qkv[:, model_features : 2 * model_features].reshape(length, HEAD_TOTAL, head_width)
    values = qkv[:, 2 * model_features :].reshape(length, HEAD_TOTAL, head_width)
    block_rows = min(length, 512)
    queries = qkv[:, :model_features].reshape(
        length // block_rows, block_rows, HEAD_TOTAL, head_width
    )
    key_mask = is_valid[None, None, :]

    def attend_block(query_rows):
        scores = jnp.einsum(
            "qhd,khd->qhk", query_rows, key_rows, preferred_element_type=jnp.float32
        ) * (1.0 / math.sqrt(head_width))
        running_max = jnp.max(jnp.where(key_mask, scores, -1e30), axis=-1)
        weights = jnp.where(key_mask, jnp.exp(scores - running_max[..., None]), 0.0)
        denominator = jnp.sum(weights, axis=-1)
        weighted = jnp.einsum(
            "qhk,khd->qhd", weights.astype(jnp.bfloat16), values, preferred_element_type=jnp.float32
        )
        return (weighted, running_max, denominator)

    weighted, running_max, denominator = lax.map(attend_block, queries)
    return (
        weighted.reshape(length, HEAD_TOTAL, head_width),
        running_max.reshape(length, HEAD_TOTAL),
        denominator.reshape(length, HEAD_TOTAL),
    )


def body(tile_embed, tile_counts, w_in, w_qkv, w_out):
    slide_id = lax.axis_index("dp")
    ctx_index = lax.axis_index("ctx")
    context_count = lax.axis_size("ctx")
    slide_total, unit_dim, sub_rows, embed_width = tile_embed.shape
    row_count = sub_rows * lax.axis_size("dp")
    model_features = w_out.shape[0]
    head_width = model_features // HEAD_TOTAL
    routed = lax.all_to_all(tile_embed, "dp", split_axis=0, concat_axis=2, tiled=True)
    hidden = jnp.dot(
        routed.reshape(row_count, embed_width), w_in, preferred_element_type=jnp.float32
    ).astype(jnp.bfloat16)
    tile_number = lax.dynamic_slice_in_dim(tile_counts, slide_id, 1)[0]
    positions = ctx_index * row_count + jnp.arange(row_count, dtype=jnp.int32)
    is_valid = positions < tile_number
    normed = normalize(hidden.astype(jnp.float32))
    qkv = jnp.dot(normed, w_qkv, preferred_element_type=jnp.float32).astype(jnp.bfloat16)
    local_accumulator, local_maximum, local_total = attend_rows(qkv, is_valid)
    dilation_step = row_count // context_count
    regrouped = lax.all_to_all(
        normed.reshape(dilation_step, context_count, model_features),
        "ctx",
        split_axis=1,
        concat_axis=0,
        tiled=True,
    )
    dilated_branch = jnp.dot(
        regrouped.reshape(row_count, model_features), w_qkv, preferred_element_type=jnp.float32
    ).astype(jnp.bfloat16)
    row_order = jnp.arange(row_count, dtype=jnp.int32)
    dilated_positions = (
        row_order // dilation_step * row_count
        + row_order % dilation_step * context_count
        + ctx_index
    )
    dilated_accumulator, dilated_maximum, dilated_total = attend_rows(
        dilated_branch, dilated_positions < tile_number
    )
    dilated_output = (dilated_accumulator / dilated_total[..., None]).astype(jnp.bfloat16)
    dilated_logsumexp = dilated_maximum + jnp.log(dilated_total)
    restored_output = lax.all_to_all(
        dilated_output.reshape(context_count, dilation_step, 1, model_features),
        "ctx",
        split_axis=0,
        concat_axis=2,
        tiled=True,
    )
    restored_logsumexp = lax.all_to_all(
        dilated_logsumexp.reshape(context_count, dilation_step, 1, HEAD_TOTAL),
        "ctx",
        split_axis=0,
        concat_axis=2,
        tiled=True,
    )
    restored_output = restored_output.reshape(row_count, HEAD_TOTAL, head_width).astype(jnp.float32)
    restored_logsumexp = restored_logsumexp.reshape(row_count, HEAD_TOTAL)
    combined_output = jnp.maximum(local_maximum, restored_logsumexp)
    local_weight = jnp.exp(local_maximum - combined_output)
    dilated_weight = jnp.exp(restored_logsumexp - combined_output)
    attention_fn = (
        local_weight[..., None] * local_accumulator + dilated_weight[..., None] * restored_output
    ) / (local_weight * local_total + dilated_weight)[..., None]
    attention_fn = attention_fn.reshape(row_count, model_features).astype(jnp.bfloat16)
    mixed = jnp.dot(attention_fn, w_out, preferred_element_type=jnp.float32)
    mixed = jnp.where(is_valid[:, None], mixed, 0.0).astype(jnp.bfloat16)
    return mixed.reshape(1, row_count, model_features)


def solution(mesh):
    in_specs = (P(None, "ctx", "dp", None), P(), P(), P(), P())
    out_specs = P("dp", "ctx", None)
    return jax.shard_map(body, mesh=mesh, in_specs=in_specs, out_specs=out_specs, check_vma=False)
```

profile of v0, /device:TPU:0, one launch (start us, length us, event | category | flops | bytes accessed | tf_op | source)
XLA Modules:
  0.0 149.3 jit_solution(3179475871549475662)
XLA Ops:
  0.0 4.6 %all-to-all-start = ((bf16[4,1,128,1536]{3,2,1,0:T(8,128)(2,1)}), bf16[4,1,128,1536]{3,2,1,0:T(8,128)(2,1)}, u32[]{:S(2)}, u32[]{:S(2)}) async-start(bf16[4,1,128,1536]{3,2,1,0:T(8,128)(2,1)} %param.5), calls=%async_computation | async-start | bytes 3145728 | tf_op jit(solution)/shard_map/all_to_all | solution.py:61
  6.5 18.9 %all-to-all-done = bf16[4,1,128,1536]{3,2,1,0:T(8,128)(2,1)} async-done(((bf16[4,1,128,1536]{3,2,1,0:T(8,128)(2,1)}), bf16[4,1,128,1536]{3,2,1,0:T(8,128)(2,1)}, u32[]{:S(2)}, u32[]{:S(2)}) %all-to-all-start) | async-done | bytes 1572896 | tf_op jit(solution)/shard_map/all_to_all | solution.py:61
  25.4 3.6 %convert_reduce_fusion = (f32[512]{0:T(512)S(1)}, bf16[512,768]{1,0:T(8,128)(2,1)S(1)}) fusion(bf16[512,1536]{1,0:T(8,128)(2,1)} %bitcast.1, bf16[1536,768]{1,0:T(8,128)(2,1)} %param.7), kind=kOutput, calls=%fused_computation.21 | convolution fusion | flops 1209138688 | bytes 4720640 | tf_op jit(solution)/shard_map/dot_general | solution.py:62
  31.2 6.6 %all-to-all-start.1 = ((bf16[64,8,768]{2,0,1:T(8,128)(2,1)}), bf16[64,8,768]{2,0,1:T(8,128)(2,1)}, u32[]{:S(2)}, u32[]{:S(2)}) async-start(bf16[64,8,768]{2,0,1:T(8,128)(2,1)} %copy.57), calls=%async_computation.1 | async-start | bytes 1572864 | tf_op jit(solution)/shard_map/all_to_all | solution.py:72
  37.8 3.2 %convolution_convert_fusion.1 = bf16[512,2304]{1,0:T(8,128)(2,1)S(1)} fusion(bf16[768,2304]{1,0:T(8,128)(2,1)S(1)} %copy-done, bf16[512,768]{1,0:T(8,128)(2,1)} %copy-done.2, f32[512]{0:T(512)S(1)} %add_rsqrt_fusion, f32[512]{0:T(512)S(1)} %broadcast_multiply_fusion), kind=kOutput, calls=%fused_computation.19 | convolution fusion | flops 1814691840 | bytes 6688768 | tf_op jit(solution)/shard_map/dot_general | solution.py:69
  42.5 2.3 %copy.55 = bf16[512,768]{0,1:T(8,128)(2,1)} copy(bf16[512,768]{1,0:T(8,128)(2,1)} %get-tuple-element.48) | data formatting | bytes 1572864 | tf_op jit(solution)/shard_map/slice | solution.py:25
  44.8 2.3 %copy.56 = bf16[512,768]{0,1:T(8,128)(2,1)} copy(bf16[512,768]{1,0:T(8,128)(2,1)} %get-tuple-element.38) | data formatting | bytes 1572864 | tf_op jit(solution)/shard_map/slice | solution.py:28
  47.1 9.4 %fusion.3 = (f32[512,12]{0,1:T(8,128)}, f32[12,512,512]{2,1,0:T(8,128)}) fusion(pred[512]{0:T(512)(128)(4,1)S(1)} %add_compare_fusion, bf16[512,12,64]{0,2,1:T(8,128)(2,1)} %bitcast.105, bf16[512,12,64]{0,2,1:T(8,128)(2,1)} %bitcast.106), kind=kOutput, calls=%fused_computation.7 | convolution fusion | flops 412084224 | bytes 14180864 | tf_op jit(solution)/shard_map/while/body/eval_jaxpr/qhd,khd->qhk/dot_general | solution.py:34
  57.9 3.1 %convolution_convert_fusion = bf16[512,2304]{1,0:T(8,128)(2,1)S(1)} fusion(bf16[512,768]{1,0:T(8,128)(2,1)} %bitcast.8, bf16[768,2304]{1,0:T(8,128)(2,1)S(1)} %copy-done), kind=kOutput, calls=%fused_computation.18 | convolution fusion | flops 1813118976 | bytes 6684672 | tf_op jit(solution)/shard_map/dot_general | solution.py:79
  62.6 2.3 %copy.64 = bf16[512,768]{0,1:T(8,128)(2,1)} copy(bf16[512,768]{1,0:T(8,128)(2,1)} %get-tuple-element.50) | data formatting | bytes 1572864 | tf_op jit(solution)/shard_map/slice | solution.py:26
  67.2 2.3 %copy.59 = bf16[512,768]{0,1:T(8,128)(2,1)} copy(bf16[512,768]{1,0:T(8,128)(2,1)} %get-tuple-element.49) | data formatting | bytes 1572864 | tf_op jit(solution)/shard_map/slice | solution.py:28
  69.5 4.5 %fusion = (f32[512,12]{0,1:T(8,128)S(1)}, f32[12,512,512]{2,1,0:T(8,128)S(1)}) fusion(pred[512]{0:T(512)(128)(4,1)S(1)} %fusion.37, bf16[512,12,64]{0,2,1:T(8,128)(2,1)} %bitcast.104, bf16[512,12,64]{0,2,1:T(8,128)(2,1)} %bitcast.107), kind=kOutput, calls=%fused_computation.2 | convolution fusion | flops 412084224 | bytes 14180864 | tf_op jit(solution)/shard_map/while/body/eval_jaxpr/qhd,khd->qhk/dot_general | solution.py:34
  74.0 2.6 %fusion.9 = f32[512,12]{0,1:T(8,128)S(1)} fusion(f32[12,512,512]{2,1,0:T(8,128)S(1)} %get-tuple-element.55, f32[512,12]{0,1:T(8,128)S(1)} %get-tuple-element.54, pred[512]{0:T(512)(128)(4,1)S(1)} %fusion.37), kind=kLoop, calls=%fused_computation.13 | loop fusion | flops 12576768 | bytes 12632576 | tf_op jit(solution)/shard_map/while/body/eval_jaxpr/reduce_sum | solution.py:39
  86.9 4.5 %all-to-all-start.2 = ((f32[8,1,768]{2,1,0:T(1,128)}), f32[8,1,768]{2,1,0:T(1,128)}, u32[]{:S(2)}, u32[]{:S(2)}) async-start(f32[8,1,768]{2,1,0:T(1,128)} %reshape.206), calls=%async_computation.2 | async-start | bytes 49152 | tf_op jit(solution)/shard_map/all_to_all | solution.py:100
  91.4 8.0 %fusion.21 = bf16[512,12,64]{0,2,1:T(8,128)(2,1)} fusion(bf16[512,12,64]{0,2,1:T(8,128)(2,1)} %bitcast.108, f32[12,512,512]{2,1,0:T(8,128)} %copy-done.1, f32[512,12]{0,1:T(8,128)} %copy-done.3, pred[512]{0:T(512)(128)(4,1)S(1)} %fusion.37, f32[512,12]{0,1:T(8,128)} %copy-done.4), kind=kOutput, calls=%fused_computation.30 | convolution fusion | flops 416022528 | bytes 14205440 | tf_op jit(solution)/shard_map/while/body/eval_jaxpr/qhk,khd->qhd/dot_general | solution.py:40
  99.4 3.2 %convert_element_type.63 = bf16[8,64,1,768]{1,0,3,2:T(8,128)(2,1)} reshape(bf16[512,12,64]{0,2,1:T(8,128)(2,1)} %fusion.21) | data formatting | bytes 1572864 | tf_op jit(solution)/shard_map/convert_element_type | solution.py:91
  102.5 2.7 %copy.66 = bf16[8,64,1,768]{3,1,2,0:T(8,128)(2,1)} copy(bf16[8,64,1,768]{1,0,3,2:T(8,128)(2,1)} %convert_element_type.63) | data formatting | bytes 1572864 | tf_op jit(solution)/shard_map/convert_element_type | solution.py:91
  105.2 6.0 %all-to-all-start.3 = ((bf16[8,64,1,768]{3,1,2,0:T(8,128)(2,1)}), bf16[8,64,1,768]{3,1,2,0:T(8,128)(2,1)}, u32[]{:S(2)}, u32[]{:S(2)}) async-start(bf16[8,64,1,768]{3,1,2,0:T(8,128)(2,1)} %copy.66), calls=%async_computation.3 | async-start | bytes 1572864 | tf_op jit(solution)/shard_map/all_to_all | solution.py:93
  111.2 7.7 %fusion.6 = f32[512,12]{0,1:T(8,128)} fusion(f32[12,512,512]{2,1,0:T(8,128)} %get-tuple-element.66, f32[512,12]{0,1:T(8,128)} %get-tuple-element.64, pred[512]{0:T(512)(128)(4,1)S(1)} %add_compare_fusion), kind=kLoop, calls=%fused_computation.10 | loop fusion | flops 12576768 | bytes 12632576 | tf_op jit(solution)/shard_map/while/body/eval_jaxpr/reduce_sum | solution.py:39
  119.0 2.3 %copy.62 = bf16[512,768]{0,1:T(8,128)(2,1)} copy(bf16[512,768]{1,0:T(8,128)(2,1)} %get-tuple-element.39) | data formatting | bytes 1572864 | tf_op jit(solution)/shard_map/slice | solution.py:26
  131.2 8.2 %bitcast_multiply_fusion.1 = f32[512,12,64]{0,2,1:T(8,128)} fusion(bf16[512,12,64]{0,2,1:T(8,128)(2,1)} %bitcast.109, f32[12,512,512]{2,1,0:T(8,128)} %get-tuple-element.66, f32[512,12]{0,1:T(8,128)} %get-tuple-element.64, pred[512]{0:T(512)(128)(4,1)S(1)} %add_compare_fusion, f32[512,12]{0,1:T(8,128)S(1)} %get-tuple-element.37), kind=kOutput, calls=%fused_computation.33 | convolution fusion | flops 415629312 | bytes 14991872 | tf_op jit(solution)/shard_map/while/body/eval_jaxpr/qhk,khd->qhd/dot_general | solution.py:40
  139.4 2.7 %convert_bitcast_fusion = f32[512,768]{1,0:T(8,128)} fusion(bf16[8,64,1,768]{3,1,2,0:T(8,128)(2,1)} %all-to-all-done.3), kind=kLoop, calls=%fused_computation.26 | loop fusion | flops 393216 | bytes 2359296 | tf_op jit(solution)/shard_map/convert_element_type | solution.py:107
  142.1 3.0 %copy.68 = f32[512,768]{0,1:T(8,128)} copy(f32[512,768]{1,0:T(8,128)} %convert_bitcast_fusion) | data formatting | bytes 3145728 | tf_op jit(solution)/shard_map/convert_element_type | solution.py:107
  145.2 2.4 %fusion.20 = bf16[512,768]{0,1:T(8,128)(2,1)S(1)} fusion(f32[512,768]{0,1:T(8,128)} %copy.68, f32[512,12,64]{0,2,1:T(8,128)} %bitcast_multiply_fusion.1, f32[512,12]{0,1:T(8,128)} %get-tuple-element.35, f32[512,12]{0,1:T(8,128)} %get-tuple-element.36), kind=kLoop, calls=%fused_computation.28 | loop fusion | flops 1572864 | bytes 3981312 | tf_op jit(solution)/shard_map/convert_element_type | solution.py:115
  (41 shorter events, 32.6 us)
Async XLA Ops:
  0.0 37.8 %copy-start = (bf16[768,2304]{1,0:T(8,128)(2,1)S(1)}, bf16[768,2304]{1,0:T(8,128)(2,1)}, u32[]{:S(2)}) copy-start(bf16[768,2304]{1,0:T(8,128)(2,1)} %param.8) | copy-start | bytes 10616836
  0.0 4.6 %copy-start.6 = (s32[4]{0:T(128)S(1)}, s32[4]{0:T(128)}, u32[]{:S(2)}) copy-start(s32[4]{0:T(128)} %param.6) | copy-start | bytes 52
  0.0 25.4 %all-to-all-start = ((bf16[4,1,128,1536]{3,2,1,0:T(8,128)(2,1)}), bf16[4,1,128,1536]{3,2,1,0:T(8,128)(2,1)}, u32[]{:S(2)}, u32[]{:S(2)}) async-start(bf16[4,1,128,1536]{3,2,1,0:T(8,128)(2,1)} %param.5), calls=%async_computation | async-start | bytes 3145728 | tf_op jit(solution)/shard_map/all_to_all | solution.py:61
  29.0 0.9 copy-start.2
  31.2 26.8 %all-to-all-start.1 = ((bf16[64,8,768]{2,0,1:T(8,128)(2,1)}), bf16[64,8,768]{2,0,1:T(8,128)(2,1)}, u32[]{:S(2)}, u32[]{:S(2)}) async-start(bf16[64,8,768]{2,0,1:T(8,128)(2,1)} %copy.57), calls=%async_computation.1 | async-start | bytes 1572864 | tf_op jit(solution)/shard_map/all_to_all | solution.py:72
  74.0 4.5 %copy-start.1 = (f32[12,512,512]{2,1,0:T(8,128)}, f32[12,512,512]{2,1,0:T(8,128)S(1)}, u32[]{:S(2)}) copy-start(f32[12,512,512]{2,1,0:T(8,128)S(1)} %get-tuple-element.55) | copy-start | bytes 37748740
  74.0 4.5 %copy-start.3 = (f32[512,12]{0,1:T(8,128)}, f32[512,12]{0,1:T(8,128)S(1)}, u32[]{:S(2)}) copy-start(f32[512,12]{0,1:T(8,128)S(1)} %get-tuple-element.54) | copy-start | bytes 73732
  78.5 0.6 copy-start.4
  86.9 18.4 %all-to-all-start.2 = ((f32[8,1,768]{2,1,0:T(1,128)}), f32[8,1,768]{2,1,0:T(1,128)}, u32[]{:S(2)}, u32[]{:S(2)}) async-start(f32[8,1,768]{2,1,0:T(1,128)} %reshape.206), calls=%async_computation.2 | async-start | bytes 49152 | tf_op jit(solution)/shard_map/all_to_all | solution.py:100
  105.2 34.2 %all-to-all-start.3 = ((bf16[8,64,1,768]{3,1,2,0:T(8,128)(2,1)}), bf16[8,64,1,768]{3,1,2,0:T(8,128)(2,1)}, u32[]{:S(2)}, u32[]{:S(2)}) async-start(bf16[8,64,1,768]{3,1,2,0:T(8,128)(2,1)} %copy.66), calls=%async_computation.3 | async-start | bytes 1572864 | tf_op jit(solution)/shard_map/all_to_all | solution.py:93
  145.2 2.4 %copy-start.5 = (bf16[768,768]{1,0:T(8,128)(2,1)S(1)}, bf16[768,768]{1,0:T(8,128)(2,1)}, u32[]{:S(2)}) copy-start(bf16[768,768]{1,0:T(8,128)(2,1)} %param.9) | copy-start | bytes 3538948
where the time goes:
time: 151 us; the launch traced here: 149 us
  local copies, waits for them, and re-layouts  41.7 us (28%)
  matrix products  41.7 us (28%)
  other arithmetic  23.6 us (16%)
  starting transfers between devices  21.8 us (14%)
  waiting for transfers between devices  20.3 us (13%)
    all_to_all x1, waiting for transfers between devices, body(): lax.all_to_all(tile_embed, 'dp', split_axis=0, concat_axis=2, tiled=True)  18.9 us
    dot_general x2, matrix products, attend_block(): jnp.einsum('qhk,khd->qhd', weights.astype(jnp.bfloat16), values, preferre...  16.2 us
    dot_general x2, matrix products, attend_block(): jnp.einsum('qhd,khd->qhk', query_rows, key_rows, preferred_element_type=j...  13.9 us
    reduce_sum x2, other arithmetic, attend_block(): denominator = jnp.sum(weights, axis=-1)  10.3 us
    slice x4, local copies, waits for them, and re-layouts, attend_rows(): qkv[:, :model_features]  7.6 us
    all_to_all x1, starting transfers between devices, body(): lax.all_to_all(normed.reshape(dilation_step, context_count, model_feature...  6.64 us
    unnamed x17, local copies, waits for them, and re-layouts  6.53 us
    all_to_all x1, starting transfers between devices, body(): lax.all_to_all(dilated_output.reshape(context_count, dilation_step, 1, mo...  6 us
  transfers between devices with their start and end apart: 4, of which 2 were waited for; matrix products, arithmetic and copies ran while one was open for 42% of the time, Pallas kernels for 0%

commit v1 on v0

v1 whole, which is shorter than its diff:
```python
import functools
import math

import jax
import jax.numpy as jnp
from jax import lax
from jax.experimental import pallas as pl
from jax.experimental.pallas import tpu as pltpu
from jax.sharding import PartitionSpec as P

HEAD_TOTAL = 12
EPSILON = 1e-05
F32 = jnp.float32
BF16 = jnp.bfloat16
NT = (((1,), (1,)), ((), ()))
MIB = 1024 * 1024


def dot(a, b):
    return jnp.dot(a, b, preferred_element_type=F32)


def iota(shape, dim):
    return lax.broadcasted_iota(jnp.int32, shape, dim)


def embed_kernel(ctx, steps, x_ref, w_ref, by_residue_ref, *rest):
    slides, _, sub, width = x_ref.shape
    slide_refs, total = rest[:-1], rest[-1]
    step = pl.program_id(0)
    product = dot(x_ref[...].reshape(slides * sub, width), w_ref[...])

    @pl.when(step == 0)
    def _():
        total[...] = product

    @pl.when(step > 0)
    def _():
        total[...] += product

    @pl.when(step == steps - 1)
    def _():
        me = lax.axis_index("dp")
        each = sub // ctx
        target, source = iota((sub, sub), 0), iota((sub, sub), 1)
        order = (source == target % each * ctx + target // each).astype(BF16)
        for other in range(slides):
            slide = me ^ other
            rows = pl.ds(pl.multiple_of(slide * sub, sub), sub)
            hidden = total[rows, :].astype(BF16).astype(F32)
            centered = hidden - jnp.mean(hidden, axis=-1, keepdims=True)
            variance = jnp.mean(centered * centered, axis=-1, keepdims=True)
            normed = (centered * lax.rsqrt(variance + EPSILON)).astype(BF16)
            sorted_rows = dot(order, normed).astype(BF16)
            slide_refs[other][...] = sorted_rows
            if by_residue_ref is not None:
                by_residue_ref[:, pl.ds(slide, 1)] = sorted_rows.reshape(ctx, 1, each, -1)


def embed(tile_embed, w_in, ctx, split):
    slides, _, sub, width = tile_embed.shape
    features = w_in.shape[1]
    steps = 3
    part = width // steps
    outs = [jax.ShapeDtypeStruct((sub, features), BF16)] * slides
    specs = [pl.BlockSpec((sub, features), lambda i: (0, 0))] * slides
    if split:
        outs = [jax.ShapeDtypeStruct((ctx, slides, sub // ctx, features), BF16)] + outs
        specs = [pl.BlockSpec((ctx, slides, sub // ctx, features), lambda i: (0, 0, 0, 0))] + specs
        body = functools.partial(embed_kernel, ctx, steps)
    else:

        def body(x_ref, w_ref, *rest):
            embed_kernel(ctx, steps, x_ref, w_ref, None, *rest)

    return pl.pallas_call(
        body,
        out_shape=outs,
        grid=(steps,),
        in_specs=[
            pl.BlockSpec((slides, 1, sub, part), lambda i: (0, 0, 0, i)),
            pl.BlockSpec((part, features), lambda i: (i, 0)),
        ],
        out_specs=specs,
        scratch_shapes=[pltpu.VMEM((slides * sub, features), F32)],
        compiler_params=pltpu.CompilerParams(vmem_limit_bytes=24 * MIB),
        name="embed",
    )(tile_embed, w_in)


def project(rows, weight_ref, is_valid, keys, values):
    features = weight_ref.shape[0]
    made = dot(rows, weight_ref[:, features : 2 * features])
    keys[...] = jnp.where(is_valid, made, made[0:1]).astype(BF16)
    made = dot(rows, weight_ref[:, 2 * features :])
    values[...] = jnp.where(is_valid, made, 0.0).astype(BF16)


def queries_of(rows, weight_ref):
    features = weight_ref.shape[0]
    scale = math.log2(math.e) / math.sqrt(features // HEAD_TOTAL)
    return (dot(rows, weight_ref[:, :features]) * scale).astype(BF16)


def attend(queries, keys, values, counted, put, put_total):
    count, features = queries.shape
    width = features // HEAD_TOTAL
    pair = 2 * width
    even = iota((1, pair), 1) < width
    lane = iota((1, 128), 1)
    logs = jnp.zeros((count, 128), F32)
    for at in range(0, features, pair):
        columns = slice(at, at + pair)
        both = queries[:, columns]
        key_pair = keys[:, columns]
        value_pair = jnp.concatenate([values[:, columns], counted], axis=1)
        outs = []
        for side in range(2):
            mine = even if side == 0 else ~even
            scores = lax.dot_general(jnp.where(mine, both, 0).astype(BF16), key_pair, NT, preferred_element_type=F32)
            top = jnp.max(scores, axis=-1, keepdims=True)
            weights = jnp.exp2(scores - top).astype(BF16)
            summed = dot(weights, value_pair)
            outs.append(summed)
            logs = jnp.where(lane == at // width + side, top + jnp.log2(summed[:, pair : pair + 128]), logs)
        total = jnp.where(even, outs[0][:, pair:], outs[1][:, pair:])
        out = jnp.where(even, outs[0][:, :pair], outs[1][:, :pair])
        put(columns, (out / jnp.where(total > 0, total, 1.0)).astype(BF16))
    put_total(logs)


def local_kernel(dp, ctx, block, counts_ref, *refs):
    pieces, (weight_ref, out_ref, log_ref, rows, keys, values) = refs[:dp], refs[dp:]
    me = lax.axis_index("dp")
    sub = pieces[0].shape[0]
    for other, piece in enumerate(pieces):
        rows[pl.ds(pl.multiple_of((me ^ other) * sub, sub), sub), :] = piece[...]
    count = rows.shape[0]
    each = sub // ctx
    spot = iota((count, 1), 0)
    inner = spot % sub
    position = lax.axis_index("ctx") * count + spot // sub * sub + inner % each * ctx + inner // each
    is_valid = position < counts_ref[me]
    project(rows[...], weight_ref, is_valid, keys, values)
    counted = jnp.broadcast_to(is_valid.astype(F32), (count, 128)).astype(BF16)
    for start in range(0, count, block):

        def put(columns, out):
            out_ref[start : start + block, columns] = out

        def put_total(logs):
            log_ref[start : start + block, :] = logs

        attend(queries_of(rows[start : start + block, :], weight_ref), keys, values, counted, put, put_total)


def local_attention(tile_counts, pieces, w_qkv, ctx):
    dp = len(pieces)
    sub, features = pieces[0].shape
    count = dp * sub
    vmem = pl.BlockSpec(memory_space=pltpu.VMEM)
    return pl.pallas_call(
        functools.partial(local_kernel, dp, ctx, min(256, count)),
        out_shape=[jax.ShapeDtypeStruct((count, features), BF16), jax.ShapeDtypeStruct((count, 128), F32)],
        in_specs=[pl.BlockSpec(memory_space=pltpu.SMEM)] + [vmem] * (dp + 1),
        out_specs=[vmem] * 2,
        scratch_shapes=[pltpu.VMEM((count, features), BF16)] * 3,
        compiler_params=pltpu.CompilerParams(vmem_limit_bytes=24 * MIB),
        cost_estimate=pl.CostEstimate(flops=9 * 10**9, bytes_accessed=8 * 10**6, transcendentals=0),
        name="local",
    )(tile_counts, *pieces, w_qkv)


def dilated_kernel(dp, ctx, block, sends, counts_ref, rows_ref, weight_ref, *refs):
    out_refs, (rows, keys, values) = refs[:-3], refs[-3:]
    me, mine = lax.axis_index("dp"), lax.axis_index("ctx")
    count, features = rows_ref.shape
    portion = count // ctx
    each = portion // dp
    spot = iota((count, 1), 0)
    inner = spot % portion
    position = spot // portion * count + inner // each * (count // dp) + inner % each * ctx + mine
    is_valid = position < counts_ref[me]
    project(rows_ref[...], weight_ref, is_valid, keys, values)
    counted = jnp.broadcast_to(is_valid.astype(F32), (count, 128)).astype(BF16)
    if sends is None:
        source = rows_ref
    else:
        source = rows
        for place, other in enumerate(sends):
            at = pl.multiple_of((mine ^ other) * portion, portion)
            rows[place * portion : (place + 1) * portion, :] = rows_ref[pl.ds(at, portion), :]
    for start in range(0, count, block):

        def spread(columns, out):
            for at in range(start, start + block, portion):
                piece = out[at - start : at - start + portion]
                if sends is None:
                    out_refs[0][at : at + portion, columns] = piece
                else:
                    out_refs[at // portion][:, columns] = piece

        def put_total(logs):
            high = logs.astype(BF16).astype(F32)
            low = logs - high
            lane = iota((1, 128), 1)
            both = jnp.where(lane < 16, high, pltpu.roll(low, 16, 1))
            spread(slice(features, features + 128), jnp.where(lane < 32, both, 0.0).astype(BF16))

        attend(queries_of(source[start : start + block, :], weight_ref), keys, values, counted, spread, put_total)


def dilated_attention(tile_counts, rows, w_qkv, dp, ctx, sends):
    count, features = rows.shape
    vmem = pl.BlockSpec(memory_space=pltpu.VMEM)
    if sends is None:
        outs = [jax.ShapeDtypeStruct((count, features + 128), BF16)]
    else:
        outs = [jax.ShapeDtypeStruct((count // ctx, features + 128), BF16)] * ctx
    return pl.pallas_call(
        functools.partial(dilated_kernel, dp, ctx, min(256, count), sends),
        out_shape=outs,
        in_specs=[pl.BlockSpec(memory_space=pltpu.SMEM)] + [vmem] * 2,
        out_specs=[vmem] * len(outs),
        scratch_shapes=[pltpu.VMEM((count, features), BF16)] * 3,
        compiler_params=pltpu.CompilerParams(vmem_limit_bytes=24 * MIB),
        cost_estimate=pl.CostEstimate(flops=9 * 10**9, bytes_accessed=8 * 10**6, transcendentals=0),
        name="dilated",
    )(tile_counts, rows, w_qkv)


def merge_kernel(dp, ctx, sends, counts_ref, out_ref, log_ref, weight_ref, *refs):
    received, (mixed_ref, dilated) = refs[:-2], refs[-2:]
    me, mine = lax.axis_index("dp"), lax.axis_index("ctx")
    count, features = out_ref.shape
    sub = count // dp
    each = sub // ctx
    if sends is None:
        dilated[...] = received[0][...]
    else:
        for other, piece in zip(sends, received):
            for part in range(dp):
                at = pl.multiple_of(part * sub + (mine ^ other) * each, each)
                dilated[pl.ds(at, each), :] = piece[part * each : (part + 1) * each, :]
    lane = iota((1, 128), 1)
    heads = iota((128, features), 0) == iota((128, features), 1) // (features // HEAD_TOTAL)
    heads = heads.astype(BF16)
    target, source = iota((sub, sub), 0), iota((sub, sub), 1)
    order = (target == source % each * ctx + source // each).astype(BF16)
    for part in range(dp):
        rows = slice(part * sub, (part + 1) * sub)
        logs = dilated[rows, features:].astype(F32)
        logs = logs + pltpu.roll(logs, 128 - 16, 1)
        share = jnp.where(lane < HEAD_TOTAL, 1.0 / (1.0 + jnp.exp2(log_ref[rows, :] - logs)), 0.0)
        high = share.astype(BF16)
        low = (share - high.astype(F32)).astype(BF16)
        wide = dot(high, heads) + dot(low, heads)
        own = out_ref[rows, :].astype(F32)
        merged = own + wide * (dilated[rows, :features].astype(F32) - own)
        inner = iota((sub, 1), 0)
        position = mine * count + part * sub + inner % each * ctx + inner // each
        mixed = jnp.where(position < counts_ref[me], dot(merged.astype(BF16), weight_ref[...]), 0.0)
        mixed_ref[0, rows, :] = dot(order, mixed.astype(BF16)).astype(BF16)


def merge(tile_counts, out, logs, w_out, received, dp, ctx, sends):
    count, features = out.shape
    vmem = pl.BlockSpec(memory_space=pltpu.VMEM)
    return pl.pallas_call(
        functools.partial(merge_kernel, dp, ctx, sends),
        out_shape=jax.ShapeDtypeStruct((1, count, features), BF16),
        in_specs=[pl.BlockSpec(memory_space=pltpu.SMEM)] + [vmem] * (3 + len(received)),
        out_specs=vmem,
        scratch_shapes=[pltpu.VMEM((count, features + 128), BF16)],
        compiler_params=pltpu.CompilerParams(vmem_limit_bytes=24 * MIB),
        name="merge",
    )(tile_counts, out, logs, w_out, *received)


def exchange(value, axis, other):
    if other == 0:
        return value
    return lax.ppermute(value, axis, [(i, i ^ other) for i in range(lax.axis_size(axis))])


def body(tile_embed, tile_counts, w_in, w_qkv, w_out):
    dp, ctx = lax.axis_size("dp"), lax.axis_size("ctx")
    slides, _, sub, _ = tile_embed.shape
    features = w_out.shape[0]
    count = sub * dp
    each = sub // ctx
    aligned = each % 16 == 0 and ctx <= 8
    made = embed(tile_embed, w_in, ctx, aligned)
    if aligned:
        by_residue, made = made[0], made[1:]
    else:
        slide_of = [lax.axis_index("dp") ^ other for other in range(dp)]
        stacked = jnp.stack(made)[jnp.stack(slide_of)]
        by_residue = stacked.reshape(slides, ctx, each, features).swapaxes(0, 1)
    regrouped = lax.all_to_all(
        by_residue.reshape(ctx * dp, each, features), ("ctx", "dp"), split_axis=0, concat_axis=0, tiled=True
    ).reshape(count, features)
    pieces = [exchange(piece, "dp", other) for other, piece in enumerate(made)]
    out, logs = local_attention(tile_counts, pieces, w_qkv, ctx)
    if aligned:
        sends = [4, 5, 6, 7, 2, 3, 1, 0] if ctx == 8 else list(range(ctx))
        made = dilated_attention(tile_counts, regrouped, w_qkv, dp, ctx, sends)
        received = [exchange(piece, "ctx", other) for other, piece in zip(sends, made)]
    else:
        sends = None
        made = dilated_attention(tile_counts, regrouped, w_qkv, dp, ctx, sends)[0]
        received = lax.all_to_all(made.reshape(ctx, count // ctx, -1), "ctx", split_axis=0, concat_axis=0, tiled=True)
        received = received.reshape(ctx, dp, each, -1).swapaxes(0, 1).reshape(count, -1)
        received = [received]
    return merge(tile_counts, out, logs, w_out, received, dp, ctx, sends)


def solution(mesh):
    in_specs = (P(None, "ctx", "dp", None), P(), P(), P(), P())
    out_specs = P("dp", "ctx", None)
    return jax.shard_map(body, mesh=mesh, in_specs=in_specs, out_specs=out_specs, check_vma=False)
```

time: 151 us -> 74.9 us (0.50)
  matrix products: 41.7 us -> 0 us
  local copies, waits for them, and re-layouts: 41.7 us -> 5.08 us
  other arithmetic: 23.6 us -> 0 us
  Pallas kernels: 0 us -> 20.8 us
  waiting for transfers between devices: 20.3 us -> 29.9 us
  starting transfers between devices: 21.8 us -> 18.8 us
    dot_general x8 -> x0, matrix products: 41.7 us -> none  [the longest x2 16.2 us: attend_block(): jnp.einsum('qhk,khd->qhd', weights.astype(jnp.bfloat16), values, preferre...]
    pallas_call x0 -> x4, Pallas kernels: none -> 20.8 us  [the longest x1 6.53 us: local_attention(): pl.pallas_call(functools.partial(local_kernel, dp, ctx, min(256, count)),...]
    slice x8 -> x0, local copies, waits for them, and re-layouts: 16.8 us -> none  [the longest x4 7.6 us: attend_rows(): qkv[:, :model_features]]
    all_to_all x4 -> x1, starting transfers between devices: 21.8 us -> 7.3 us  [body(): lax.all_to_all(by_residue.reshape(ctx * dp, each, features), ('ctx', 'dp'...]
    ppermute x0 -> x10, starting transfers between devices: none -> 11.5 us  [exchange(): lax.ppermute(value, axis, [(i, i ^ other) for i in range(lax.axis_size(ax...]
    ppermute x0 -> x10, waiting for transfers between devices: none -> 11.3 us  [exchange(): lax.ppermute(value, axis, [(i, i ^ other) for i in range(lax.axis_size(ax...]
    reduce_sum x3 -> x0, other arithmetic: 10.6 us -> none  [the longest x2 10.3 us: attend_block(): denominator = jnp.sum(weights, axis=-1)]
    convert_element_type x3 -> x0, local copies, waits for them, and re-layouts: 8.92 us -> none  [the longest x2 5.89 us: body(): (dilated_accumulator / dilated_total[..., None]).astype(jnp.bfloat16)]
  transfers between devices with their start and end apart: 4 -> 11, of which waited for: 2 -> 3; matrix products, arithmetic and copies ran while one was open for 42% -> 0% of each run, Pallas kernels for 0% -> 18%
where the time goes in v1:
time: 74.9 us; the launch traced here: 74.6 us
  waiting for transfers between devices  29.9 us (40%)
  Pallas kernels  20.8 us (28%)
  starting transfers between devices  18.8 us (25%)
  local copies, waits for them, and re-layouts  5.08 us (7%)
    all_to_all x1, waiting for transfers between devices, body(): lax.all_to_all(by_residue.reshape(ctx * dp, each, features), ('ctx', 'dp'...  18.6 us
    ppermute x10, starting transfers between devices, exchange(): lax.ppermute(value, axis, [(i, i ^ other) for i in range(lax.axis_size(ax...  11.5 us
    ppermute x10, waiting for transfers between devices, exchange(): lax.ppermute(value, axis, [(i, i ^ other) for i in range(lax.axis_size(ax...  11.3 us
    all_to_all x1, starting transfers between devices, body(): lax.all_to_all(by_residue.reshape(ctx * dp, each, features), ('ctx', 'dp'...  7.3 us
    pallas_call x1, Pallas kernels, local_attention(): pl.pallas_call(functools.partial(local_kernel, dp, ctx, min(256, count)),...  6.53 us
    pallas_call x1, Pallas kernels, dilated_attention(): pl.pallas_call(functools.partial(dilated_kernel, dp, ctx, min(256, count)...  6.52 us
    unnamed x12, local copies, waits for them, and re-layouts  5.08 us
    pallas_call x1, Pallas kernels, embed(): pl.pallas_call(body, out_shape=outs, grid=(steps,), in_specs=[pl.BlockSpe...  3.88 us
  transfers between devices with their start and end apart: 11, of which 3 were waited for; matrix products, arithmetic and copies ran while one was open for 0% of the time, Pallas kernels for 18%

profile of v1, /device:TPU:0, one launch (start us, length us, event | category | flops | bytes accessed | tf_op | source)
XLA Modules:
  0.0 74.6 jit_solution(5907891763276219858)
XLA Ops:
  0.0 1.7 %copy-done = bf16[1536,768]{1,0:T(8,128)(2,1)S(1)} copy-done((bf16[1536,768]{1,0:T(8,128)(2,1)S(1)}, bf16[1536,768]{1,0:T(8,128)(2,1)}, u32[]{:S(2)}) %copy-start) | copy-done | bytes 2359320
  1.7 1.4 %copy-done.1 = bf16[4,1,128,1536]{3,2,1,0:T(8,128)(2,1)S(1)} copy-done((bf16[4,1,128,1536]{3,2,1,0:T(8,128)(2,1)S(1)}, bf16[4,1,128,1536]{3,2,1,0:T(8,128)(2,1)}, u32[]{:S(2)}) %copy-start.1) | copy-done | bytes 1572888
  3.1 3.9 %embed.1 = (bf16[8,4,16,768]{3,2,1,0:T(8,128)(2,1)}, bf16[128,768]{1,0:T(8,128)(2,1)S(1)}, bf16[128,768]{1,0:T(8,128)(2,1)S(1)}, bf16[128,768]{1,0:T(8,128)(2,1)S(1)}, bf16[128,768]{1,0:T(8,128)(2,1)S(1)}) custom-call(bf16[4,1,128,1536]{3,2,1,0:T(8,128)(2,1)S(1)} %copy-done.1, bf16[1536,768]{1,0:T(8,128)(2,1)S(1)} %copy-done), custom_call_target="tpu_custom_call" | custom-call | tf_op jit(solution)/shard_map/embed/pallas_call | solution.py:76
  7.0 7.3 %all-to-all-start = ((bf16[32,16,768]{2,1,0:T(8,128)(2,1)}), bf16[32,16,768]{2,1,0:T(8,128)(2,1)S(1)}, u32[]{:S(2)}, u32[]{:S(2)}) async-start(bf16[32,16,768]{2,1,0:T(8,128)(2,1)} %bitcast), calls=%async_computation | async-start | bytes 1572864 | tf_op jit(solution)/shard_map/all_to_all | solution.py:300
  14.3 0.3 collective-permute-start
  14.6 1.7 %collective-permute-start.1 = (bf16[128,768]{1,0:T(8,128)(2,1)S(1)}, bf16[128,768]{1,0:T(8,128)(2,1)S(1)}, u32[]{:S(2)}, u32[]{:S(2)}) collective-permute-start(bf16[128,768]{1,0:T(8,128)(2,1)S(1)} %get-tuple-element.22), channel_id=1, source_target_pairs={{0,16},{8,24},{16,0},{24,8},{1,17},{9,25},{17,1},{25,9},{2,18},{10... | collective-permute-start | bytes 589832 | tf_op jit(solution)/shard_map/ppermute | solution.py:283
  16.3 0.0 collective-permute-start.2
  16.3 18.6 %all-to-all-done = bf16[32,16,768]{2,1,0:T(8,128)(2,1)S(1)} async-done(((bf16[32,16,768]{2,1,0:T(8,128)(2,1)}), bf16[32,16,768]{2,1,0:T(8,128)(2,1)S(1)}, u32[]{:S(2)}, u32[]{:S(2)}) %all-to-all-start) | async-done | bytes 786464 | tf_op jit(solution)/shard_map/all_to_all | solution.py:300
  34.9 2.0 %copy-done.4 = bf16[768,2304]{1,0:T(8,128)(2,1)S(1)} copy-done((bf16[768,2304]{1,0:T(8,128)(2,1)S(1)}, bf16[768,2304]{1,0:T(8,128)(2,1)}, u32[]{:S(2)}) %copy-start.4) | copy-done | bytes 3538968
  36.9 6.5 %dilated.1 = (bf16[64,896]{1,0:T(8,128)(2,1)S(1)}, bf16[64,896]{1,0:T(8,128)(2,1)S(1)}, bf16[64,896]{1,0:T(8,128)(2,1)S(1)}, bf16[64,896]{1,0:T(8,128)(2,1)S(1)}...) custom-call(s32[4]{0:T(128)S(1)} %copy-done.3, ...), custom_call_target="tpu_custom_call" | custom-call | flops 8999999488 | bytes 8000000 | tf_op jit(solution)/shard_map/dilated/pallas_call | solution.py:220
  43.4 1.0 %collective-permute-start.3 = (bf16[64,896]{1,0:T(8,128)(2,1)S(1)}, bf16[64,896]{1,0:T(8,128)(2,1)S(1)}, u32[]{:S(2)}, u32[]{:S(2)}) collective-permute-start(bf16[64,896]{1,0:T(8,128)(2,1)S(1)} %get-tuple-element.27), channel_id=1, source_target_pairs={{0,4},{1,5},{2,6},{3,7},{4,0},{5,1},{6,2},{7,3},{8,12},{9,13},{10,... | collective-permute-start | bytes 344072 | tf_op jit(solution)/shard_map/ppermute | solution.py:283
  44.4 3.0 %collective-permute-start.4 = (bf16[64,896]{1,0:T(8,128)(2,1)S(1)}, bf16[64,896]{1,0:T(8,128)(2,1)S(1)}, u32[]{:S(2)}, u32[]{:S(2)}) collective-permute-start(bf16[64,896]{1,0:T(8,128)(2,1)S(1)} %get-tuple-element.28), channel_id=1, source_target_pairs={{0,5},{1,4},{2,7},{3,6},{4,1},{5,0},{6,3},{7,2},{8,13},{9,12},{10,... | collective-permute-start | bytes 344072 | tf_op jit(solution)/shard_map/ppermute | solution.py:283
  47.4 1.4 %collective-permute-start.5 = (bf16[64,896]{1,0:T(8,128)(2,1)S(1)}, bf16[64,896]{1,0:T(8,128)(2,1)S(1)}, u32[]{:S(2)}, u32[]{:S(2)}) collective-permute-start(bf16[64,896]{1,0:T(8,128)(2,1)S(1)} %get-tuple-element.29), channel_id=1, source_target_pairs={{0,6},{1,7},{2,4},{3,5},{4,2},{5,3},{6,0},{7,1},{8,14},{9,15},{10,... | collective-permute-start | bytes 344072 | tf_op jit(solution)/shard_map/ppermute | solution.py:283
  48.8 2.3 %collective-permute-start.6 = (bf16[64,896]{1,0:T(8,128)(2,1)S(1)}, bf16[64,896]{1,0:T(8,128)(2,1)S(1)}, u32[]{:S(2)}, u32[]{:S(2)}) collective-permute-start(bf16[64,896]{1,0:T(8,128)(2,1)S(1)} %get-tuple-element.30), channel_id=1, source_target_pairs={{0,7},{1,6},{2,5},{3,4},{4,3},{5,2},{6,1},{7,0},{8,15},{9,14},{10,... | collective-permute-start | bytes 344072 | tf_op jit(solution)/shard_map/ppermute | solution.py:283
  51.1 0.0 collective-permute-done.2.refs_3_
  51.1 0.0 collective-permute-start.7
  51.1 9.1 %collective-permute-done.3.refs_0_ = bf16[64,896]{1,0:T(8,128)(2,1)S(1)} collective-permute-done((bf16[64,896]{1,0:T(8,128)(2,1)S(1)}, bf16[64,896]{1,0:T(8,128)(2,1)S(1)}, u32[]{:S(2)}, u32[]{:S(2)}) %collective-permute-start.3) | collective-permute-done | bytes 114720 | tf_op jit(solution)/shard_map/ppermute | solution.py:283
  60.3 2.1 %collective-permute-done.4.refs_1_ = bf16[64,896]{1,0:T(8,128)(2,1)S(1)} collective-permute-done((bf16[64,896]{1,0:T(8,128)(2,1)S(1)}, bf16[64,896]{1,0:T(8,128)(2,1)S(1)}, u32[]{:S(2)}, u32[]{:S(2)}) %collective-permute-start.4) | collective-permute-done | bytes 114720 | tf_op jit(solution)/shard_map/ppermute | solution.py:283
  62.4 1.8 %collective-permute-start.9 = (bf16[64,896]{1,0:T(8,128)(2,1)S(1)}, bf16[64,896]{1,0:T(8,128)(2,1)S(1)}, u32[]{:S(2)}, u32[]{:S(2)}) collective-permute-start(bf16[64,896]{1,0:T(8,128)(2,1)S(1)} %get-tuple-element.33), channel_id=1, source_target_pairs={{0,1},{1,0},{2,3},{3,2},{4,5},{5,4},{6,7},{7,6},{8,9},{9,8},{10,11... | collective-permute-start | bytes 344072 | tf_op jit(solution)/shard_map/ppermute | solution.py:283
  64.2 6.5 %local.1 = (bf16[512,768]{1,0:T(8,128)(2,1)S(1)}, f32[512,128]{1,0:T(8,128)S(1)}) custom-call(s32[4]{0:T(128)S(1)} %copy-done.3, bf16[128,768]{1,0:T(8,128)(2,1)S(1)} %get-tuple-element.20.refs_0_, bf16[128,768]{1,0:T(8,128)(2,1)S(1)} %collective-permute-done.refs_1_, bf16[128,768]{1,0:T(8,128)(2,1)S(1)} %collective-permute-done.1.refs_2_, ...), custom_call_target="tpu_custom_call" | custom-call | flops 8999999488 | bytes 8000000 | tf_op jit(solution)/shard_map/local/pallas_call | solution.py:162
  70.7 0.0 collective-permute-done.6.refs_3_
  70.7 0.0 collective-permute-done.7.refs_4_
  70.7 0.0 collective-permute-done.9.refs_6_
  70.8 3.9 %merge.1 = bf16[1,512,768]{2,1,0:T(8,128)(2,1)} custom-call(s32[4]{0:T(128)S(1)} %copy-done.3, bf16[512,768]{1,0:T(8,128)(2,1)S(1)} %get-tuple-element.24.out_ref, f32[512,128]{1,0:T(8,128)S(1)} %get-tuple-element.25.log_ref, bf16[768,768]{1,0:T(8,128)(2,1)S(1)} %copy-done.2, bf16[64,896]{1,0:T(8,128)(2,1)S(1)} %collective-permute-done.3.refs_0_, ...), custom_call_target="tpu_custom_call" | custom-call | tf_op jit(solution)/shard_map/merge/pallas_call | solution.py:269
  (14 shorter events, 0.0 us)
Async XLA Ops:
  0.0 1.7 %copy-start = (bf16[1536,768]{1,0:T(8,128)(2,1)S(1)}, bf16[1536,768]{1,0:T(8,128)(2,1)}, u32[]{:S(2)}) copy-start(bf16[1536,768]{1,0:T(8,128)(2,1)} %w_ref.1) | copy-start | bytes 7077892
  1.7 1.4 %copy-start.1 = (bf16[4,1,128,1536]{3,2,1,0:T(8,128)(2,1)S(1)}, bf16[4,1,128,1536]{3,2,1,0:T(8,128)(2,1)}, u32[]{:S(2)}) copy-start(bf16[4,1,128,1536]{3,2,1,0:T(8,128)(2,1)} %x_ref.1) | copy-start | bytes 4718596
  3.1 31.8 %copy-start.3 = (s32[4]{0:T(128)S(1)}, s32[4]{0:T(128)}, u32[]{:S(2)}) copy-start(s32[4]{0:T(128)} %counts_ref.5) | copy-start | bytes 52
  7.0 27.9 %all-to-all-start = ((bf16[32,16,768]{2,1,0:T(8,128)(2,1)}), bf16[32,16,768]{2,1,0:T(8,128)(2,1)S(1)}, u32[]{:S(2)}, u32[]{:S(2)}) async-start(bf16[32,16,768]{2,1,0:T(8,128)(2,1)} %bitcast), calls=%async_computation | async-start | bytes 1572864 | tf_op jit(solution)/shard_map/all_to_all | solution.py:300
  14.3 33.1 %collective-permute-start = (bf16[128,768]{1,0:T(8,128)(2,1)S(1)}, bf16[128,768]{1,0:T(8,128)(2,1)S(1)}, u32[]{:S(2)}, u32[]{:S(2)}) collective-permute-start(bf16[128,768]{1,0:T(8,128)(2,1)S(1)} %get-tuple-element.21), channel_id=1, source_target_pairs={{0,8},{8,0},{16,24},{24,16},{1,9},{9,1},{17,25},{25,17},{2,10},{10... | collective-permute-start | bytes 589832 | tf_op jit(solution)/shard_map/ppermute | solution.py:283
  14.6 34.2 %collective-permute-start.1 = (bf16[128,768]{1,0:T(8,128)(2,1)S(1)}, bf16[128,768]{1,0:T(8,128)(2,1)S(1)}, u32[]{:S(2)}, u32[]{:S(2)}) collective-permute-start(bf16[128,768]{1,0:T(8,128)(2,1)S(1)} %get-tuple-element.22), channel_id=1, source_target_pairs={{0,16},{8,24},{16,0},{24,8},{1,17},{9,25},{17,1},{25,9},{2,18},{10... | collective-permute-start | bytes 589832 | tf_op jit(solution)/shard_map/ppermute | solution.py:283
  16.3 34.9 %collective-permute-start.2 = (bf16[128,768]{1,0:T(8,128)(2,1)S(1)}, bf16[128,768]{1,0:T(8,128)(2,1)S(1)}, u32[]{:S(2)}, u32[]{:S(2)}) collective-permute-start(bf16[128,768]{1,0:T(8,128)(2,1)S(1)} %get-tuple-element.23), channel_id=1, source_target_pairs={{0,24},{8,16},{16,8},{24,0},{1,25},{9,17},{17,9},{25,1},{2,26},{10... | collective-permute-start | bytes 589832 | tf_op jit(solution)/shard_map/ppermute | solution.py:283
  34.9 2.0 %copy-start.4 = (bf16[768,2304]{1,0:T(8,128)(2,1)S(1)}, bf16[768,2304]{1,0:T(8,128)(2,1)}, u32[]{:S(2)}) copy-start(bf16[768,2304]{1,0:T(8,128)(2,1)} %weight_ref.2) | copy-start | bytes 10616836
  36.9 27.3 %copy-start.5 = (bf16[768,2304]{1,0:T(8,128)(2,1)S(1)}, bf16[768,2304]{1,0:T(8,128)(2,1)}, u32[]{:S(2)}) copy-start(bf16[768,2304]{1,0:T(8,128)(2,1)} %weight_ref.2) | copy-start | bytes 10616836
  43.4 16.9 %collective-permute-start.3 = (bf16[64,896]{1,0:T(8,128)(2,1)S(1)}, bf16[64,896]{1,0:T(8,128)(2,1)S(1)}, u32[]{:S(2)}, u32[]{:S(2)}) collective-permute-start(bf16[64,896]{1,0:T(8,128)(2,1)S(1)} %get-tuple-element.27), channel_id=1, source_target_pairs={{0,4},{1,5},{2,6},{3,7},{4,0},{5,1},{6,2},{7,3},{8,12},{9,13},{10,... | collective-permute-start | bytes 344072 | tf_op jit(solution)/shard_map/ppermute | solution.py:283
  44.4 18.0 %collective-permute-start.4 = (bf16[64,896]{1,0:T(8,128)(2,1)S(1)}, bf16[64,896]{1,0:T(8,128)(2,1)S(1)}, u32[]{:S(2)}, u32[]{:S(2)}) collective-permute-start(bf16[64,896]{1,0:T(8,128)(2,1)S(1)} %get-tuple-element.28), channel_id=1, source_target_pairs={{0,5},{1,4},{2,7},{3,6},{4,1},{5,0},{6,3},{7,2},{8,13},{9,12},{10,... | collective-permute-start | bytes 344072 | tf_op jit(solution)/shard_map/ppermute | solution.py:283
  47.4 23.3 %collective-permute-start.5 = (bf16[64,896]{1,0:T(8,128)(2,1)S(1)}, bf16[64,896]{1,0:T(8,128)(2,1)S(1)}, u32[]{:S(2)}, u32[]{:S(2)}) collective-permute-start(bf16[64,896]{1,0:T(8,128)(2,1)S(1)} %get-tuple-element.29), channel_id=1, source_target_pairs={{0,6},{1,7},{2,4},{3,5},{4,2},{5,3},{6,0},{7,1},{8,14},{9,15},{10,... | collective-permute-start | bytes 344072 | tf_op jit(solution)/shard_map/ppermute | solution.py:283
  48.8 21.9 %collective-permute-start.6 = (bf16[64,896]{1,0:T(8,128)(2,1)S(1)}, bf16[64,896]{1,0:T(8,128)(2,1)S(1)}, u32[]{:S(2)}, u32[]{:S(2)}) collective-permute-start(bf16[64,896]{1,0:T(8,128)(2,1)S(1)} %get-tuple-element.30), channel_id=1, source_target_pairs={{0,7},{1,6},{2,5},{3,4},{4,3},{5,2},{6,1},{7,0},{8,15},{9,14},{10,... | collective-permute-start | bytes 344072 | tf_op jit(solution)/shard_map/ppermute | solution.py:283
  51.1 19.6 %collective-permute-start.7 = (bf16[64,896]{1,0:T(8,128)(2,1)S(1)}, bf16[64,896]{1,0:T(8,128)(2,1)S(1)}, u32[]{:S(2)}, u32[]{:S(2)}) collective-permute-start(bf16[64,896]{1,0:T(8,128)(2,1)S(1)} %get-tuple-element.31), channel_id=1, source_target_pairs={{0,2},{1,3},{2,0},{3,1},{4,6},{5,7},{6,4},{7,5},{8,10},{9,11},{10,... | collective-permute-start | bytes 344072 | tf_op jit(solution)/shard_map/ppermute | solution.py:283
  60.3 10.4 %collective-permute-start.8 = (bf16[64,896]{1,0:T(8,128)(2,1)S(1)}, bf16[64,896]{1,0:T(8,128)(2,1)S(1)}, u32[]{:S(2)}, u32[]{:S(2)}) collective-permute-start(bf16[64,896]{1,0:T(8,128)(2,1)S(1)} %get-tuple-element.32), channel_id=1, source_target_pairs={{0,3},{1,2},{2,1},{3,0},{4,7},{5,6},{6,5},{7,4},{8,11},{9,10},{10,... | collective-permute-start | bytes 344072 | tf_op jit(solution)/shard_map/ppermute | solution.py:283
  62.4 8.4 %collective-permute-start.9 = (bf16[64,896]{1,0:T(8,128)(2,1)S(1)}, bf16[64,896]{1,0:T(8,128)(2,1)S(1)}, u32[]{:S(2)}, u32[]{:S(2)}) collective-permute-start(bf16[64,896]{1,0:T(8,128)(2,1)S(1)} %get-tuple-element.33), channel_id=1, source_target_pairs={{0,1},{1,0},{2,3},{3,2},{4,5},{5,4},{6,7},{7,6},{8,9},{9,8},{10,11... | collective-permute-start | bytes 344072 | tf_op jit(solution)/shard_map/ppermute | solution.py:283
  64.2 6.6 %copy-start.2 = (bf16[768,768]{1,0:T(8,128)(2,1)S(1)}, bf16[768,768]{1,0:T(8,128)(2,1)}, u32[]{:S(2)}) copy-start(bf16[768,768]{1,0:T(8,128)(2,1)} %weight_ref.3) | copy-start | bytes 3538948

commit v2 on v1

--- a/solution.py
+++ b/solution.py
@@ -24,37 +24,48 @@
     return lax.broadcasted_iota(jnp.int32, shape, dim)
 
 
-def embed_kernel(ctx, steps, x_ref, w_ref, by_residue_ref, *rest):
-    slides, _, sub, width = x_ref.shape
-    slide_refs, total = rest[:-1], rest[-1]
-    step = pl.program_id(0)
-    product = dot(x_ref[...].reshape(slides * sub, width), w_ref[...])
-
-    @pl.when(step == 0)
-    def _():
-        total[...] = product
-
-    @pl.when(step > 0)
-    def _():
-        total[...] += product
-
-    @pl.when(step == steps - 1)
-    def _():
-        me = lax.axis_index("dp")
-        each = sub // ctx
-        target, source = iota((sub, sub), 0), iota((sub, sub), 1)
-        order = (source == target % each * ctx + target // each).astype(BF16)
-        for other in range(slides):
-            slide = me ^ other
-            rows = pl.ds(pl.multiple_of(slide * sub, sub), sub)
-            hidden = total[rows, :].astype(BF16).astype(F32)
-            centered = hidden - jnp.mean(hidden, axis=-1, keepdims=True)
-            variance = jnp.mean(centered * centered, axis=-1, keepdims=True)
-            normed = (centered * lax.rsqrt(variance + EPSILON)).astype(BF16)
-            sorted_rows = dot(order, normed).astype(BF16)
-            slide_refs[other][...] = sorted_rows
-            if by_residue_ref is not None:
-                by_residue_ref[:, pl.ds(slide, 1)] = sorted_rows.reshape(ctx, 1, each, -1)
+def embed_kernel(ctx, steps, split, x_hbm, w_hbm, *refs):
+    slides, _, sub, width = x_hbm.shape
+    outs = refs[: slides + split]
+    x_parts, w_parts, made, arrived, sent = refs[slides + split :]
+    part = width // steps
+    loads = []
+    for step in range(steps):
+        columns = pl.ds(step * part, part)
+        loads.append(
+            (
+                pltpu.make_async_copy(w_hbm.at[columns], w_parts.at[step], arrived.at[0, step]),
+                pltpu.make_async_copy(x_hbm.at[:, 0, :, columns], x_parts.at[step], arrived.at[1, step]),
+            )
+        )
+        for load in loads[-1]:
+            load.start()
+    total = None
+    for step in range(steps):
+        for load in loads[step]:
+            load.wait()
+        product = dot(x_parts[step].reshape(slides * sub, part), w_parts[step])
+        total = product if total is None else total + product
+    hidden = total.astype(BF16).astype(F32)
+    centered = hidden - jnp.mean(hidden, axis=-1, keepdims=True)
+    variance = jnp.mean(centered * centered, axis=-1, keepdims=True)
+    normed = (centered * lax.rsqrt(variance + EPSILON)).astype(BF16)
+    me = lax.axis_index("dp")
+    each = sub // ctx
+    target, source = iota((sub, sub), 0), iota((sub, sub), 1)
+    order = (source == target % each * ctx + target // each).astype(BF16)
+    for slide in range(slides):
+        made[slide] = dot(order, normed[slide * sub : (slide + 1) * sub]).astype(BF16).reshape(made.shape[1:])
+    stores = []
+    if split:
+        for slide in range(slides):
+            stores.append(pltpu.make_async_copy(made.at[slide], outs[0].at[:, slide], sent.at[1, slide]))
+            stores[-1].start()
+    for other in range(slides):
+        stores.append(pltpu.make_async_copy(made.at[me ^ other], outs[split + other], sent.at[0, other]))
+        stores[-1].start()
+    for store in stores:
+        store.wait()
 
 
 def embed(tile_embed, w_in, ctx, split):
@@ -62,27 +73,23 @@
     features = w_in.shape[1]
     steps = 3
     part = width // steps
-    outs = [jax.ShapeDtypeStruct((sub, features), BF16)] * slides
-    specs = [pl.BlockSpec((sub, features), lambda i: (0, 0))] * slides
+    shape = (ctx, sub // ctx, features) if split else (sub, features)
+    outs = [jax.ShapeDtypeStruct(shape, BF16)] * slides
     if split:
         outs = [jax.ShapeDtypeStruct((ctx, slides, sub // ctx, features), BF16)] + outs
-        specs = [pl.BlockSpec((ctx, slides, sub // ctx, features), lambda i: (0, 0, 0, 0))] + specs
-        body = functools.partial(embed_kernel, ctx, steps)
-    else:
-
-        def body(x_ref, w_ref, *rest):
-            embed_kernel(ctx, steps, x_ref, w_ref, None, *rest)
-
+    hbm = pl.BlockSpec(memory_space=pltpu.HBM)
     return pl.pallas_call(
-        body,
+        functools.partial(embed_kernel, ctx, steps, int(split)),
         out_shape=outs,
-        grid=(steps,),
-        in_specs=[
-            pl.BlockSpec((slides, 1, sub, part), lambda i: (0, 0, 0, i)),
-            pl.BlockSpec((part, features), lambda i: (i, 0)),
+        in_specs=[hbm] * 2,
+        out_specs=[hbm] * len(outs),
+        scratch_shapes=[
+            pltpu.VMEM((steps, slides, sub, part), BF16),
+            pltpu.VMEM((steps, part, features), BF16),
+            pltpu.VMEM((slides,) + shape, BF16),
+            pltpu.SemaphoreType.DMA((2, steps)),
+            pltpu.SemaphoreType.DMA((2, slides)),
         ],
-        out_specs=specs,
-        scratch_shapes=[pltpu.VMEM((slides * sub, features), F32)],
         compiler_params=pltpu.CompilerParams(vmem_limit_bytes=24 * MIB),
         name="embed",
     )(tile_embed, w_in)
@@ -171,60 +178,72 @@
     )(tile_counts, *pieces, w_qkv)
 
 
-def dilated_kernel(dp, ctx, block, sends, counts_ref, rows_ref, weight_ref, *refs):
-    out_refs, (rows, keys, values) = refs[:-3], refs[-3:]
+def packed_rows(portion, features):
+    return portion * (features // 128) + 16
+
+
+def dilated_kernel(dp, ctx, block, sends, counts_ref, rows_hbm, weight_ref, *refs):
+    out_refs, (rows, keys, values, ready) = refs[:-4], refs[-4:]
     me, mine = lax.axis_index("dp"), lax.axis_index("ctx")
-    count, features = rows_ref.shape
+    count, features = rows_hbm.shape
     portion = count // ctx
     each = portion // dp
+    quarter = count // 4
+    loads = []
+    for part in range(4):
+        span = pl.ds(part * quarter, quarter)
+        loads.append(pltpu.make_async_copy(rows_hbm.at[span], rows.at[span], ready.at[part]))
+        loads[-1].start()
     spot = iota((count, 1), 0)
     inner = spot % portion
     position = spot // portion * count + inner // each * (count // dp) + inner % each * ctx + mine
     is_valid = position < counts_ref[me]
-    project(rows_ref[...], weight_ref, is_valid, keys, values)
     counted = jnp.broadcast_to(is_valid.astype(F32), (count, 128)).astype(BF16)
-    if sends is None:
-        source = rows_ref
-    else:
-        source = rows
-        for place, other in enumerate(sends):
+    for load in loads:
+        load.wait()
+    project(rows[...], weight_ref, is_valid, keys, values)
+    portions = block // portion
+    for start in range(0, len(sends), portions):
+        some = sends[start : start + portions]
+        wanted = []
+        for other in some:
             at = pl.multiple_of((mine ^ other) * portion, portion)
-            rows[place * portion : (place + 1) * portion, :] = rows_ref[pl.ds(at, portion), :]
-    for start in range(0, count, block):
+            wanted.append(rows[pl.ds(at, portion), :])
 
         def spread(columns, out):
-            for at in range(start, start + block, portion):
-                piece = out[at - start : at - start + portion]
-                if sends is None:
-                    out_refs[0][at : at + portion, columns] = piece
-                else:
-                    out_refs[at // portion][:, columns] = piece
+            for place in range(len(some)):
+                first = columns.start // 128 * portion
+                out_refs[start + place][first : first + portion, :] = out[place * portion : (place + 1) * portion]
 
         def put_total(logs):
             high = logs.astype(BF16).astype(F32)
             low = logs - high
             lane = iota((1, 128), 1)
             both = jnp.where(lane < 16, high, pltpu.roll(low, 16, 1))
-            spread(slice(features, features + 128), jnp.where(lane < 32, both, 0.0).astype(BF16))
-
-        attend(queries_of(source[start : start + block, :], weight_ref), keys, values, counted, spread, put_total)
+            both = jnp.where(lane < 32, both, 0.0)
+            for place in range(len(some)):
+                merged = both[place * portion : place * portion + 16]
+                for group in range(1, portion // 16):
+                    at = place * portion + group * 16
+                    merged = merged + pltpu.roll(both[at : at + 16], 32 * group, 1)
+                out_refs[start + place][-16:, :] = merged.astype(BF16)
+
+        attend(queries_of(jnp.concatenate(wanted, axis=0), weight_ref), keys, values, counted, spread, put_total)
 
 
 def dilated_attention(tile_counts, rows, w_qkv, dp, ctx, sends):
     count, features = rows.shape
+    portion = count // ctx
     vmem = pl.BlockSpec(memory_space=pltpu.VMEM)
-    if sends is None:
-        outs = [jax.ShapeDtypeStruct((count, features + 128), BF16)]
-    else:
-        outs = [jax.ShapeDtypeStruct((count // ctx, features + 128), BF16)] * ctx
+    outs = [jax.ShapeDtypeStruct((packed_rows(portion, features), 128), BF16)] * len(sends)
     return pl.pallas_call(
         functools.partial(dilated_kernel, dp, ctx, min(256, count), sends),
         out_shape=outs,
-        in_specs=[pl.BlockSpec(memory_space=pltpu.SMEM)] + [vmem] * 2,
+        in_specs=[pl.BlockSpec(memory_space=pltpu.SMEM), pl.BlockSpec(memory_space=pltpu.HBM), vmem],
         out_specs=[vmem] * len(outs),
-        scratch_shapes=[pltpu.VMEM((count, features), BF16)] * 3,
+        scratch_shapes=[pltpu.VMEM((count, features), BF16)] * 3 + [pltpu.SemaphoreType.DMA((4,))],
         compiler_params=pltpu.CompilerParams(vmem_limit_bytes=24 * MIB),
-        cost_estimate=pl.CostEstimate(flops=9 * 10**9, bytes_accessed=8 * 10**6, transcendentals=0),
+        cost_estimate=pl.CostEstimate(flops=6 * 10**9, bytes_accessed=5 * 10**6, transcendentals=0),
         name="dilated",
     )(tile_counts, rows, w_qkv)
 
@@ -238,10 +257,16 @@
     if sends is None:
         dilated[...] = received[0][...]
     else:
+        portion = count // ctx
         for other, piece in zip(sends, received):
             for part in range(dp):
                 at = pl.multiple_of(part * sub + (mine ^ other) * each, each)
-                dilated[pl.ds(at, each), :] = piece[part * each : (part + 1) * each, :]
+                for block in range(features // 128):
+                    first = block * portion + part * each
+                    dilated[pl.ds(at, each), block * 128 : (block + 1) * 128] = piece[first : first + each, :]
+                dilated[pl.ds(at, each), features:] = pltpu.roll(
+                    piece[-16:, :].astype(F32), (128 - 32 * part) % 128, 1
+                ).astype(BF16)
     lane = iota((1, 128), 1)
     heads = iota((128, features), 0) == iota((128, features), 1) // (features // HEAD_TOTAL)
     heads = heads.astype(BF16)
@@ -300,18 +325,25 @@
     regrouped = lax.all_to_all(
         by_residue.reshape(ctx * dp, each, features), ("ctx", "dp"), split_axis=0, concat_axis=0, tiled=True
     ).reshape(count, features)
-    pieces = [exchange(piece, "dp", other) for other, piece in enumerate(made)]
+    pieces = [exchange(piece, "dp", other).reshape(sub, features) for other, piece in enumerate(made)]
     out, logs = local_attention(tile_counts, pieces, w_qkv, ctx)
+    regrouped, out, logs = lax.optimization_barrier((regrouped, out, logs))
+    portion = count // ctx
     if aligned:
-        sends = [4, 5, 6, 7, 2, 3, 1, 0] if ctx == 8 else list(range(ctx))
-        made = dilated_attention(tile_counts, regrouped, w_qkv, dp, ctx, sends)
-        received = [exchange(piece, "ctx", other) for other, piece in zip(sends, made)]
+        sends, received = [], []
+        for some in ([4, 5, 6, 7], [2, 3, 1, 0]) if ctx == 8 else (list(range(ctx)),):
+            made = dilated_attention(tile_counts, regrouped, w_qkv, dp, ctx, some)
+            received += [exchange(piece, "ctx", other) for other, piece in zip(some, made)]
+            sends += some
     else:
+        made = dilated_attention(tile_counts, regrouped, w_qkv, dp, ctx, list(range(ctx)))
+        order = jnp.stack([lax.axis_index("ctx") ^ other for other in range(ctx)])
+        packed = lax.all_to_all(jnp.stack(made)[order], "ctx", split_axis=0, concat_axis=0, tiled=True)
+        wide = packed[:, :-16].reshape(ctx, features // 128, portion, 128).swapaxes(1, 2).reshape(ctx, portion, features)
+        lanes = packed[:, -16:].reshape(ctx, 16, 4, 32).swapaxes(1, 2)[:, : portion // 16].reshape(ctx, portion, 32)
+        whole = jnp.concatenate([wide, jnp.pad(lanes, ((0, 0), (0, 0), (0, 96)))], axis=-1)
+        received = [whole.reshape(ctx, dp, each, -1).swapaxes(0, 1).reshape(count, -1)]
         sends = None
-        made = dilated_attention(tile_counts, regrouped, w_qkv, dp, ctx, sends)[0]
-        received = lax.all_to_all(made.reshape(ctx, count // ctx, -1), "ctx", split_axis=0, concat_axis=0, tiled=True)
-        received = received.reshape(ctx, dp, each, -1).swapaxes(0, 1).reshape(count, -1)
-        received = [received]
     return merge(tile_counts, out, logs, w_out, received, dp, ctx, sends)
 
 

time: 74.9 us -> 78 us (1.041)
  waiting for transfers between devices: 29.9 us -> 23.3 us
  Pallas kernels: 20.8 us -> 25.8 us
  starting transfers between devices: 18.8 us -> 21.4 us
  local copies, waits for them, and re-layouts: 5.08 us -> 7.08 us
    all_to_all x1, waiting for transfers between devices: 18.6 us -> 0.01 us  [body(): lax.all_to_all(by_residue.reshape(ctx * dp, each, features), ('ctx', 'dp'...]
    ppermute x10, waiting for transfers between devices: 11.3 us -> 23.3 us  [exchange(): lax.ppermute(value, axis, [(i, i ^ other) for i in range(lax.axis_size(ax...]
    pallas_call x1 -> x2, Pallas kernels: 6.52 us -> 11.4 us  [dilated_attention(): pl.pallas_call(functools.partial(dilated_kernel, dp, ctx, min(256, count)...]
    ppermute x10, starting transfers between devices: 11.5 us -> 14 us  [exchange(): lax.ppermute(value, axis, [(i, i ^ other) for i in range(lax.axis_size(ax...]
    unnamed x12, local copies, waits for them, and re-layouts: 5.08 us -> 7.08 us
  transfers between devices with their start and end apart: 11 -> 11, of which waited for: 3 -> 5; matrix products, arithmetic and copies ran while one was open for 0% -> 0% of each run, Pallas kernels for 18% -> 16%
where the time goes in v2:
time: 78 us; the launch traced here: 77.7 us
  Pallas kernels  25.8 us (33%)
  waiting for transfers between devices  23.3 us (30%)
  starting transfers between devices  21.4 us (27%)
  local copies, waits for them, and re-layouts  7.08 us (9%)
    ppermute x10, waiting for transfers between devices, exchange(): lax.ppermute(value, axis, [(i, i ^ other) for i in range(lax.axis_size(ax...  23.3 us
    ppermute x10, starting transfers between devices, exchange(): lax.ppermute(value, axis, [(i, i ^ other) for i in range(lax.axis_size(ax...  14 us
    pallas_call x2, Pallas kernels, dilated_attention(): pl.pallas_call(functools.partial(dilated_kernel, dp, ctx, min(256, count)...  11.4 us
    all_to_all x1, starting transfers between devices, body(): lax.all_to_all(by_residue.reshape(ctx * dp, each, features), ('ctx', 'dp'...  7.48 us
    unnamed x12, local copies, waits for them, and re-layouts  7.08 us
    pallas_call x1, Pallas kernels, local_attention(): pl.pallas_call(functools.partial(local_kernel, dp, ctx, min(256, count)),...  6.53 us
    pallas_call x1, Pallas kernels, merge(): pl.pallas_call(functools.partial(merge_kernel, dp, ctx, sends), out_shape...  3.98 us
    pallas_call x1, Pallas kernels, embed(): pl.pallas_call(functools.partial(embed_kernel, ctx, steps, int(split)), o...  3.88 us
  transfers between devices with their start and end apart: 11, of which 5 were waited for; matrix products, arithmetic and copies ran while one was open for 0% of the time, Pallas kernels for 16%

profile of v2, /device:TPU:0, one launch (start us, length us, event | category | flops | bytes accessed | tf_op | source)
XLA Modules:
  0.0 77.7 jit_solution(14044274653360188670)
XLA Ops:
  0.0 1.7 %copy-done = bf16[1536,768]{1,0:T(8,128)(2,1)S(1)} copy-done((bf16[1536,768]{1,0:T(8,128)(2,1)S(1)}, bf16[1536,768]{1,0:T(8,128)(2,1)}, u32[]{:S(2)}) %copy-start) | copy-done | bytes 2359320
  1.7 1.4 %copy-done.1 = bf16[4,1,128,1536]{3,2,1,0:T(8,128)(2,1)S(1)} copy-done((bf16[4,1,128,1536]{3,2,1,0:T(8,128)(2,1)S(1)}, bf16[4,1,128,1536]{3,2,1,0:T(8,128)(2,1)}, u32[]{:S(2)}) %copy-start.1) | copy-done | bytes 1572888
  3.1 3.9 %embed.1 = (bf16[8,4,16,768]{3,2,1,0:T(8,128)(2,1)}, bf16[8,16,768]{2,1,0:T(8,128)(2,1)S(1)}, bf16[8,16,768]{2,1,0:T(8,128)(2,1)S(1)}, bf16[8,16,768]{2,1,0:T(8,128)(2,1)S(1)}, bf16[8,16,768]{2,1,0:T(8,128)(2,1)S(1)}) custom-call(bf16[4,1,128,1536]{3,2,1,0:T(8,128)(2,1)S(1)} %copy-done.1, bf16[1536,768]{1,0:T(8,128)(2,1)S(1)} %copy-done), custom_call_target="tpu_custom_call" | custom-call | tf_op jit(solution)/shard_map/embed/pallas_call | solution.py:81
  7.0 7.5 %all-to-all-start = ((bf16[32,16,768]{2,1,0:T(8,128)(2,1)}), bf16[32,16,768]{2,1,0:T(8,128)(2,1)S(1)}, u32[]{:S(2)}, u32[]{:S(2)}) async-start(bf16[32,16,768]{2,1,0:T(8,128)(2,1)} %bitcast), calls=%async_computation | async-start | bytes 1572864 | tf_op jit(solution)/shard_map/all_to_all | solution.py:325
  14.5 0.1 collective-permute-start
  14.6 1.7 %collective-permute-start.1 = (bf16[8,16,768]{2,1,0:T(8,128)(2,1)S(1)}, bf16[8,16,768]{2,1,0:T(8,128)(2,1)S(1)}, u32[]{:S(2)}, u32[]{:S(2)}) collective-permute-start(bf16[8,16,768]{2,1,0:T(8,128)(2,1)S(1)} %get-tuple-element.26), channel_id=1, source_target_pairs={{0,16},{8,24},{16,0},{24,8},{1,17},{9,25},{17,1},{25,9},{2,18},{10... | collective-permute-start | bytes 589832 | tf_op jit(solution)/shard_map/ppermute | solution.py:308
  16.3 0.1 collective-permute-start.2
  16.4 12.5 %collective-permute-done.1 = bf16[8,16,768]{2,1,0:T(8,128)(2,1)S(1)} collective-permute-done((bf16[8,16,768]{2,1,0:T(8,128)(2,1)S(1)}, bf16[8,16,768]{2,1,0:T(8,128)(2,1)S(1)}, u32[]{:S(2)}, u32[]{:S(2)}) %collective-permute-start.1) | collective-permute-done | bytes 196640 | tf_op jit(solution)/shard_map/ppermute | solution.py:308
  28.9 3.6 %collective-permute-done.2 = bf16[8,16,768]{2,1,0:T(8,128)(2,1)S(1)} collective-permute-done((bf16[8,16,768]{2,1,0:T(8,128)(2,1)S(1)}, bf16[8,16,768]{2,1,0:T(8,128)(2,1)S(1)}, u32[]{:S(2)}, u32[]{:S(2)}) %collective-permute-start.2) | collective-permute-done | bytes 196640 | tf_op jit(solution)/shard_map/ppermute | solution.py:308
  32.5 2.0 %copy-done.4 = bf16[768,2304]{1,0:T(8,128)(2,1)S(1)} copy-done((bf16[768,2304]{1,0:T(8,128)(2,1)S(1)}, bf16[768,2304]{1,0:T(8,128)(2,1)}, u32[]{:S(2)}) %copy-start.4) | copy-done | bytes 3538968
  34.5 6.5 %local.1 = (bf16[512,768]{1,0:T(8,128)(2,1)S(1)}, f32[512,128]{1,0:T(8,128)S(1)}) custom-call(s32[4]{0:T(128)S(1)} %copy-done.3, bf16[128,768]{1,0:T(8,128)(2,1)S(1)} %bitcast.8, bf16[128,768]{1,0:T(8,128)(2,1)S(1)} %bitcast.9, bf16[128,768]{1,0:T(8,128)(2,1)S(1)} %bitcast.10, bf16[128,768]{1,0:T(8,128)(2,1)S(1)} %bitcast.11, bf16[768,2304]{1,0:T(8,128)(2,1)S(1)} %copy-done.4), custom_call_target="tpu_custom_call" | custom-call | flops 8999999488 | bytes 8000000 | tf_op jit(solution)/shard_map/local/pallas_call | solution.py:169
  41.0 2.0 %copy-done.5 = bf16[768,2304]{1,0:T(8,128)(2,1)S(1)} copy-done((bf16[768,2304]{1,0:T(8,128)(2,1)S(1)}, bf16[768,2304]{1,0:T(8,128)(2,1)}, u32[]{:S(2)}) %copy-start.5) | copy-done | bytes 3538968
  43.0 5.6 %dilated.2 = (bf16[400,128]{1,0:T(8,128)(2,1)S(1)}, bf16[400,128]{1,0:T(8,128)(2,1)S(1)}, bf16[400,128]{1,0:T(8,128)(2,1)S(1)}, bf16[400,128]{1,0:T(8,128)(2,1)S(1)}) custom-call(s32[4]{0:T(128)S(1)} %copy-done.3, bf16[512,768]{1,0:T(8,128)(2,1)S(1)} %bitcast.6, bf16[768,2304]{1,0:T(8,128)(2,1)S(1)} %copy-done.5), custom_call_target="tpu_custom_call" | custom-call | flops 6000000000 | bytes 5000000 | tf_op jit(solution)/shard_map/dilated/pallas_call | solution.py:239
  48.6 3.6 %collective-permute-start.3 = (bf16[400,128]{1,0:T(8,128)(2,1)S(1)}, bf16[400,128]{1,0:T(8,128)(2,1)S(1)}, u32[]{:S(2)}, u32[]{:S(2)}) collective-permute-start(bf16[400,128]{1,0:T(8,128)(2,1)S(1)} %get-tuple-element.33), channel_id=1, source_target_pairs={{0,4},{1,5},{2,6},{3,7},{4,0},{5,1},{6,2},{7,3},{8,12},{9,13},{10,... | collective-permute-start | bytes 307208 | tf_op jit(solution)/shard_map/ppermute | solution.py:308
  52.2 0.9 %collective-permute-start.4 = (bf16[400,128]{1,0:T(8,128)(2,1)S(1)}, bf16[400,128]{1,0:T(8,128)(2,1)S(1)}, u32[]{:S(2)}, u32[]{:S(2)}) collective-permute-start(bf16[400,128]{1,0:T(8,128)(2,1)S(1)} %get-tuple-element.34), channel_id=1, source_target_pairs={{0,5},{1,4},{2,7},{3,6},{4,1},{5,0},{6,3},{7,2},{8,13},{9,12},{10,... | collective-permute-start | bytes 307208 | tf_op jit(solution)/shard_map/ppermute | solution.py:308
  53.1 5.8 %dilated.3 = (bf16[400,128]{1,0:T(8,128)(2,1)S(1)}, bf16[400,128]{1,0:T(8,128)(2,1)S(1)}, bf16[400,128]{1,0:T(8,128)(2,1)S(1)}, bf16[400,128]{1,0:T(8,128)(2,1)S(1)}) custom-call(s32[4]{0:T(128)S(1)} %copy-done.3, bf16[512,768]{1,0:T(8,128)(2,1)S(1)} %bitcast.7, bf16[768,2304]{1,0:T(8,128)(2,1)S(1)} %copy-done.5), custom_call_target="tpu_custom_call" | custom-call | flops 6000000000 | bytes 5000000 | tf_op jit(solution)/shard_map/dilated/pallas_call | solution.py:239
  59.0 4.0 %collective-permute-start.5 = (bf16[400,128]{1,0:T(8,128)(2,1)S(1)}, bf16[400,128]{1,0:T(8,128)(2,1)S(1)}, u32[]{:S(2)}, u32[]{:S(2)}) collective-permute-start(bf16[400,128]{1,0:T(8,128)(2,1)S(1)} %get-tuple-element.35), channel_id=1, source_target_pairs={{0,6},{1,7},{2,4},{3,5},{4,2},{5,3},{6,0},{7,1},{8,14},{9,15},{10,... | collective-permute-start | bytes 307208 | tf_op jit(solution)/shard_map/ppermute | solution.py:308
  63.0 0.0 collective-permute-start.6
  63.0 3.0 %collective-permute-start.8 = (bf16[400,128]{1,0:T(8,128)(2,1)S(1)}, bf16[400,128]{1,0:T(8,128)(2,1)S(1)}, u32[]{:S(2)}, u32[]{:S(2)}) collective-permute-start(bf16[400,128]{1,0:T(8,128)(2,1)S(1)} %get-tuple-element.38), channel_id=1, source_target_pairs={{0,3},{1,2},{2,1},{3,0},{4,7},{5,6},{6,5},{7,4},{8,11},{9,10},{10,... | collective-permute-start | bytes 307208 | tf_op jit(solution)/shard_map/ppermute | solution.py:308
  66.0 0.5 collective-permute-start.9
  66.5 5.0 %collective-permute-done.6.refs_3_ = bf16[400,128]{1,0:T(8,128)(2,1)S(1)} collective-permute-done((bf16[400,128]{1,0:T(8,128)(2,1)S(1)}, bf16[400,128]{1,0:T(8,128)(2,1)S(1)}, u32[]{:S(2)}, u32[]{:S(2)}) %collective-permute-start.6) | collective-permute-done | bytes 102432 | tf_op jit(solution)/shard_map/ppermute | solution.py:308
  71.5 1.2 %collective-permute-done.8.refs_5_ = bf16[400,128]{1,0:T(8,128)(2,1)S(1)} collective-permute-done((bf16[400,128]{1,0:T(8,128)(2,1)S(1)}, bf16[400,128]{1,0:T(8,128)(2,1)S(1)}, u32[]{:S(2)}, u32[]{:S(2)}) %collective-permute-start.8) | collective-permute-done | bytes 102432 | tf_op jit(solution)/shard_map/ppermute | solution.py:308
  72.7 1.0 %collective-permute-done.9.refs_6_ = bf16[400,128]{1,0:T(8,128)(2,1)S(1)} collective-permute-done((bf16[400,128]{1,0:T(8,128)(2,1)S(1)}, bf16[400,128]{1,0:T(8,128)(2,1)S(1)}, u32[]{:S(2)}, u32[]{:S(2)}) %collective-permute-start.9) | collective-permute-done | bytes 102432 | tf_op jit(solution)/shard_map/ppermute | solution.py:308
  73.7 4.0 %merge.1 = bf16[1,512,768]{2,1,0:T(8,128)(2,1)} custom-call(s32[4]{0:T(128)S(1)} %copy-done.3, bf16[512,768]{1,0:T(8,128)(2,1)S(1)} %get-tuple-element.30.out_ref, f32[512,128]{1,0:T(8,128)S(1)} %get-tuple-element.31.log_ref, bf16[768,768]{1,0:T(8,128)(2,1)S(1)} %copy-done.2, bf16[400,128]{1,0:T(8,128)(2,1)S(1)} %collective-permute-done.3.refs_0_, ...), custom_call_target="tpu_custom_call" | custom-call | tf_op jit(solution)/shard_map/merge/pallas_call | solution.py:294
  (15 shorter events, 0.0 us)
Async XLA Ops:
  0.0 1.7 %copy-start = (bf16[1536,768]{1,0:T(8,128)(2,1)S(1)}, bf16[1536,768]{1,0:T(8,128)(2,1)}, u32[]{:S(2)}) copy-start(bf16[1536,768]{1,0:T(8,128)(2,1)} %w_hbm.1) | copy-start | bytes 7077892
  1.7 1.4 %copy-start.1 = (bf16[4,1,128,1536]{3,2,1,0:T(8,128)(2,1)S(1)}, bf16[4,1,128,1536]{3,2,1,0:T(8,128)(2,1)}, u32[]{:S(2)}) copy-start(bf16[4,1,128,1536]{3,2,1,0:T(8,128)(2,1)} %x_hbm.1) | copy-start | bytes 4718596
  3.1 29.4 %copy-start.3 = (s32[4]{0:T(128)S(1)}, s32[4]{0:T(128)}, u32[]{:S(2)}) copy-start(s32[4]{0:T(128)} %counts_ref.7) | copy-start | bytes 52
  7.0 34.0 %all-to-all-start = ((bf16[32,16,768]{2,1,0:T(8,128)(2,1)}), bf16[32,16,768]{2,1,0:T(8,128)(2,1)S(1)}, u32[]{:S(2)}, u32[]{:S(2)}) async-start(bf16[32,16,768]{2,1,0:T(8,128)(2,1)} %bitcast), calls=%async_computation | async-start | bytes 1572864 | tf_op jit(solution)/shard_map/all_to_all | solution.py:325
  14.5 1.9 %collective-permute-start = (bf16[8,16,768]{2,1,0:T(8,128)(2,1)S(1)}, bf16[8,16,768]{2,1,0:T(8,128)(2,1)S(1)}, u32[]{:S(2)}, u32[]{:S(2)}) collective-permute-start(bf16[8,16,768]{2,1,0:T(8,128)(2,1)S(1)} %get-tuple-element.25), channel_id=1, source_target_pairs={{0,8},{8,0},{16,24},{24,16},{1,9},{9,1},{17,25},{25,17},{2,10},{10... | collective-permute-start | bytes 589832 | tf_op jit(solution)/shard_map/ppermute | solution.py:308
  14.6 14.3 %collective-permute-start.1 = (bf16[8,16,768]{2,1,0:T(8,128)(2,1)S(1)}, bf16[8,16,768]{2,1,0:T(8,128)(2,1)S(1)}, u32[]{:S(2)}, u32[]{:S(2)}) collective-permute-start(bf16[8,16,768]{2,1,0:T(8,128)(2,1)S(1)} %get-tuple-element.26), channel_id=1, source_target_pairs={{0,16},{8,24},{16,0},{24,8},{1,17},{9,25},{17,1},{25,9},{2,18},{10... | collective-permute-start | bytes 589832 | tf_op jit(solution)/shard_map/ppermute | solution.py:308
  16.3 16.2 %collective-permute-start.2 = (bf16[8,16,768]{2,1,0:T(8,128)(2,1)S(1)}, bf16[8,16,768]{2,1,0:T(8,128)(2,1)S(1)}, u32[]{:S(2)}, u32[]{:S(2)}) collective-permute-start(bf16[8,16,768]{2,1,0:T(8,128)(2,1)S(1)} %get-tuple-element.27), channel_id=1, source_target_pairs={{0,24},{8,16},{16,8},{24,0},{1,25},{9,17},{17,9},{25,1},{2,26},{10... | collective-permute-start | bytes 589832 | tf_op jit(solution)/shard_map/ppermute | solution.py:308
  32.5 2.0 %copy-start.4 = (bf16[768,2304]{1,0:T(8,128)(2,1)S(1)}, bf16[768,2304]{1,0:T(8,128)(2,1)}, u32[]{:S(2)}) copy-start(bf16[768,2304]{1,0:T(8,128)(2,1)} %weight_ref.4) | copy-start | bytes 10616836
  41.0 2.0 %copy-start.5 = (bf16[768,2304]{1,0:T(8,128)(2,1)S(1)}, bf16[768,2304]{1,0:T(8,128)(2,1)}, u32[]{:S(2)}) copy-start(bf16[768,2304]{1,0:T(8,128)(2,1)} %weight_ref.4) | copy-start | bytes 10616836
  48.6 14.4 %collective-permute-start.3 = (bf16[400,128]{1,0:T(8,128)(2,1)S(1)}, bf16[400,128]{1,0:T(8,128)(2,1)S(1)}, u32[]{:S(2)}, u32[]{:S(2)}) collective-permute-start(bf16[400,128]{1,0:T(8,128)(2,1)S(1)} %get-tuple-element.33), channel_id=1, source_target_pairs={{0,4},{1,5},{2,6},{3,7},{4,0},{5,1},{6,2},{7,3},{8,12},{9,13},{10,... | collective-permute-start | bytes 307208 | tf_op jit(solution)/shard_map/ppermute | solution.py:308
  52.2 21.5 %copy-start.2 = (bf16[768,768]{1,0:T(8,128)(2,1)S(1)}, bf16[768,768]{1,0:T(8,128)(2,1)}, u32[]{:S(2)}) copy-start(bf16[768,768]{1,0:T(8,128)(2,1)} %weight_ref.5) | copy-start | bytes 3538948
  52.2 13.8 %collective-permute-start.4 = (bf16[400,128]{1,0:T(8,128)(2,1)S(1)}, bf16[400,128]{1,0:T(8,128)(2,1)S(1)}, u32[]{:S(2)}, u32[]{:S(2)}) collective-permute-start(bf16[400,128]{1,0:T(8,128)(2,1)S(1)} %get-tuple-element.34), channel_id=1, source_target_pairs={{0,5},{1,4},{2,7},{3,6},{4,1},{5,0},{6,3},{7,2},{8,13},{9,12},{10,... | collective-permute-start | bytes 307208 | tf_op jit(solution)/shard_map/ppermute | solution.py:308
  59.0 7.5 %collective-permute-start.5 = (bf16[400,128]{1,0:T(8,128)(2,1)S(1)}, bf16[400,128]{1,0:T(8,128)(2,1)S(1)}, u32[]{:S(2)}, u32[]{:S(2)}) collective-permute-start(bf16[400,128]{1,0:T(8,128)(2,1)S(1)} %get-tuple-element.35), channel_id=1, source_target_pairs={{0,6},{1,7},{2,4},{3,5},{4,2},{5,3},{6,0},{7,1},{8,14},{9,15},{10,... | collective-permute-start | bytes 307208 | tf_op jit(solution)/shard_map/ppermute | solution.py:308
  63.0 8.5 %collective-permute-start.6 = (bf16[400,128]{1,0:T(8,128)(2,1)S(1)}, bf16[400,128]{1,0:T(8,128)(2,1)S(1)}, u32[]{:S(2)}, u32[]{:S(2)}) collective-permute-start(bf16[400,128]{1,0:T(8,128)(2,1)S(1)} %get-tuple-element.36), channel_id=1, source_target_pairs={{0,7},{1,6},{2,5},{3,4},{4,3},{5,2},{6,1},{7,0},{8,15},{9,14},{10,... | collective-permute-start | bytes 307208 | tf_op jit(solution)/shard_map/ppermute | solution.py:308
  63.0 8.5 %collective-permute-start.7 = (bf16[400,128]{1,0:T(8,128)(2,1)S(1)}, bf16[400,128]{1,0:T(8,128)(2,1)S(1)}, u32[]{:S(2)}, u32[]{:S(2)}) collective-permute-start(bf16[400,128]{1,0:T(8,128)(2,1)S(1)} %get-tuple-element.37), channel_id=1, source_target_pairs={{0,2},{1,3},{2,0},{3,1},{4,6},{5,7},{6,4},{7,5},{8,10},{9,11},{10,... | collective-permute-start | bytes 307208 | tf_op jit(solution)/shard_map/ppermute | solution.py:308
  63.0 9.7 %collective-permute-start.8 = (bf16[400,128]{1,0:T(8,128)(2,1)S(1)}, bf16[400,128]{1,0:T(8,128)(2,1)S(1)}, u32[]{:S(2)}, u32[]{:S(2)}) collective-permute-start(bf16[400,128]{1,0:T(8,128)(2,1)S(1)} %get-tuple-element.38), channel_id=1, source_target_pairs={{0,3},{1,2},{2,1},{3,0},{4,7},{5,6},{6,5},{7,4},{8,11},{9,10},{10,... | collective-permute-start | bytes 307208 | tf_op jit(solution)/shard_map/ppermute | solution.py:308
  66.0 7.7 %collective-permute-start.9 = (bf16[400,128]{1,0:T(8,128)(2,1)S(1)}, bf16[400,128]{1,0:T(8,128)(2,1)S(1)}, u32[]{:S(2)}, u32[]{:S(2)}) collective-permute-start(bf16[400,128]{1,0:T(8,128)(2,1)S(1)} %get-tuple-element.39), channel_id=1, source_target_pairs={{0,1},{1,0},{2,3},{3,2},{4,5},{5,4},{6,7},{7,6},{8,9},{9,8},{10,11... | collective-permute-start | bytes 307208 | tf_op jit(solution)/shard_map/ppermute | solution.py:308

commit v3 on v2

--- a/solution.py
+++ b/solution.py
@@ -46,19 +46,18 @@
             load.wait()
         product = dot(x_parts[step].reshape(slides * sub, part), w_parts[step])
         total = product if total is None else total + product
-    hidden = total.astype(BF16).astype(F32)
-    centered = hidden - jnp.mean(hidden, axis=-1, keepdims=True)
-    variance = jnp.mean(centered * centered, axis=-1, keepdims=True)
-    normed = (centered * lax.rsqrt(variance + EPSILON)).astype(BF16)
     me = lax.axis_index("dp")
     each = sub // ctx
     target, source = iota((sub, sub), 0), iota((sub, sub), 1)
     order = (source == target % each * ctx + target // each).astype(BF16)
+    stores = []
     for slide in range(slides):
-        made[slide] = dot(order, normed[slide * sub : (slide + 1) * sub]).astype(BF16).reshape(made.shape[1:])
-    stores = []
-    if split:
-        for slide in range(slides):
+        hidden = total[slide * sub : (slide + 1) * sub].astype(BF16).astype(F32)
+        centered = hidden - jnp.mean(hidden, axis=-1, keepdims=True)
+        variance = jnp.mean(centered * centered, axis=-1, keepdims=True)
+        normed = (centered * lax.rsqrt(variance + EPSILON)).astype(BF16)
+        made[slide] = dot(order, normed).astype(BF16).reshape(made.shape[1:])
+        if split:
             stores.append(pltpu.make_async_copy(made.at[slide], outs[0].at[:, slide], sent.at[1, slide]))
             stores[-1].start()
     for other in range(slides):
@@ -71,7 +70,7 @@
 def embed(tile_embed, w_in, ctx, split):
     slides, _, sub, width = tile_embed.shape
     features = w_in.shape[1]
-    steps = 3
+    steps = 6
     part = width // steps
     shape = (ctx, sub // ctx, features) if split else (sub, features)
     outs = [jax.ShapeDtypeStruct(shape, BF16)] * slides
@@ -90,9 +89,29 @@
             pltpu.SemaphoreType.DMA((2, steps)),
             pltpu.SemaphoreType.DMA((2, slides)),
         ],
-        compiler_params=pltpu.CompilerParams(vmem_limit_bytes=24 * MIB),
+        compiler_params=pltpu.CompilerParams(vmem_limit_bytes=60 * MIB),
         name="embed",
     )(tile_embed, w_in)
+
+
+def fetch_kernel(source, after, kept, ready):
+    copy = pltpu.make_async_copy(source, kept, ready)
+    copy.start()
+    copy.wait()
+
+
+def fetch(value, after):
+    hbm = pl.BlockSpec(memory_space=pltpu.HBM)
+    return pl.pallas_call(
+        fetch_kernel,
+        out_shape=jax.ShapeDtypeStruct(value.shape, value.dtype),
+        in_specs=[hbm] * 2,
+        out_specs=pl.BlockSpec(memory_space=pltpu.VMEM),
+        scratch_shapes=[pltpu.SemaphoreType.DMA],
+        compiler_params=pltpu.CompilerParams(vmem_limit_bytes=50 * MIB),
+        cost_estimate=pl.CostEstimate(flops=0, bytes_accessed=8 * 10**6, transcendentals=0),
+        name="fetch",
+    )(value, after)
 
 
 def project(rows, weight_ref, is_valid, keys, values):
@@ -173,7 +192,7 @@
         out_specs=[vmem] * 2,
         scratch_shapes=[pltpu.VMEM((count, features), BF16)] * 3,
         compiler_params=pltpu.CompilerParams(vmem_limit_bytes=24 * MIB),
-        cost_estimate=pl.CostEstimate(flops=9 * 10**9, bytes_accessed=8 * 10**6, transcendentals=0),
+        cost_estimate=pl.CostEstimate(flops=10**12, bytes_accessed=10**10, transcendentals=0),
         name="local",
     )(tile_counts, *pieces, w_qkv)
 
@@ -182,26 +201,22 @@
     return portion * (features // 128) + 16
 
 
-def dilated_kernel(dp, ctx, block, sends, counts_ref, rows_hbm, weight_ref, *refs):
-    out_refs, (rows, keys, values, ready) = refs[:-4], refs[-4:]
+def dilated_kernel(dp, ctx, block, sends, first_call, counts_ref, rows, weight_ref, *refs):
+    if first_call:
+        out_refs, (keys, values) = refs[:-2], refs[-2:]
+    else:
+        (keys, values), out_refs = refs[:2], refs[2:]
     me, mine = lax.axis_index("dp"), lax.axis_index("ctx")
-    count, features = rows_hbm.shape
+    count, features = rows.shape
     portion = count // ctx
     each = portion // dp
-    quarter = count // 4
-    loads = []
-    for part in range(4):
-        span = pl.ds(part * quarter, quarter)
-        loads.append(pltpu.make_async_copy(rows_hbm.at[span], rows.at[span], ready.at[part]))
-        loads[-1].start()
     spot = iota((count, 1), 0)
     inner = spot % portion
     position = spot // portion * count + inner // each * (count // dp) + inner % each * ctx + mine
     is_valid = position < counts_ref[me]
     counted = jnp.broadcast_to(is_valid.astype(F32), (count, 128)).astype(BF16)
-    for load in loads:
-        load.wait()
-    project(rows[...], weight_ref, is_valid, keys, values)
+    if first_call:
+        project(rows[...], weight_ref, is_valid, keys, values)
     portions = block // portion
     for start in range(0, len(sends), portions):
         some = sends[start : start + portions]
@@ -231,75 +246,132 @@
         attend(queries_of(jnp.concatenate(wanted, axis=0), weight_ref), keys, values, counted, spread, put_total)
 
 
-def dilated_attention(tile_counts, rows, w_qkv, dp, ctx, sends):
+def dilated_attention(tile_counts, rows, w_qkv, dp, ctx, sends, kept=()):
     count, features = rows.shape
     portion = count // ctx
     vmem = pl.BlockSpec(memory_space=pltpu.VMEM)
     outs = [jax.ShapeDtypeStruct((packed_rows(portion, features), 128), BF16)] * len(sends)
-    return pl.pallas_call(
-        functools.partial(dilated_kernel, dp, ctx, min(256, count), sends),
+    if not kept:
+        outs += [jax.ShapeDtypeStruct((count, features), BF16)] * 2
+    return pl.pallas_call(
+        functools.partial(dilated_kernel, dp, ctx, min(256, count), sends, not kept),
         out_shape=outs,
-        in_specs=[pl.BlockSpec(memory_space=pltpu.SMEM), pl.BlockSpec(memory_space=pltpu.HBM), vmem],
+        in_specs=[pl.BlockSpec(memory_space=pltpu.SMEM)] + [vmem] * (2 + len(kept)),
         out_specs=[vmem] * len(outs),
-        scratch_shapes=[pltpu.VMEM((count, features), BF16)] * 3 + [pltpu.SemaphoreType.DMA((4,))],
         compiler_params=pltpu.CompilerParams(vmem_limit_bytes=24 * MIB),
-        cost_estimate=pl.CostEstimate(flops=6 * 10**9, bytes_accessed=5 * 10**6, transcendentals=0),
+        cost_estimate=pl.CostEstimate(flops=10**6, bytes_accessed=10**4, transcendentals=0),
         name="dilated",
-    )(tile_counts, rows, w_qkv)
-
-
-def merge_kernel(dp, ctx, sends, counts_ref, out_ref, log_ref, weight_ref, *refs):
-    received, (mixed_ref, dilated) = refs[:-2], refs[-2:]
+    )(tile_counts, rows, w_qkv, *kept)
+
+
+def merge_rows(own, own_logs, features_of, logs, heads, weight):
+    lane = iota((1, 128), 1)
+    share = jnp.where(lane < HEAD_TOTAL, 1.0 / (1.0 + jnp.exp2(own_logs - logs)), 0.0)
+    high = share.astype(BF16)
+    low = (share - high.astype(F32)).astype(BF16)
+    wide = dot(high, heads) + dot(low, heads)
+    own = own.astype(F32)
+    merged = own + wide * (features_of.astype(F32) - own)
+    return dot(merged.astype(BF16), weight)
+
+
+def heads_of(features):
+    return (iota((128, features), 0) == iota((128, features), 1) // (features // HEAD_TOTAL)).astype(BF16)
+
+
+def merge_kernel(dp, ctx, counts_ref, out_ref, log_ref, weight_ref, dilated, mixed_ref):
     me, mine = lax.axis_index("dp"), lax.axis_index("ctx")
     count, features = out_ref.shape
     sub = count // dp
     each = sub // ctx
-    if sends is None:
-        dilated[...] = received[0][...]
-    else:
-        portion = count // ctx
-        for other, piece in zip(sends, received):
-            for part in range(dp):
-                at = pl.multiple_of(part * sub + (mine ^ other) * each, each)
-                for block in range(features // 128):
-                    first = block * portion + part * each
-                    dilated[pl.ds(at, each), block * 128 : (block + 1) * 128] = piece[first : first + each, :]
-                dilated[pl.ds(at, each), features:] = pltpu.roll(
-                    piece[-16:, :].astype(F32), (128 - 32 * part) % 128, 1
-                ).astype(BF16)
-    lane = iota((1, 128), 1)
-    heads = iota((128, features), 0) == iota((128, features), 1) // (features // HEAD_TOTAL)
-    heads = heads.astype(BF16)
+    heads = heads_of(features)
     target, source = iota((sub, sub), 0), iota((sub, sub), 1)
     order = (target == source % each * ctx + source // each).astype(BF16)
     for part in range(dp):
         rows = slice(part * sub, (part + 1) * sub)
         logs = dilated[rows, features:].astype(F32)
         logs = logs + pltpu.roll(logs, 128 - 16, 1)
-        share = jnp.where(lane < HEAD_TOTAL, 1.0 / (1.0 + jnp.exp2(log_ref[rows, :] - logs)), 0.0)
-        high = share.astype(BF16)
-        low = (share - high.astype(F32)).astype(BF16)
-        wide = dot(high, heads) + dot(low, heads)
-        own = out_ref[rows, :].astype(F32)
-        merged = own + wide * (dilated[rows, :features].astype(F32) - own)
+        mixed = merge_rows(out_ref[rows, :], log_ref[rows, :], dilated[rows, :features], logs, heads, weight_ref[...])
         inner = iota((sub, 1), 0)
         position = mine * count + part * sub + inner % each * ctx + inner // each
-        mixed = jnp.where(position < counts_ref[me], dot(merged.astype(BF16), weight_ref[...]), 0.0)
+        mixed = jnp.where(position < counts_ref[me], mixed, 0.0)
         mixed_ref[0, rows, :] = dot(order, mixed.astype(BF16)).astype(BF16)
 
 
-def merge(tile_counts, out, logs, w_out, received, dp, ctx, sends):
+def merge(tile_counts, out, logs, w_out, received, dp, ctx):
     count, features = out.shape
     vmem = pl.BlockSpec(memory_space=pltpu.VMEM)
     return pl.pallas_call(
-        functools.partial(merge_kernel, dp, ctx, sends),
+        functools.partial(merge_kernel, dp, ctx),
         out_shape=jax.ShapeDtypeStruct((1, count, features), BF16),
-        in_specs=[pl.BlockSpec(memory_space=pltpu.SMEM)] + [vmem] * (3 + len(received)),
+        in_specs=[pl.BlockSpec(memory_space=pltpu.SMEM)] + [vmem] * 4,
         out_specs=vmem,
-        scratch_shapes=[pltpu.VMEM((count, features + 128), BF16)],
         compiler_params=pltpu.CompilerParams(vmem_limit_bytes=24 * MIB),
         name="merge",
-    )(tile_counts, out, logs, w_out, *received)
+    )(tile_counts, out, logs, w_out, received)
+
+
+def merge_part_kernel(dp, ctx, sends, with_others, counts_ref, out_ref, log_ref, weight_ref, *refs):
+    pieces, refs = refs[: len(sends)], refs[len(sends) :]
+    mixed_ref, (dilated, own, own_logs) = refs[-4], refs[-3:]
+    me, mine = lax.axis_index("dp"), lax.axis_index("ctx")
+    count, features = out_ref.shape
+    sub = count // dp
+    each = sub // ctx
+    portion = count // ctx
+    span = len(sends) * each
+    first = (mine ^ sends[0]) // len(sends) * len(sends)
+    for part in range(dp):
+        at = pl.multiple_of(part * sub + first * each, each)
+        own[part * span : (part + 1) * span, :] = out_ref[pl.ds(at, span), :]
+        own_logs[part * span : (part + 1) * span, :] = log_ref[pl.ds(at, span), :]
+    for other, piece in zip(sends, pieces):
+        for part in range(dp):
+            at = pl.multiple_of(part * span + ((mine ^ other) - first) * each, each)
+            for block in range(features // 128):
+                start = block * portion + part * each
+                dilated[pl.ds(at, each), block * 128 : (block + 1) * 128] = piece[start : start + each, :]
+            dilated[pl.ds(at, each), features:] = pltpu.roll(
+                piece[-16:, :].astype(F32), (128 - 32 * part) % 128, 1
+            ).astype(BF16)
+    logs = dilated[:, features:].astype(F32)
+    logs = logs + pltpu.roll(logs, 128 - 16, 1)
+    mixed = merge_rows(own[...], own_logs[...], dilated[:, :features], logs, heads_of(features), weight_ref[...])
+    spot = iota((dp * span, 1), 0)
+    inner = spot % span
+    position = mine * count + spot // span * sub + inner % each * ctx + first + inner // each
+    mixed = jnp.where(position < counts_ref[me], mixed, 0.0).astype(BF16)
+    target, source = iota((sub, span), 0), iota((sub, span), 1)
+    order = (target == source % each * ctx + first + source // each).astype(BF16)
+    for part in range(dp):
+        made = dot(order, mixed[part * span : (part + 1) * span])
+        rows = slice(part * sub, (part + 1) * sub)
+        if with_others:
+            made = made + refs[0][rows, :].astype(F32)
+            mixed_ref[0, rows, :] = made.astype(BF16)
+        else:
+            mixed_ref[rows, :] = made.astype(BF16)
+
+
+def merge_part(tile_counts, out, logs, w_out, received, dp, ctx, sends, others=()):
+    count, features = out.shape
+    vmem = pl.BlockSpec(memory_space=pltpu.VMEM)
+    shape = (1, count, features) if others else (count, features)
+    rows = count * len(sends) // ctx
+    return pl.pallas_call(
+        functools.partial(merge_part_kernel, dp, ctx, sends, len(others)),
+        out_shape=jax.ShapeDtypeStruct(shape, BF16),
+        in_specs=[pl.BlockSpec(memory_space=pltpu.SMEM)] + [vmem] * (3 + len(received) + len(others)),
+        out_specs=vmem,
+        scratch_shapes=[
+            pltpu.VMEM((rows, features + 128), BF16),
+            pltpu.VMEM((rows, features), BF16),
+            pltpu.VMEM((rows, 128), F32),
+        ],
+        compiler_params=pltpu.CompilerParams(vmem_limit_bytes=24 * MIB),
+        cost_estimate=pl.CostEstimate(flops=10**6, bytes_accessed=10**4, transcendentals=0),
+        name="merge",
+    )(tile_counts, out, logs, w_out, *received, *others)
 
 
 def exchange(value, axis, other):
@@ -322,29 +394,34 @@
         slide_of = [lax.axis_index("dp") ^ other for other in range(dp)]
         stacked = jnp.stack(made)[jnp.stack(slide_of)]
         by_residue = stacked.reshape(slides, ctx, each, features).swapaxes(0, 1)
+    pieces = [exchange(piece, "dp", other).reshape(sub, features) for other, piece in enumerate(made)]
     regrouped = lax.all_to_all(
         by_residue.reshape(ctx * dp, each, features), ("ctx", "dp"), split_axis=0, concat_axis=0, tiled=True
     ).reshape(count, features)
-    pieces = [exchange(piece, "dp", other).reshape(sub, features) for other, piece in enumerate(made)]
-    out, logs = local_attention(tile_counts, pieces, w_qkv, ctx)
+    w_near = fetch(w_qkv, made[0])
+    out, logs = local_attention(tile_counts, pieces, w_near, ctx)
     regrouped, out, logs = lax.optimization_barrier((regrouped, out, logs))
     portion = count // ctx
     if aligned:
-        sends, received = [], []
-        for some in ([4, 5, 6, 7], [2, 3, 1, 0]) if ctx == 8 else (list(range(ctx)),):
-            made = dilated_attention(tile_counts, regrouped, w_qkv, dp, ctx, some)
-            received += [exchange(piece, "ctx", other) for other, piece in zip(some, made)]
-            sends += some
+        found, kept, mixed = {}, (), ()
+        halves = ((4, 5, 6, 7), (2, 3, 1, 0)) if ctx == 8 else (tuple(range(ctx)),)
+        for some in halves:
+            made = dilated_attention(tile_counts, regrouped, w_near, dp, ctx, some, kept)
+            made, kept = made[: len(some)], kept or made[len(some) :]
+            found.update((other, exchange(piece, "ctx", other)) for other, piece in zip(some, made))
+        for some in halves:
+            received = [found[other] for other in some]
+            mixed = (merge_part(tile_counts, out, logs, w_out, received, dp, ctx, some, mixed),)
+        return mixed[0].reshape(1, count, features)
     else:
-        made = dilated_attention(tile_counts, regrouped, w_qkv, dp, ctx, list(range(ctx)))
+        made = dilated_attention(tile_counts, regrouped, w_near, dp, ctx, list(range(ctx)))[:ctx]
         order = jnp.stack([lax.axis_index("ctx") ^ other for other in range(ctx)])
         packed = lax.all_to_all(jnp.stack(made)[order], "ctx", split_axis=0, concat_axis=0, tiled=True)
         wide = packed[:, :-16].reshape(ctx, features // 128, portion, 128).swapaxes(1, 2).reshape(ctx, portion, features)
         lanes = packed[:, -16:].reshape(ctx, 16, 4, 32).swapaxes(1, 2)[:, : portion // 16].reshape(ctx, portion, 32)
         whole = jnp.concatenate([wide, jnp.pad(lanes, ((0, 0), (0, 0), (0, 96)))], axis=-1)
-        received = [whole.reshape(ctx, dp, each, -1).swapaxes(0, 1).reshape(count, -1)]
-        sends = None
-    return merge(tile_counts, out, logs, w_out, received, dp, ctx, sends)
+        received = whole.reshape(ctx, dp, each, -1).swapaxes(0, 1).reshape(count, -1)
+        return merge(tile_counts, out, logs, w_out, received, dp, ctx)
 
 
 def solution(mesh):

time: 78 us -> 66.3 us (0.85)
  waiting for transfers between devices: 23.3 us -> 16.8 us
  local copies, waits for them, and re-layouts: 7.08 us -> 2.54 us
  starting transfers between devices: 21.4 us -> 18.9 us
  Pallas kernels: 25.8 us -> 27.7 us
    ppermute x10, waiting for transfers between devices: 23.3 us -> 8.89 us  [exchange(): lax.ppermute(value, axis, [(i, i ^ other) for i in range(lax.axis_size(ax...]
    all_to_all x1, waiting for transfers between devices: 0.01 us -> 7.87 us  [body(): lax.all_to_all(by_residue.reshape(ctx * dp, each, features), ('ctx', 'dp'...]
    unnamed x12 -> x14, local copies, waits for them, and re-layouts: 7.08 us -> 2.54 us
    pallas_call x1 -> x3, Pallas kernels: 3.98 us -> 6.45 us  [the longest x2 4.43 us: merge_part(): pl.pallas_call(functools.partial(merge_part_kernel, dp, ctx, sends, len(o...]
    pallas_call x2, Pallas kernels: 11.4 us -> 9.1 us  [dilated_attention(): pl.pallas_call(functools.partial(dilated_kernel, dp, ctx, min(256, count)...]
    ppermute x10, starting transfers between devices: 14 us -> 12.5 us  [exchange(): lax.ppermute(value, axis, [(i, i ^ other) for i in range(lax.axis_size(ax...]
    all_to_all x1, starting transfers between devices: 7.48 us -> 6.37 us  [body(): lax.all_to_all(by_residue.reshape(ctx * dp, each, features), ('ctx', 'dp'...]
    pallas_call x1, Pallas kernels: 3.88 us -> 4.98 us  [embed(): pl.pallas_call(functools.partial(embed_kernel, ctx, steps, int(split)), o...]
  transfers between devices with their start and end apart: 11 -> 11, of which waited for: 5 -> 6; matrix products, arithmetic and copies ran while one was open for 0% -> 0% of each run, Pallas kernels for 16% -> 23%
where the time goes in v3:
time: 66.3 us; the launch traced here: 65.9 us
  Pallas kernels  27.7 us (42%)
  starting transfers between devices  18.9 us (29%)
  waiting for transfers between devices  16.8 us (25%)
  local copies, waits for them, and re-layouts  2.54 us (4%)
    ppermute x10, starting transfers between devices, exchange(): lax.ppermute(value, axis, [(i, i ^ other) for i in range(lax.axis_size(ax...  12.5 us
    pallas_call x2, Pallas kernels, dilated_attention(): pl.pallas_call(functools.partial(dilated_kernel, dp, ctx, min(256, count)...  9.1 us
    ppermute x10, waiting for transfers between devices, exchange(): lax.ppermute(value, axis, [(i, i ^ other) for i in range(lax.axis_size(ax...  8.89 us
    all_to_all x1, waiting for transfers between devices, body(): lax.all_to_all(by_residue.reshape(ctx * dp, each, features), ('ctx', 'dp'...  7.87 us
    pallas_call x1, Pallas kernels, local_attention(): pl.pallas_call(functools.partial(local_kernel, dp, ctx, min(256, count)),...  7.11 us
    all_to_all x1, starting transfers between devices, body(): lax.all_to_all(by_residue.reshape(ctx * dp, each, features), ('ctx', 'dp'...  6.37 us
    pallas_call x1, Pallas kernels, embed(): pl.pallas_call(functools.partial(embed_kernel, ctx, steps, int(split)), o...  4.98 us
    pallas_call x2, Pallas kernels, merge_part(): pl.pallas_call(functools.partial(merge_part_kernel, dp, ctx, sends, len(o...  4.43 us
  transfers between devices with their start and end apart: 11, of which 6 were waited for; matrix products, arithmetic and copies ran while one was open for 0% of the time, Pallas kernels for 23%

profile of v3, /device:TPU:0, one launch (start us, length us, event | category | flops | bytes accessed | tf_op | source)
XLA Modules:
  0.0 65.9 jit_solution(5285042834452750223)
XLA Ops:
  0.0 5.0 %embed.1 = (bf16[8,4,16,768]{3,2,1,0:T(8,128)(2,1)}, bf16[8,16,768]{2,1,0:T(8,128)(2,1)}, bf16[8,16,768]{2,1,0:T(8,128)(2,1)}, bf16[8,16,768]{2,1,0:T(8,128)(2,1)}, bf16[8,16,768]{2,1,0:T(8,128)(2,1)}) custom-call(bf16[4,1,128,1536]{3,2,1,0:T(8,128)(2,1)} %x_hbm.1, bf16[1536,768]{1,0:T(8,128)(2,1)} %w_hbm.1), custom_call_target="tpu_custom_call" | custom-call | tf_op jit(solution)/shard_map/embed/pallas_call | solution.py:80
  5.0 0.5 collective-permute-start
  5.5 2.6 %collective-permute-start.1 = (bf16[8,16,768]{2,1,0:T(8,128)(2,1)}, bf16[8,16,768]{2,1,0:T(8,128)(2,1)}, u32[]{:S(2)}, u32[]{:S(2)}) collective-permute-start(bf16[8,16,768]{2,1,0:T(8,128)(2,1)} %get-tuple-element.28), channel_id=1, source_target_pairs={{0,16},{8,24},{16,0},{24,8},{1,17},{9,25},{17,1},{25,9},{2,18},{10... | collective-permute-start | bytes 589832 | tf_op jit(solution)/shard_map/ppermute | solution.py:380
  8.2 6.4 %all-to-all-start = ((bf16[32,16,768]{2,1,0:T(8,128)(2,1)}), bf16[32,16,768]{2,1,0:T(8,128)(2,1)}, u32[]{:S(2)}, u32[]{:S(2)}) async-start(bf16[32,16,768]{2,1,0:T(8,128)(2,1)} %bitcast.7), calls=%async_computation | async-start | bytes 1572864 | tf_op jit(solution)/shard_map/all_to_all | solution.py:398
  14.5 0.9 %copy-done.5 = bf16[8,16,768]{2,1,0:T(8,128)(2,1)S(1)} copy-done((bf16[8,16,768]{2,1,0:T(8,128)(2,1)S(1)}, bf16[8,16,768]{2,1,0:T(8,128)(2,1)}, u32[]{:S(2)}) %copy-start.5) | copy-done | bytes 196632
  15.5 2.0 %fetch.1.refs_4_.weight_ref = bf16[768,2304]{1,0:T(8,128)(2,1)S(1)} custom-call(bf16[768,2304]{1,0:T(8,128)(2,1)} %source.1, bf16[8,16,768]{2,1,0:T(8,128)(2,1)S(1)} %copy-done.5), custom_call_target="tpu_custom_call" | custom-call | bytes 8000000 | tf_op jit(solution)/shard_map/fetch/pallas_call | solution.py:105
  17.5 0.8 %collective-permute-done.2 = bf16[8,16,768]{2,1,0:T(8,128)(2,1)} collective-permute-done((bf16[8,16,768]{2,1,0:T(8,128)(2,1)}, bf16[8,16,768]{2,1,0:T(8,128)(2,1)}, u32[]{:S(2)}, u32[]{:S(2)}) %collective-permute-start.2) | collective-permute-done | bytes 196640 | tf_op jit(solution)/shard_map/ppermute | solution.py:380
  18.4 7.1 %local.1 = (bf16[512,768]{1,0:T(8,128)(2,1)S(1)}, f32[512,128]{1,0:T(8,128)S(1)}) custom-call(s32[4]{0:T(128)S(1)} %copy-done.6, bf16[128,768]{1,0:T(8,128)(2,1)S(1)} %bitcast.6, bf16[128,768]{1,0:T(8,128)(2,1)} %bitcast.3.refs_1_, bf16[128,768]{1,0:T(8,128)(2,1)} %bitcast.4.refs_2_, bf16[128,768]{1,0:T(8,128)(2,1)} %bitcast.5.refs_3_, ...), custom_call_target="tpu_custom_call" | custom-call | flops 999999995904 | bytes 10000000000 | tf_op jit(solution)/shard_map/local/pallas_call | solution.py:188
  25.5 0.9 %copy-done.1 = bf16[512,768]{1,0:T(8,128)(2,1)} copy-done((bf16[512,768]{1,0:T(8,128)(2,1)}, bf16[512,768]{1,0:T(8,128)(2,1)S(1)}, u32[]{:S(2)}) %copy-start.1) | copy-done | bytes 786456
  26.4 0.7 %copy-done.3 = f32[512,128]{1,0:T(8,128)} copy-done((f32[512,128]{1,0:T(8,128)}, f32[512,128]{1,0:T(8,128)S(1)}, u32[]{:S(2)}) %copy-start.3) | copy-done | bytes 262168
  27.1 7.9 %all-to-all-done = bf16[32,16,768]{2,1,0:T(8,128)(2,1)} async-done(((bf16[32,16,768]{2,1,0:T(8,128)(2,1)}), bf16[32,16,768]{2,1,0:T(8,128)(2,1)}, u32[]{:S(2)}, u32[]{:S(2)}) %all-to-all-start) | async-done | bytes 786464 | tf_op jit(solution)/shard_map/all_to_all | solution.py:398
  35.0 5.1 %dilated.2 = (bf16[400,128]{1,0:T(8,128)(2,1)S(1)}, bf16[400,128]{1,0:T(8,128)(2,1)S(1)}, bf16[400,128]{1,0:T(8,128)(2,1)S(1)}, bf16[400,128]{1,0:T(8,128)(2,1)S...) custom-call(s32[4]{0:T(128)S(1)} %copy-done.6, bf16[512,768]{1,0:T(8,128)(2,1)} %bitcast.1.rows, ...), custom_call_target="tpu_custom_call" | custom-call | flops 1000000 | bytes 10000 | tf_op jit(solution)/shard_map/dilated/pallas_call | solution.py:256
  40.1 1.0 %collective-permute-start.6 = (bf16[400,128]{1,0:T(8,128)(2,1)S(1)}, bf16[400,128]{1,0:T(8,128)(2,1)S(1)}, u32[]{:S(2)}, u32[]{:S(2)}) collective-permute-start(bf16[400,128]{1,0:T(8,128)(2,1)S(1)} %get-tuple-element.41), channel_id=1, source_target_pairs={{0,4},{1,5},{2,6},{3,7},{4,0},{5,1},{6,2},{7,3},{8,12},{9,13},{10,... | collective-permute-start | bytes 307208 | tf_op jit(solution)/shard_map/ppermute | solution.py:380
  41.1 3.0 %collective-permute-start.7 = (bf16[400,128]{1,0:T(8,128)(2,1)S(1)}, bf16[400,128]{1,0:T(8,128)(2,1)S(1)}, u32[]{:S(2)}, u32[]{:S(2)}) collective-permute-start(bf16[400,128]{1,0:T(8,128)(2,1)S(1)} %get-tuple-element.42), channel_id=1, source_target_pairs={{0,5},{1,4},{2,7},{3,6},{4,1},{5,0},{6,3},{7,2},{8,13},{9,12},{10,... | collective-permute-start | bytes 307208 | tf_op jit(solution)/shard_map/ppermute | solution.py:380
  44.0 1.4 %collective-permute-start.8 = (bf16[400,128]{1,0:T(8,128)(2,1)S(1)}, bf16[400,128]{1,0:T(8,128)(2,1)S(1)}, u32[]{:S(2)}, u32[]{:S(2)}) collective-permute-start(bf16[400,128]{1,0:T(8,128)(2,1)S(1)} %get-tuple-element.43), channel_id=1, source_target_pairs={{0,6},{1,7},{2,4},{3,5},{4,2},{5,3},{6,0},{7,1},{8,14},{9,15},{10,... | collective-permute-start | bytes 307208 | tf_op jit(solution)/shard_map/ppermute | solution.py:380
  45.5 2.3 %collective-permute-start.9 = (bf16[400,128]{1,0:T(8,128)(2,1)S(1)}, bf16[400,128]{1,0:T(8,128)(2,1)S(1)}, u32[]{:S(2)}, u32[]{:S(2)}) collective-permute-start(bf16[400,128]{1,0:T(8,128)(2,1)S(1)} %get-tuple-element.44), channel_id=1, source_target_pairs={{0,7},{1,6},{2,5},{3,4},{4,3},{5,2},{6,1},{7,0},{8,15},{9,14},{10,... | collective-permute-start | bytes 307208 | tf_op jit(solution)/shard_map/ppermute | solution.py:380
  47.8 4.0 %dilated.3 = (bf16[400,128]{1,0:T(8,128)(2,1)S(1)}, bf16[400,128]{1,0:T(8,128)(2,1)S(1)}, bf16[400,128]{1,0:T(8,128)(2,1)S(1)}, bf16[400,128]{1,0:T(8,128)(2,1)S(1)}) custom-call(s32[4]{0:T(128)S(1)} %copy-done.6, bf16[512,768]{1,0:T(8,128)(2,1)} %bitcast.1.rows, bf16[768,2304]{1,0:T(8,128)(2,1)S(1)} %fetch.1.refs_4_.weight_ref, ...), custom_call_target="tpu_custom_call" | custom-call | flops 1000000 | bytes 10000 | tf_op jit(solution)/shard_map/dilated/pallas_call | solution.py:256
  51.9 3.7 %collective-permute-done.6.refs_0_ = bf16[400,128]{1,0:T(8,128)(2,1)S(1)} collective-permute-done((bf16[400,128]{1,0:T(8,128)(2,1)S(1)}, bf16[400,128]{1,0:T(8,128)(2,1)S(1)}, u32[]{:S(2)}, u32[]{:S(2)}) %collective-permute-start.6) | collective-permute-done | bytes 102432 | tf_op jit(solution)/shard_map/ppermute | solution.py:380
  55.6 2.1 %collective-permute-done.7.refs_1_ = bf16[400,128]{1,0:T(8,128)(2,1)S(1)} collective-permute-done((bf16[400,128]{1,0:T(8,128)(2,1)S(1)}, bf16[400,128]{1,0:T(8,128)(2,1)S(1)}, u32[]{:S(2)}, u32[]{:S(2)}) %collective-permute-start.7) | collective-permute-done | bytes 102432 | tf_op jit(solution)/shard_map/ppermute | solution.py:380
  57.7 1.6 %collective-permute-start.5 = (bf16[400,128]{1,0:T(8,128)(2,1)S(1)}, bf16[400,128]{1,0:T(8,128)(2,1)S(1)}, u32[]{:S(2)}, u32[]{:S(2)}) collective-permute-start(bf16[400,128]{1,0:T(8,128)(2,1)S(1)} %get-tuple-element.39), channel_id=1, source_target_pairs={{0,1},{1,0},{2,3},{3,2},{4,5},{5,4},{6,7},{7,6},{8,9},{9,8},{10,11... | collective-permute-start | bytes 307208 | tf_op jit(solution)/shard_map/ppermute | solution.py:380
  59.3 1.8 %merge.2.refs_4_ = bf16[512,768]{1,0:T(8,128)(2,1)S(1)} custom-call(s32[4]{0:T(128)S(1)} %copy-done.6, bf16[512,768]{1,0:T(8,128)(2,1)S(1)} %copy-done.2, f32[512,128]{1,0:T(8,128)S(1)} %copy-done.4, bf16[768,768]{1,0:T(8,128)(2,1)S(1)} %copy-done, bf16[400,128]{1,0:T(8,128)(2,1)S(1)} %collective-permute-done.6.refs_0_, ...), custom_call_target="tpu_custom_call" | custom-call | flops 1000000 | bytes 10000 | tf_op jit(solution)/shard_map/merge/pallas_call | solution.py:361
  61.1 0.3 collective-permute-done.4.refs_1_
  61.4 1.9 %collective-permute-done.5.refs_2_ = bf16[400,128]{1,0:T(8,128)(2,1)S(1)} collective-permute-done((bf16[400,128]{1,0:T(8,128)(2,1)S(1)}, bf16[400,128]{1,0:T(8,128)(2,1)S(1)}, u32[]{:S(2)}, u32[]{:S(2)}) %collective-permute-start.5) | collective-permute-done | bytes 102432 | tf_op jit(solution)/shard_map/ppermute | solution.py:380
  63.3 2.7 %merge.3 = bf16[1,512,768]{2,1,0:T(8,128)(2,1)} custom-call(s32[4]{0:T(128)S(1)} %copy-done.6, bf16[512,768]{1,0:T(8,128)(2,1)S(1)} %copy-done.2, f32[512,128]{1,0:T(8,128)S(1)} %copy-done.4, bf16[768,768]{1,0:T(8,128)(2,1)S(1)} %copy-done, bf16[400,128]{1,0:T(8,128)(2,1)S(1)} %collective-permute-done.3.refs_0_, ...), custom_call_target="tpu_custom_call" | custom-call | flops 1000000 | bytes 10000 | tf_op jit(solution)/shard_map/merge/pallas_call | solution.py:361
  (19 shorter events, 0.2 us)
Async XLA Ops:
  5.0 12.5 %collective-permute-start = (bf16[8,16,768]{2,1,0:T(8,128)(2,1)}, bf16[8,16,768]{2,1,0:T(8,128)(2,1)}, u32[]{:S(2)}, u32[]{:S(2)}) collective-permute-start(bf16[8,16,768]{2,1,0:T(8,128)(2,1)} %get-tuple-element.27), channel_id=1, source_target_pairs={{0,8},{8,0},{16,24},{24,16},{1,9},{9,1},{17,25},{25,17},{2,10},{10... | collective-permute-start | bytes 589832 | tf_op jit(solution)/shard_map/ppermute | solution.py:380
  5.5 12.0 %collective-permute-start.1 = (bf16[8,16,768]{2,1,0:T(8,128)(2,1)}, bf16[8,16,768]{2,1,0:T(8,128)(2,1)}, u32[]{:S(2)}, u32[]{:S(2)}) collective-permute-start(bf16[8,16,768]{2,1,0:T(8,128)(2,1)} %get-tuple-element.28), channel_id=1, source_target_pairs={{0,16},{8,24},{16,0},{24,8},{1,17},{9,25},{17,1},{25,9},{2,18},{10... | collective-permute-start | bytes 589832 | tf_op jit(solution)/shard_map/ppermute | solution.py:380
  8.1 10.3 %collective-permute-start.2 = (bf16[8,16,768]{2,1,0:T(8,128)(2,1)}, bf16[8,16,768]{2,1,0:T(8,128)(2,1)}, u32[]{:S(2)}, u32[]{:S(2)}) collective-permute-start(bf16[8,16,768]{2,1,0:T(8,128)(2,1)} %get-tuple-element.29), channel_id=1, source_target_pairs={{0,24},{8,16},{16,8},{24,0},{1,25},{9,17},{17,9},{25,1},{2,26},{10... | collective-permute-start | bytes 589832 | tf_op jit(solution)/shard_map/ppermute | solution.py:380
  8.2 26.8 %all-to-all-start = ((bf16[32,16,768]{2,1,0:T(8,128)(2,1)}), bf16[32,16,768]{2,1,0:T(8,128)(2,1)}, u32[]{:S(2)}, u32[]{:S(2)}) async-start(bf16[32,16,768]{2,1,0:T(8,128)(2,1)} %bitcast.7), calls=%async_computation | async-start | bytes 1572864 | tf_op jit(solution)/shard_map/all_to_all | solution.py:398
  14.5 0.9 %copy-start.5 = (bf16[8,16,768]{2,1,0:T(8,128)(2,1)S(1)}, bf16[8,16,768]{2,1,0:T(8,128)(2,1)}, u32[]{:S(2)}) copy-start(bf16[8,16,768]{2,1,0:T(8,128)(2,1)} %get-tuple-element.26.after) | copy-start | bytes 589828
  15.5 2.9 %copy-start.6 = (s32[4]{0:T(128)S(1)}, s32[4]{0:T(128)}, u32[]{:S(2)}) copy-start(s32[4]{0:T(128)} %counts_ref.9) | copy-start | bytes 52
  25.5 0.9 %copy-start.1 = (bf16[512,768]{1,0:T(8,128)(2,1)}, bf16[512,768]{1,0:T(8,128)(2,1)S(1)}, u32[]{:S(2)}) copy-start(bf16[512,768]{1,0:T(8,128)(2,1)S(1)} %get-tuple-element.32.out_ref) | copy-start | bytes 2359300
  26.4 0.7 %copy-start.3 = (f32[512,128]{1,0:T(8,128)}, f32[512,128]{1,0:T(8,128)S(1)}, u32[]{:S(2)}) copy-start(f32[512,128]{1,0:T(8,128)S(1)} %get-tuple-element.33.log_ref) | copy-start | bytes 786436
  40.1 15.5 %collective-permute-start.6 = (bf16[400,128]{1,0:T(8,128)(2,1)S(1)}, bf16[400,128]{1,0:T(8,128)(2,1)S(1)}, u32[]{:S(2)}, u32[]{:S(2)}) collective-permute-start(bf16[400,128]{1,0:T(8,128)(2,1)S(1)} %get-tuple-element.41), channel_id=1, source_target_pairs={{0,4},{1,5},{2,6},{3,7},{4,0},{5,1},{6,2},{7,3},{8,12},{9,13},{10,... | collective-permute-start | bytes 307208 | tf_op jit(solution)/shard_map/ppermute | solution.py:380
  41.1 16.6 %collective-permute-start.7 = (bf16[400,128]{1,0:T(8,128)(2,1)S(1)}, bf16[400,128]{1,0:T(8,128)(2,1)S(1)}, u32[]{:S(2)}, u32[]{:S(2)}) collective-permute-start(bf16[400,128]{1,0:T(8,128)(2,1)S(1)} %get-tuple-element.42), channel_id=1, source_target_pairs={{0,5},{1,4},{2,7},{3,6},{4,1},{5,0},{6,3},{7,2},{8,13},{9,12},{10,... | collective-permute-start | bytes 307208 | tf_op jit(solution)/shard_map/ppermute | solution.py:380
  44.0 15.2 %collective-permute-start.8 = (bf16[400,128]{1,0:T(8,128)(2,1)S(1)}, bf16[400,128]{1,0:T(8,128)(2,1)S(1)}, u32[]{:S(2)}, u32[]{:S(2)}) collective-permute-start(bf16[400,128]{1,0:T(8,128)(2,1)S(1)} %get-tuple-element.43), channel_id=1, source_target_pairs={{0,6},{1,7},{2,4},{3,5},{4,2},{5,3},{6,0},{7,1},{8,14},{9,15},{10,... | collective-permute-start | bytes 307208 | tf_op jit(solution)/shard_map/ppermute | solution.py:380
  45.5 13.8 %collective-permute-start.9 = (bf16[400,128]{1,0:T(8,128)(2,1)S(1)}, bf16[400,128]{1,0:T(8,128)(2,1)S(1)}, u32[]{:S(2)}, u32[]{:S(2)}) collective-permute-start(bf16[400,128]{1,0:T(8,128)(2,1)S(1)} %get-tuple-element.44), channel_id=1, source_target_pairs={{0,7},{1,6},{2,5},{3,4},{4,3},{5,2},{6,1},{7,0},{8,15},{9,14},{10,... | collective-permute-start | bytes 307208 | tf_op jit(solution)/shard_map/ppermute | solution.py:380
  47.8 11.5 %copy-start = (bf16[768,768]{1,0:T(8,128)(2,1)S(1)}, bf16[768,768]{1,0:T(8,128)(2,1)}, u32[]{:S(2)}) copy-start(bf16[768,768]{1,0:T(8,128)(2,1)} %weight_ref.3) | copy-start | bytes 3538948
  47.8 11.5 %copy-start.2 = (bf16[512,768]{1,0:T(8,128)(2,1)S(1)}, bf16[512,768]{1,0:T(8,128)(2,1)}, u32[]{:S(2)}) copy-start(bf16[512,768]{1,0:T(8,128)(2,1)} %copy-done.1) | copy-start | bytes 2359300
  47.8 11.5 %copy-start.4 = (f32[512,128]{1,0:T(8,128)S(1)}, f32[512,128]{1,0:T(8,128)}, u32[]{:S(2)}) copy-start(f32[512,128]{1,0:T(8,128)} %copy-done.3) | copy-start | bytes 786436
  51.8 9.3 %collective-permute-start.3 = (bf16[400,128]{1,0:T(8,128)(2,1)S(1)}, bf16[400,128]{1,0:T(8,128)(2,1)S(1)}, u32[]{:S(2)}, u32[]{:S(2)}) collective-permute-start(bf16[400,128]{1,0:T(8,128)(2,1)S(1)} %get-tuple-element.37), channel_id=1, source_target_pairs={{0,2},{1,3},{2,0},{3,1},{4,6},{5,7},{6,4},{7,5},{8,10},{9,11},{10,... | collective-permute-start | bytes 307208 | tf_op jit(solution)/shard_map/ppermute | solution.py:380
  55.6 5.8 %collective-permute-start.4 = (bf16[400,128]{1,0:T(8,128)(2,1)S(1)}, bf16[400,128]{1,0:T(8,128)(2,1)S(1)}, u32[]{:S(2)}, u32[]{:S(2)}) collective-permute-start(bf16[400,128]{1,0:T(8,128)(2,1)S(1)} %get-tuple-element.38), channel_id=1, source_target_pairs={{0,3},{1,2},{2,1},{3,0},{4,7},{5,6},{6,5},{7,4},{8,11},{9,10},{10,... | collective-permute-start | bytes 307208 | tf_op jit(solution)/shard_map/ppermute | solution.py:380
  57.7 5.6 %collective-permute-start.5 = (bf16[400,128]{1,0:T(8,128)(2,1)S(1)}, bf16[400,128]{1,0:T(8,128)(2,1)S(1)}, u32[]{:S(2)}, u32[]{:S(2)}) collective-permute-start(bf16[400,128]{1,0:T(8,128)(2,1)S(1)} %get-tuple-element.39), channel_id=1, source_target_pairs={{0,1},{1,0},{2,3},{3,2},{4,5},{5,4},{6,7},{7,6},{8,9},{9,8},{10,11... | collective-permute-start | bytes 307208 | tf_op jit(solution)/shard_map/ppermute | solution.py:380

commit v4 on v3

--- a/solution.py
+++ b/solution.py
@@ -192,7 +192,7 @@
         out_specs=[vmem] * 2,
         scratch_shapes=[pltpu.VMEM((count, features), BF16)] * 3,
         compiler_params=pltpu.CompilerParams(vmem_limit_bytes=24 * MIB),
-        cost_estimate=pl.CostEstimate(flops=10**12, bytes_accessed=10**10, transcendentals=0),
+        cost_estimate=pl.CostEstimate(flops=8 * 10**9, bytes_accessed=10**7, transcendentals=0),
         name="local",
     )(tile_counts, *pieces, w_qkv)
 
@@ -201,11 +201,8 @@
     return portion * (features // 128) + 16
 
 
-def dilated_kernel(dp, ctx, block, sends, first_call, counts_ref, rows, weight_ref, *refs):
-    if first_call:
-        out_refs, (keys, values) = refs[:-2], refs[-2:]
-    else:
-        (keys, values), out_refs = refs[:2], refs[2:]
+def dilated_kernel(dp, ctx, block, sends, counts_ref, rows, weight_ref, *refs):
+    out_refs, (keys, values) = refs[:-2], refs[-2:]
     me, mine = lax.axis_index("dp"), lax.axis_index("ctx")
     count, features = rows.shape
     portion = count // ctx
@@ -215,8 +212,7 @@
     position = spot // portion * count + inner // each * (count // dp) + inner % each * ctx + mine
     is_valid = position < counts_ref[me]
     counted = jnp.broadcast_to(is_valid.astype(F32), (count, 128)).astype(BF16)
-    if first_call:
-        project(rows[...], weight_ref, is_valid, keys, values)
+    project(rows[...], weight_ref, is_valid, keys, values)
     portions = block // portion
     for start in range(0, len(sends), portions):
         some = sends[start : start + portions]
@@ -246,22 +242,20 @@
         attend(queries_of(jnp.concatenate(wanted, axis=0), weight_ref), keys, values, counted, spread, put_total)
 
 
-def dilated_attention(tile_counts, rows, w_qkv, dp, ctx, sends, kept=()):
+def dilated_attention(tile_counts, rows, w_qkv, dp, ctx, sends):
     count, features = rows.shape
     portion = count // ctx
     vmem = pl.BlockSpec(memory_space=pltpu.VMEM)
-    outs = [jax.ShapeDtypeStruct((packed_rows(portion, features), 128), BF16)] * len(sends)
-    if not kept:
-        outs += [jax.ShapeDtypeStruct((count, features), BF16)] * 2
-    return pl.pallas_call(
-        functools.partial(dilated_kernel, dp, ctx, min(256, count), sends, not kept),
-        out_shape=outs,
-        in_specs=[pl.BlockSpec(memory_space=pltpu.SMEM)] + [vmem] * (2 + len(kept)),
-        out_specs=[vmem] * len(outs),
+    return pl.pallas_call(
+        functools.partial(dilated_kernel, dp, ctx, min(256, count), sends),
+        out_shape=[jax.ShapeDtypeStruct((packed_rows(portion, features), 128), BF16)] * len(sends),
+        in_specs=[pl.BlockSpec(memory_space=pltpu.SMEM)] + [vmem] * 2,
+        out_specs=[vmem] * len(sends),
+        scratch_shapes=[pltpu.VMEM((count, features), BF16)] * 2,
         compiler_params=pltpu.CompilerParams(vmem_limit_bytes=24 * MIB),
         cost_estimate=pl.CostEstimate(flops=10**6, bytes_accessed=10**4, transcendentals=0),
         name="dilated",
-    )(tile_counts, rows, w_qkv, *kept)
+    )(tile_counts, rows, w_qkv)
 
 
 def merge_rows(own, own_logs, features_of, logs, heads, weight):
@@ -399,22 +393,22 @@
         by_residue.reshape(ctx * dp, each, features), ("ctx", "dp"), split_axis=0, concat_axis=0, tiled=True
     ).reshape(count, features)
     w_near = fetch(w_qkv, made[0])
-    out, logs = local_attention(tile_counts, pieces, w_near, ctx)
-    regrouped, out, logs = lax.optimization_barrier((regrouped, out, logs))
     portion = count // ctx
     if aligned:
-        found, kept, mixed = {}, (), ()
-        halves = ((4, 5, 6, 7), (2, 3, 1, 0)) if ctx == 8 else (tuple(range(ctx)),)
-        for some in halves:
-            made = dilated_attention(tile_counts, regrouped, w_near, dp, ctx, some, kept)
-            made, kept = made[: len(some)], kept or made[len(some) :]
-            found.update((other, exchange(piece, "ctx", other)) for other, piece in zip(some, made))
-        for some in halves:
+        sends = (4, 5, 6, 7, 2, 3, 1, 0) if ctx == 8 else tuple(range(ctx))
+        made = dilated_attention(tile_counts, regrouped, w_near, dp, ctx, sends)
+        found = {other: exchange(piece, "ctx", other) for other, piece in zip(sends, made)}
+        tied = lax.optimization_barrier((found[0], *pieces))
+        found[0], pieces = tied[0], tied[1:]
+        out, logs = local_attention(tile_counts, pieces, w_near, ctx)
+        mixed = ()
+        for some in ((2, 3, 1, 0), (4, 5, 6, 7)) if ctx == 8 else (sends,):
             received = [found[other] for other in some]
             mixed = (merge_part(tile_counts, out, logs, w_out, received, dp, ctx, some, mixed),)
         return mixed[0].reshape(1, count, features)
     else:
-        made = dilated_attention(tile_counts, regrouped, w_near, dp, ctx, list(range(ctx)))[:ctx]
+        out, logs = local_attention(tile_counts, pieces, w_near, ctx)
+        made = dilated_attention(tile_counts, regrouped, w_near, dp, ctx, list(range(ctx)))
         order = jnp.stack([lax.axis_index("ctx") ^ other for other in range(ctx)])
         packed = lax.all_to_all(jnp.stack(made)[order], "ctx", split_axis=0, concat_axis=0, tiled=True)
         wide = packed[:, :-16].reshape(ctx, features // 128, portion, 128).swapaxes(1, 2).reshape(ctx, portion, features)

time: 66.3 us -> 64.5 us (0.973); the launches traced: 65.9 us -> 63.4 us
  Pallas kernels: 27.7 us -> 25.7 us
  starting transfers between devices: 18.9 us -> 20.6 us
  local copies, waits for them, and re-layouts: 2.54 us -> 0.94 us
  waiting for transfers between devices: 16.8 us -> 16 us
    ppermute x10, waiting for transfers between devices: 8.89 us -> 0.35 us  [exchange(): lax.ppermute(value, axis, [(i, i ^ other) for i in range(lax.axis_size(ax...]
    all_to_all x1, waiting for transfers between devices: 7.87 us -> 15.7 us  [body(): lax.all_to_all(by_residue.reshape(ctx * dp, each, features), ('ctx', 'dp'...]
    pallas_call x2 -> x1, Pallas kernels: 9.1 us -> 7.2 us  [dilated_attention(): pl.pallas_call(functools.partial(dilated_kernel, dp, ctx, min(256, count)...]
    unnamed x14 -> x8, local copies, waits for them, and re-layouts: 2.54 us -> 0.94 us
    all_to_all x1, starting transfers between devices: 6.37 us -> 7.42 us  [body(): lax.all_to_all(by_residue.reshape(ctx * dp, each, features), ('ctx', 'dp'...]
    ppermute x10, starting transfers between devices: 12.5 us -> 13.2 us  [exchange(): lax.ppermute(value, axis, [(i, i ^ other) for i in range(lax.axis_size(ax...]
  transfers between devices with their start and end apart: 11 -> 11, of which waited for: 6 -> 2; matrix products, arithmetic and copies ran while one was open for 0% -> 0% of each run, Pallas kernels for 23% -> 28%
where the time goes in v4:
time: 64.5 us; the launch traced here: 63.4 us
  Pallas kernels  25.7 us (40%)
  starting transfers between devices  20.6 us (32%)
  waiting for transfers between devices  16 us (25%)
  local copies, waits for them, and re-layouts  0.94 us (1%)
    all_to_all x1, waiting for transfers between devices, body(): lax.all_to_all(by_residue.reshape(ctx * dp, each, features), ('ctx', 'dp'...  15.7 us
    ppermute x10, starting transfers between devices, exchange(): lax.ppermute(value, axis, [(i, i ^ other) for i in range(lax.axis_size(ax...  13.2 us
    all_to_all x1, starting transfers between devices, body(): lax.all_to_all(by_residue.reshape(ctx * dp, each, features), ('ctx', 'dp'...  7.42 us
    pallas_call x1, Pallas kernels, dilated_attention(): pl.pallas_call(functools.partial(dilated_kernel, dp, ctx, min(256, count)...  7.2 us
    pallas_call x1, Pallas kernels, local_attention(): pl.pallas_call(functools.partial(local_kernel, dp, ctx, min(256, count)),...  7.06 us
    pallas_call x1, Pallas kernels, embed(): pl.pallas_call(functools.partial(embed_kernel, ctx, steps, int(split)), o...  5 us
    pallas_call x2, Pallas kernels, merge_part(): pl.pallas_call(functools.partial(merge_part_kernel, dp, ctx, sends, len(o...  4.42 us
    pallas_call x1, Pallas kernels, fetch(): pl.pallas_call(fetch_kernel, out_shape=jax.ShapeDtypeStruct(value.shape,...  2.02 us
  transfers between devices with their start and end apart: 11, of which 2 were waited for; matrix products, arithmetic and copies ran while one was open for 0% of the time, Pallas kernels for 28%

profile of v4, /device:TPU:0, one launch (start us, length us, event | category | flops | bytes accessed | tf_op | source)
XLA Modules:
  0.0 63.4 jit_solution(17950837396224750976)
XLA Ops:
  0.0 5.0 %embed.1 = (bf16[8,4,16,768]{3,2,1,0:T(8,128)(2,1)}, bf16[8,16,768]{2,1,0:T(8,128)(2,1)}, bf16[8,16,768]{2,1,0:T(8,128)(2,1)}, bf16[8,16,768]{2,1,0:T(8,128)(2,1)}, bf16[8,16,768]{2,1,0:T(8,128)(2,1)}) custom-call(bf16[4,1,128,1536]{3,2,1,0:T(8,128)(2,1)} %x_hbm.1, bf16[1536,768]{1,0:T(8,128)(2,1)} %w_hbm.1), custom_call_target="tpu_custom_call" | custom-call | tf_op jit(solution)/shard_map/embed/pallas_call | solution.py:80
  5.0 7.4 %all-to-all-start = ((bf16[32,16,768]{2,1,0:T(8,128)(2,1)}), bf16[32,16,768]{2,1,0:T(8,128)(2,1)}, u32[]{:S(2)}, u32[]{:S(2)}) async-start(bf16[32,16,768]{2,1,0:T(8,128)(2,1)} %bitcast.7), calls=%async_computation | async-start | bytes 1572864 | tf_op jit(solution)/shard_map/all_to_all | solution.py:392
  12.4 0.3 collective-permute-start
  12.7 1.7 %collective-permute-start.1 = (bf16[8,16,768]{2,1,0:T(8,128)(2,1)}, bf16[8,16,768]{2,1,0:T(8,128)(2,1)}, u32[]{:S(2)}, u32[]{:S(2)}) collective-permute-start(bf16[8,16,768]{2,1,0:T(8,128)(2,1)} %get-tuple-element.29), channel_id=1, source_target_pairs={{0,16},{8,24},{16,0},{24,8},{1,17},{9,25},{17,1},{25,9},{2,18},{10... | collective-permute-start | bytes 589832 | tf_op jit(solution)/shard_map/ppermute | solution.py:374
  14.4 0.0 collective-permute-start.2
  14.4 0.9 %copy-done.1 = bf16[8,16,768]{2,1,0:T(8,128)(2,1)S(1)} copy-done((bf16[8,16,768]{2,1,0:T(8,128)(2,1)S(1)}, bf16[8,16,768]{2,1,0:T(8,128)(2,1)}, u32[]{:S(2)}) %copy-start.1) | copy-done | bytes 196632
  15.3 2.0 %fetch.1.weight_ref.refs_4_ = bf16[768,2304]{1,0:T(8,128)(2,1)S(1)} custom-call(bf16[768,2304]{1,0:T(8,128)(2,1)} %source.1, bf16[8,16,768]{2,1,0:T(8,128)(2,1)S(1)} %copy-done.1), custom_call_target="tpu_custom_call" | custom-call | bytes 8000000 | tf_op jit(solution)/shard_map/fetch/pallas_call | solution.py:105
  17.3 15.7 %all-to-all-done = bf16[32,16,768]{2,1,0:T(8,128)(2,1)} async-done(((bf16[32,16,768]{2,1,0:T(8,128)(2,1)}), bf16[32,16,768]{2,1,0:T(8,128)(2,1)}, u32[]{:S(2)}, u32[]{:S(2)}) %all-to-all-start) | async-done | bytes 786464 | tf_op jit(solution)/shard_map/all_to_all | solution.py:392
  33.1 7.2 %dilated.1 = (bf16[400,128]{1,0:T(8,128)(2,1)S(1)}, bf16[400,128]{1,0:T(8,128)(2,1)S(1)}, bf16[400,128]{1,0:T(8,128)(2,1)S(1)}, bf16[400,128]{1,0:T(8,128)(2,1)S...) custom-call(s32[4]{0:T(128)S(1)} %copy-done.3, ...), custom_call_target="tpu_custom_call" | custom-call | flops 1000000 | bytes 10000 | tf_op jit(solution)/shard_map/dilated/pallas_call | solution.py:249
  40.3 1.5 %collective-permute-start.7 = (bf16[400,128]{1,0:T(8,128)(2,1)S(1)}, bf16[400,128]{1,0:T(8,128)(2,1)S(1)}, u32[]{:S(2)}, u32[]{:S(2)}) collective-permute-start(bf16[400,128]{1,0:T(8,128)(2,1)S(1)} %get-tuple-element.41), channel_id=1, source_target_pairs={{0,2},{1,3},{2,0},{3,1},{4,6},{5,7},{6,4},{7,5},{8,10},{9,11},{10,... | collective-permute-start | bytes 307208 | tf_op jit(solution)/shard_map/ppermute | solution.py:374
  41.7 1.6 %collective-permute-start.8 = (bf16[400,128]{1,0:T(8,128)(2,1)S(1)}, bf16[400,128]{1,0:T(8,128)(2,1)S(1)}, u32[]{:S(2)}, u32[]{:S(2)}) collective-permute-start(bf16[400,128]{1,0:T(8,128)(2,1)S(1)} %get-tuple-element.42), channel_id=1, source_target_pairs={{0,3},{1,2},{2,1},{3,0},{4,7},{5,6},{6,5},{7,4},{8,11},{9,10},{10,... | collective-permute-start | bytes 307208 | tf_op jit(solution)/shard_map/ppermute | solution.py:374
  43.3 0.0 collective-permute-done.1
  43.3 0.0 collective-permute-done.2
  43.3 0.1 collective-permute-start.3
  43.4 2.8 %collective-permute-start.4 = (bf16[400,128]{1,0:T(8,128)(2,1)S(1)}, bf16[400,128]{1,0:T(8,128)(2,1)S(1)}, u32[]{:S(2)}, u32[]{:S(2)}) collective-permute-start(bf16[400,128]{1,0:T(8,128)(2,1)S(1)} %get-tuple-element.38), channel_id=1, source_target_pairs={{0,5},{1,4},{2,7},{3,6},{4,1},{5,0},{6,3},{7,2},{8,13},{9,12},{10,... | collective-permute-start | bytes 307208 | tf_op jit(solution)/shard_map/ppermute | solution.py:374
  46.2 1.3 %collective-permute-start.5 = (bf16[400,128]{1,0:T(8,128)(2,1)S(1)}, bf16[400,128]{1,0:T(8,128)(2,1)S(1)}, u32[]{:S(2)}, u32[]{:S(2)}) collective-permute-start(bf16[400,128]{1,0:T(8,128)(2,1)S(1)} %get-tuple-element.39), channel_id=1, source_target_pairs={{0,6},{1,7},{2,4},{3,5},{4,2},{5,3},{6,0},{7,1},{8,14},{9,15},{10,... | collective-permute-start | bytes 307208 | tf_op jit(solution)/shard_map/ppermute | solution.py:374
  47.5 0.0 collective-permute-done.7.refs_0_
  47.5 3.5 %collective-permute-start.6 = (bf16[400,128]{1,0:T(8,128)(2,1)S(1)}, bf16[400,128]{1,0:T(8,128)(2,1)S(1)}, u32[]{:S(2)}, u32[]{:S(2)}) collective-permute-start(bf16[400,128]{1,0:T(8,128)(2,1)S(1)} %get-tuple-element.40), channel_id=1, source_target_pairs={{0,7},{1,6},{2,5},{3,4},{4,3},{5,2},{6,1},{7,0},{8,15},{9,14},{10,... | collective-permute-start | bytes 307208 | tf_op jit(solution)/shard_map/ppermute | solution.py:374
  51.0 0.5 collective-permute-start.9
  51.5 7.1 %local.1 = (bf16[512,768]{1,0:T(8,128)(2,1)S(1)}, f32[512,128]{1,0:T(8,128)S(1)}) custom-call(s32[4]{0:T(128)S(1)} %copy-done.3, bf16[128,768]{1,0:T(8,128)(2,1)S(1)} %bitcast.6, bf16[128,768]{1,0:T(8,128)(2,1)} %bitcast.3.refs_1_, bf16[128,768]{1,0:T(8,128)(2,1)} %bitcast.4.refs_2_, bf16[128,768]{1,0:T(8,128)(2,1)} %bitcast.5.refs_3_, ...), custom_call_target="tpu_custom_call" | custom-call | flops 8000000000 | bytes 10000000 | tf_op jit(solution)/shard_map/local/pallas_call | solution.py:188
  58.6 0.0 collective-permute-done.9.refs_2_
  58.6 1.8 %merge.2.refs_4_ = bf16[512,768]{1,0:T(8,128)(2,1)S(1)} custom-call(s32[4]{0:T(128)S(1)} %copy-done.3, bf16[512,768]{1,0:T(8,128)(2,1)S(1)} %get-tuple-element.35.out_ref, f32[512,128]{1,0:T(8,128)S(1)} %get-tuple-element.36.log_ref, bf16[768,768]{1,0:T(8,128)(2,1)S(1)} %copy-done, bf16[400,128]{1,0:T(8,128)(2,1)S(1)} %collective-permute-done.7.refs_0_, ...), custom_call_target="tpu_custom_call" | custom-call | flops 1000000 | bytes 10000 | tf_op jit(solution)/shard_map/merge/pallas_call | solution.py:355
  60.4 0.3 collective-permute-done.4.refs_1_
  60.7 2.7 %merge.3 = bf16[1,512,768]{2,1,0:T(8,128)(2,1)} custom-call(s32[4]{0:T(128)S(1)} %copy-done.3, bf16[512,768]{1,0:T(8,128)(2,1)S(1)} %get-tuple-element.35.out_ref, f32[512,128]{1,0:T(8,128)S(1)} %get-tuple-element.36.log_ref, bf16[768,768]{1,0:T(8,128)(2,1)S(1)} %copy-done, bf16[400,128]{1,0:T(8,128)(2,1)S(1)} %collective-permute-done.3.refs_0_, ...), custom_call_target="tpu_custom_call" | custom-call | flops 1000000 | bytes 10000 | tf_op jit(solution)/shard_map/merge/pallas_call | solution.py:355
  (12 shorter events, 0.0 us)
Async XLA Ops:
  5.0 28.0 %all-to-all-start = ((bf16[32,16,768]{2,1,0:T(8,128)(2,1)}), bf16[32,16,768]{2,1,0:T(8,128)(2,1)}, u32[]{:S(2)}, u32[]{:S(2)}) async-start(bf16[32,16,768]{2,1,0:T(8,128)(2,1)} %bitcast.7), calls=%async_computation | async-start | bytes 1572864 | tf_op jit(solution)/shard_map/all_to_all | solution.py:392
  12.4 30.9 %collective-permute-start = (bf16[8,16,768]{2,1,0:T(8,128)(2,1)}, bf16[8,16,768]{2,1,0:T(8,128)(2,1)}, u32[]{:S(2)}, u32[]{:S(2)}) collective-permute-start(bf16[8,16,768]{2,1,0:T(8,128)(2,1)} %get-tuple-element.28), channel_id=1, source_target_pairs={{0,8},{8,0},{16,24},{24,16},{1,9},{9,1},{17,25},{25,17},{2,10},{10... | collective-permute-start | bytes 589832 | tf_op jit(solution)/shard_map/ppermute | solution.py:374
  12.7 30.6 %collective-permute-start.1 = (bf16[8,16,768]{2,1,0:T(8,128)(2,1)}, bf16[8,16,768]{2,1,0:T(8,128)(2,1)}, u32[]{:S(2)}, u32[]{:S(2)}) collective-permute-start(bf16[8,16,768]{2,1,0:T(8,128)(2,1)} %get-tuple-element.29), channel_id=1, source_target_pairs={{0,16},{8,24},{16,0},{24,8},{1,17},{9,25},{17,1},{25,9},{2,18},{10... | collective-permute-start | bytes 589832 | tf_op jit(solution)/shard_map/ppermute | solution.py:374
  14.4 28.9 %collective-permute-start.2 = (bf16[8,16,768]{2,1,0:T(8,128)(2,1)}, bf16[8,16,768]{2,1,0:T(8,128)(2,1)}, u32[]{:S(2)}, u32[]{:S(2)}) collective-permute-start(bf16[8,16,768]{2,1,0:T(8,128)(2,1)} %get-tuple-element.30), channel_id=1, source_target_pairs={{0,24},{8,16},{16,8},{24,0},{1,25},{9,17},{17,9},{25,1},{2,26},{10... | collective-permute-start | bytes 589832 | tf_op jit(solution)/shard_map/ppermute | solution.py:374
  14.4 0.9 %copy-start.1 = (bf16[8,16,768]{2,1,0:T(8,128)(2,1)S(1)}, bf16[8,16,768]{2,1,0:T(8,128)(2,1)}, u32[]{:S(2)}) copy-start(bf16[8,16,768]{2,1,0:T(8,128)(2,1)} %get-tuple-element.26.after) | copy-start | bytes 589828
  15.3 17.7 %copy-start.3 = (s32[4]{0:T(128)S(1)}, s32[4]{0:T(128)}, u32[]{:S(2)}) copy-start(s32[4]{0:T(128)} %counts_ref.7) | copy-start | bytes 52
  33.0 18.5 %copy-start.2 = (bf16[8,16,768]{2,1,0:T(8,128)(2,1)S(1)}, bf16[8,16,768]{2,1,0:T(8,128)(2,1)}, u32[]{:S(2)}) copy-start(bf16[8,16,768]{2,1,0:T(8,128)(2,1)} %get-tuple-element.26.after) | copy-start | bytes 589828
  40.3 7.2 %collective-permute-start.7 = (bf16[400,128]{1,0:T(8,128)(2,1)S(1)}, bf16[400,128]{1,0:T(8,128)(2,1)S(1)}, u32[]{:S(2)}, u32[]{:S(2)}) collective-permute-start(bf16[400,128]{1,0:T(8,128)(2,1)S(1)} %get-tuple-element.41), channel_id=1, source_target_pairs={{0,2},{1,3},{2,0},{3,1},{4,6},{5,7},{6,4},{7,5},{8,10},{9,11},{10,... | collective-permute-start | bytes 307208 | tf_op jit(solution)/shard_map/ppermute | solution.py:374
  41.7 9.3 %collective-permute-start.8 = (bf16[400,128]{1,0:T(8,128)(2,1)S(1)}, bf16[400,128]{1,0:T(8,128)(2,1)S(1)}, u32[]{:S(2)}, u32[]{:S(2)}) collective-permute-start(bf16[400,128]{1,0:T(8,128)(2,1)S(1)} %get-tuple-element.42), channel_id=1, source_target_pairs={{0,3},{1,2},{2,1},{3,0},{4,7},{5,6},{6,5},{7,4},{8,11},{9,10},{10,... | collective-permute-start | bytes 307208 | tf_op jit(solution)/shard_map/ppermute | solution.py:374
  43.3 17.1 %collective-permute-start.3 = (bf16[400,128]{1,0:T(8,128)(2,1)S(1)}, bf16[400,128]{1,0:T(8,128)(2,1)S(1)}, u32[]{:S(2)}, u32[]{:S(2)}) collective-permute-start(bf16[400,128]{1,0:T(8,128)(2,1)S(1)} %get-tuple-element.37), channel_id=1, source_target_pairs={{0,4},{1,5},{2,6},{3,7},{4,0},{5,1},{6,2},{7,3},{8,12},{9,13},{10,... | collective-permute-start | bytes 307208 | tf_op jit(solution)/shard_map/ppermute | solution.py:374
  43.4 17.3 %collective-permute-start.4 = (bf16[400,128]{1,0:T(8,128)(2,1)S(1)}, bf16[400,128]{1,0:T(8,128)(2,1)S(1)}, u32[]{:S(2)}, u32[]{:S(2)}) collective-permute-start(bf16[400,128]{1,0:T(8,128)(2,1)S(1)} %get-tuple-element.38), channel_id=1, source_target_pairs={{0,5},{1,4},{2,7},{3,6},{4,1},{5,0},{6,3},{7,2},{8,13},{9,12},{10,... | collective-permute-start | bytes 307208 | tf_op jit(solution)/shard_map/ppermute | solution.py:374
  46.2 14.5 %collective-permute-start.5 = (bf16[400,128]{1,0:T(8,128)(2,1)S(1)}, bf16[400,128]{1,0:T(8,128)(2,1)S(1)}, u32[]{:S(2)}, u32[]{:S(2)}) collective-permute-start(bf16[400,128]{1,0:T(8,128)(2,1)S(1)} %get-tuple-element.39), channel_id=1, source_target_pairs={{0,6},{1,7},{2,4},{3,5},{4,2},{5,3},{6,0},{7,1},{8,14},{9,15},{10,... | collective-permute-start | bytes 307208 | tf_op jit(solution)/shard_map/ppermute | solution.py:374
  47.5 13.2 %collective-permute-start.6 = (bf16[400,128]{1,0:T(8,128)(2,1)S(1)}, bf16[400,128]{1,0:T(8,128)(2,1)S(1)}, u32[]{:S(2)}, u32[]{:S(2)}) collective-permute-start(bf16[400,128]{1,0:T(8,128)(2,1)S(1)} %get-tuple-element.40), channel_id=1, source_target_pairs={{0,7},{1,6},{2,5},{3,4},{4,3},{5,2},{6,1},{7,0},{8,15},{9,14},{10,... | collective-permute-start | bytes 307208 | tf_op jit(solution)/shard_map/ppermute | solution.py:374
  51.0 7.6 %copy-start = (bf16[768,768]{1,0:T(8,128)(2,1)S(1)}, bf16[768,768]{1,0:T(8,128)(2,1)}, u32[]{:S(2)}) copy-start(bf16[768,768]{1,0:T(8,128)(2,1)} %weight_ref.3) | copy-start | bytes 3538948
  51.0 7.6 %collective-permute-start.9 = (bf16[400,128]{1,0:T(8,128)(2,1)S(1)}, bf16[400,128]{1,0:T(8,128)(2,1)S(1)}, u32[]{:S(2)}, u32[]{:S(2)}) collective-permute-start(bf16[400,128]{1,0:T(8,128)(2,1)S(1)} %get-tuple-element.43), channel_id=1, source_target_pairs={{0,1},{1,0},{2,3},{3,2},{4,5},{5,4},{6,7},{7,6},{8,9},{9,8},{10,11... | collective-permute-start | bytes 307208 | tf_op jit(solution)/shard_map/ppermute | solution.py:374

commit v5 on v4

--- a/solution.py
+++ b/solution.py
@@ -203,6 +203,8 @@
 
 def dilated_kernel(dp, ctx, block, sends, counts_ref, rows, weight_ref, *refs):
     out_refs, (keys, values) = refs[:-2], refs[-2:]
+    out_refs = [ref.at[place] for ref, group in zip(out_refs, sends) for place in range(len(group))]
+    sends = [other for group in sends for other in group]
     me, mine = lax.axis_index("dp"), lax.axis_index("ctx")
     count, features = rows.shape
     portion = count // ctx
@@ -248,7 +250,7 @@
     vmem = pl.BlockSpec(memory_space=pltpu.VMEM)
     return pl.pallas_call(
         functools.partial(dilated_kernel, dp, ctx, min(256, count), sends),
-        out_shape=[jax.ShapeDtypeStruct((packed_rows(portion, features), 128), BF16)] * len(sends),
+        out_shape=[jax.ShapeDtypeStruct((len(group), packed_rows(portion, features), 128), BF16) for group in sends],
         in_specs=[pl.BlockSpec(memory_space=pltpu.SMEM)] + [vmem] * 2,
         out_specs=[vmem] * len(sends),
         scratch_shapes=[pltpu.VMEM((count, features), BF16)] * 2,
@@ -307,6 +309,8 @@
 
 def merge_part_kernel(dp, ctx, sends, with_others, counts_ref, out_ref, log_ref, weight_ref, *refs):
     pieces, refs = refs[: len(sends)], refs[len(sends) :]
+    pieces = [(other, ref.at[place]) for ref, group in zip(pieces, sends) for place, other in enumerate(group)]
+    sends = [other for other, _ in pieces]
     mixed_ref, (dilated, own, own_logs) = refs[-4], refs[-3:]
     me, mine = lax.axis_index("dp"), lax.axis_index("ctx")
     count, features = out_ref.shape
@@ -319,7 +323,7 @@
         at = pl.multiple_of(part * sub + first * each, each)
         own[part * span : (part + 1) * span, :] = out_ref[pl.ds(at, span), :]
         own_logs[part * span : (part + 1) * span, :] = log_ref[pl.ds(at, span), :]
-    for other, piece in zip(sends, pieces):
+    for other, piece in pieces:
         for part in range(dp):
             at = pl.multiple_of(part * span + ((mine ^ other) - first) * each, each)
             for block in range(features // 128):
@@ -351,7 +355,7 @@
     count, features = out.shape
     vmem = pl.BlockSpec(memory_space=pltpu.VMEM)
     shape = (1, count, features) if others else (count, features)
-    rows = count * len(sends) // ctx
+    rows = count * sum(len(group) for group in sends) // ctx
     return pl.pallas_call(
         functools.partial(merge_part_kernel, dp, ctx, sends, len(others)),
         out_shape=jax.ShapeDtypeStruct(shape, BF16),
@@ -392,25 +396,34 @@
     regrouped = lax.all_to_all(
         by_residue.reshape(ctx * dp, each, features), ("ctx", "dp"), split_axis=0, concat_axis=0, tiled=True
     ).reshape(count, features)
+    regrouped, *pieces = lax.optimization_barrier((regrouped, *pieces))
     w_near = fetch(w_qkv, made[0])
     portion = count // ctx
     if aligned:
-        sends = (4, 5, 6, 7, 2, 3, 1, 0) if ctx == 8 else tuple(range(ctx))
-        made = dilated_attention(tile_counts, regrouped, w_near, dp, ctx, sends)
-        found = {other: exchange(piece, "ctx", other) for other, piece in zip(sends, made)}
-        tied = lax.optimization_barrier((found[0], *pieces))
-        found[0], pieces = tied[0], tied[1:]
+        if ctx == 8:
+            far, sends = ((4,), (5,), (6,), (7,)), ((2, 3), (1,), (0,))
+            *across, two_three, one, own = dilated_attention(tile_counts, regrouped, w_near, dp, ctx, far + sends)
+            across = [exchange(piece, "ctx", other) for piece, (other,) in zip(across, far)]
+            two_three = exchange(two_three, "ctx", 2)
+            one_three = exchange(jnp.concatenate([one, two_three[1:]]), "ctx", 1)
+            parts = [((2,), (0,), (1, 3)), [two_three, own, one_three]], [far, across]
+        else:
+            sends = tuple((other,) for other in range(ctx))
+            own, *made = dilated_attention(tile_counts, regrouped, w_near, dp, ctx, sends)
+            made = [exchange(piece, "ctx", other) for piece, (other,) in zip(made, sends[1:])]
+            parts = ([sends, [own, *made]],)
+        own, *pieces = lax.optimization_barrier((own, *pieces))
+        parts[0][1][1 if ctx == 8 else 0] = own
         out, logs = local_attention(tile_counts, pieces, w_near, ctx)
         mixed = ()
-        for some in ((2, 3, 1, 0), (4, 5, 6, 7)) if ctx == 8 else (sends,):
-            received = [found[other] for other in some]
-            mixed = (merge_part(tile_counts, out, logs, w_out, received, dp, ctx, some, mixed),)
+        for sends, received in parts:
+            mixed = (merge_part(tile_counts, out, logs, w_out, received, dp, ctx, sends, mixed),)
         return mixed[0].reshape(1, count, features)
     else:
         out, logs = local_attention(tile_counts, pieces, w_near, ctx)
-        made = dilated_attention(tile_counts, regrouped, w_near, dp, ctx, list(range(ctx)))
+        made = dilated_attention(tile_counts, regrouped, w_near, dp, ctx, (tuple(range(ctx)),))[0]
         order = jnp.stack([lax.axis_index("ctx") ^ other for other in range(ctx)])
-        packed = lax.all_to_all(jnp.stack(made)[order], "ctx", split_axis=0, concat_axis=0, tiled=True)
+        packed = lax.all_to_all(made[order], "ctx", split_axis=0, concat_axis=0, tiled=True)
         wide = packed[:, :-16].reshape(ctx, features // 128, portion, 128).swapaxes(1, 2).reshape(ctx, portion, features)
         lanes = packed[:, -16:].reshape(ctx, 16, 4, 32).swapaxes(1, 2)[:, : portion // 16].reshape(ctx, portion, 32)
         whole = jnp.concatenate([wide, jnp.pad(lanes, ((0, 0), (0, 0), (0, 96)))], axis=-1)

time: 64.5 us -> 63.9 us (level); the launches traced: 63.4 us -> 63.6 us
  local copies, waits for them, and re-layouts: 0.94 us -> 2.98 us
  waiting for transfers between devices: 16 us -> 14.9 us
    all_to_all x1, waiting for transfers between devices: 15.7 us -> 1.86 us  [body(): lax.all_to_all(by_residue.reshape(ctx * dp, each, features), ('ctx', 'dp'...]
    ppermute x10 -> x9, waiting for transfers between devices: 0.35 us -> 13.1 us  [exchange(): lax.ppermute(value, axis, [(i, i ^ other) for i in range(lax.axis_size(ax...]
    unnamed x8 -> x20, local copies, waits for them, and re-layouts: 0.94 us -> 2.97 us
    ppermute x10 -> x9, starting transfers between devices: 13.2 us -> 12.9 us  [exchange(): lax.ppermute(value, axis, [(i, i ^ other) for i in range(lax.axis_size(ax...]
  transfers between devices with their start and end apart: 11 -> 10, of which waited for: 2 -> 5; matrix products, arithmetic and copies ran while one was open for 0% -> 0% of each run, Pallas kernels for 28% -> 16%
where the time goes in v5:
time: 63.9 us; the launch traced here: 63.6 us
  Pallas kernels  25.2 us (39%)
  starting transfers between devices  20.3 us (32%)
  waiting for transfers between devices  14.9 us (23%)
  local copies, waits for them, and re-layouts  2.98 us (5%)
    ppermute x9, waiting for transfers between devices, exchange(): lax.ppermute(value, axis, [(i, i ^ other) for i in range(lax.axis_size(ax...  13.1 us
    ppermute x9, starting transfers between devices, exchange(): lax.ppermute(value, axis, [(i, i ^ other) for i in range(lax.axis_size(ax...  12.9 us
    all_to_all x1, starting transfers between devices, body(): lax.all_to_all(by_residue.reshape(ctx * dp, each, features), ('ctx', 'dp'...  7.42 us
    pallas_call x1, Pallas kernels, dilated_attention(): pl.pallas_call(functools.partial(dilated_kernel, dp, ctx, min(256, count)...  7.24 us
    pallas_call x1, Pallas kernels, local_attention(): pl.pallas_call(functools.partial(local_kernel, dp, ctx, min(256, count)),...  6.48 us
    pallas_call x1, Pallas kernels, embed(): pl.pallas_call(functools.partial(embed_kernel, ctx, steps, int(split)), o...  5.01 us
    pallas_call x2, Pallas kernels, merge_part(): pl.pallas_call(functools.partial(merge_part_kernel, dp, ctx, sends, len(o...  4.43 us
    unnamed x20, local copies, waits for them, and re-layouts  2.97 us
  transfers between devices with their start and end apart: 10, of which 5 were waited for; matrix products, arithmetic and copies ran while one was open for 0% of the time, Pallas kernels for 16%

profile of v5, /device:TPU:0, one launch (start us, length us, event | category | flops | bytes accessed | tf_op | source)
XLA Modules:
  0.0 63.6 jit_solution(503963258418797884)
XLA Ops:
  0.0 5.0 %embed.1 = (bf16[8,4,16,768]{3,2,1,0:T(8,128)(2,1)}, bf16[8,16,768]{2,1,0:T(8,128)(2,1)}, bf16[8,16,768]{2,1,0:T(8,128)(2,1)}, bf16[8,16,768]{2,1,0:T(8,128)(2,1)}, bf16[8,16,768]{2,1,0:T(8,128)(2,1)}) custom-call(bf16[4,1,128,1536]{3,2,1,0:T(8,128)(2,1)} %x_hbm.1, bf16[1536,768]{1,0:T(8,128)(2,1)} %w_hbm.1), custom_call_target="tpu_custom_call" | custom-call | tf_op jit(solution)/shard_map/embed/pallas_call | solution.py:80
  5.0 7.4 %all-to-all-start = ((bf16[32,16,768]{2,1,0:T(8,128)(2,1)}), bf16[32,16,768]{2,1,0:T(8,128)(2,1)}, u32[]{:S(2)}, u32[]{:S(2)}) async-start(bf16[32,16,768]{2,1,0:T(8,128)(2,1)} %bitcast.10), calls=%async_computation | async-start | bytes 1572864 | tf_op jit(solution)/shard_map/all_to_all | solution.py:396
  12.4 0.3 collective-permute-start
  12.7 1.7 %collective-permute-start.1 = (bf16[8,16,768]{2,1,0:T(8,128)(2,1)}, bf16[8,16,768]{2,1,0:T(8,128)(2,1)S(1)}, u32[]{:S(2)}, u32[]{:S(2)}) collective-permute-start(bf16[8,16,768]{2,1,0:T(8,128)(2,1)} %get-tuple-element.32), channel_id=1, source_target_pairs={{0,16},{8,24},{16,0},{24,8},{1,17},{9,25},{17,1},{25,9},{2,18},{10... | collective-permute-start | bytes 589832 | tf_op jit(solution)/shard_map/ppermute | solution.py:378
  14.4 0.9 %copy-done.1 = bf16[8,16,768]{2,1,0:T(8,128)(2,1)S(1)} copy-done((bf16[8,16,768]{2,1,0:T(8,128)(2,1)S(1)}, bf16[8,16,768]{2,1,0:T(8,128)(2,1)}, u32[]{:S(2)}) %copy-start.1) | copy-done | bytes 196632
  15.3 2.0 %fetch.1.weight_ref.refs_4_ = bf16[768,2304]{1,0:T(8,128)(2,1)S(1)} custom-call(bf16[768,2304]{1,0:T(8,128)(2,1)} %source.1, bf16[8,16,768]{2,1,0:T(8,128)(2,1)S(1)} %copy-done.1), custom_call_target="tpu_custom_call" | custom-call | bytes 8000000 | tf_op jit(solution)/shard_map/fetch/pallas_call | solution.py:105
  17.4 0.7 %copy-done.4 = bf16[8,16,768]{2,1,0:T(8,128)(2,1)} copy-done((bf16[8,16,768]{2,1,0:T(8,128)(2,1)}, bf16[8,16,768]{2,1,0:T(8,128)(2,1)S(1)}, u32[]{:S(2)}) %copy-start.4) | copy-done | bytes 196632
  18.0 8.9 %collective-permute-done.1 = bf16[8,16,768]{2,1,0:T(8,128)(2,1)S(1)} collective-permute-done((bf16[8,16,768]{2,1,0:T(8,128)(2,1)}, bf16[8,16,768]{2,1,0:T(8,128)(2,1)S(1)}, u32[]{:S(2)}, u32[]{:S(2)}) %collective-permute-start.1) | collective-permute-done | bytes 196640 | tf_op jit(solution)/shard_map/ppermute | solution.py:378
  27.0 0.7 %copy-done.6 = bf16[8,16,768]{2,1,0:T(8,128)(2,1)} copy-done((bf16[8,16,768]{2,1,0:T(8,128)(2,1)}, bf16[8,16,768]{2,1,0:T(8,128)(2,1)S(1)}, u32[]{:S(2)}) %copy-start.6) | copy-done | bytes 196632
  27.6 2.9 %collective-permute-done.2 = bf16[8,16,768]{2,1,0:T(8,128)(2,1)S(1)} collective-permute-done((bf16[8,16,768]{2,1,0:T(8,128)(2,1)}, bf16[8,16,768]{2,1,0:T(8,128)(2,1)S(1)}, u32[]{:S(2)}, u32[]{:S(2)}) %collective-permute-start.2) | collective-permute-done | bytes 196640 | tf_op jit(solution)/shard_map/ppermute | solution.py:378
  30.5 0.7 %copy-done.8 = bf16[8,16,768]{2,1,0:T(8,128)(2,1)} copy-done((bf16[8,16,768]{2,1,0:T(8,128)(2,1)}, bf16[8,16,768]{2,1,0:T(8,128)(2,1)S(1)}, u32[]{:S(2)}) %copy-start.8) | copy-done | bytes 196632
  31.2 1.9 %all-to-all-done = bf16[32,16,768]{2,1,0:T(8,128)(2,1)} async-done(((bf16[32,16,768]{2,1,0:T(8,128)(2,1)}), bf16[32,16,768]{2,1,0:T(8,128)(2,1)}, u32[]{:S(2)}, u32[]{:S(2)}) %all-to-all-start) | async-done | bytes 786464 | tf_op jit(solution)/shard_map/all_to_all | solution.py:396
  33.1 7.2 %dilated.1 = (bf16[1,400,128]{2,1,0:T(8,128)(2,1)S(1)}, bf16[1,400,128]{2,1,0:T(8,128)(2,1)S(1)}, bf16[1,400,128]{2,1,0:T(8,128)(2,1)S(1)}, bf16[1,400,128]{2,1,...) custom-call(s32[4]{0:T(128)S(1)} %copy-done.3, ...), custom_call_target="tpu_custom_call" | custom-call | flops 1000000 | bytes 10000 | tf_op jit(solution)/shard_map/dilated/pallas_call | solution.py:251
  40.3 1.5 %collective-permute-start.7 = (bf16[2,400,128]{2,1,0:T(8,128)(2,1)S(1)}, bf16[2,400,128]{2,1,0:T(8,128)(2,1)S(1)}, u32[]{:S(2)}, u32[]{:S(2)}) collective-permute-start(bf16[2,400,128]{2,1,0:T(8,128)(2,1)S(1)} %get-tuple-element.50), channel_id=1, source_target_pairs={{0,2},{1,3},{2,0},{3,1},{4,6},{5,7},{6,4},{7,5},{8,10},{9,11},{10,... | collective-permute-start | bytes 614408 | tf_op jit(solution)/shard_map/ppermute | solution.py:378
  41.8 1.8 %collective-permute-start.3 = (bf16[1,400,128]{2,1,0:T(8,128)(2,1)S(1)}, bf16[1,400,128]{2,1,0:T(8,128)(2,1)S(1)}, u32[]{:S(2)}, u32[]{:S(2)}) collective-permute-start(bf16[1,400,128]{2,1,0:T(8,128)(2,1)S(1)} %get-tuple-element.46), channel_id=1, source_target_pairs={{0,4},{1,5},{2,6},{3,7},{4,0},{5,1},{6,2},{7,3},{8,12},{9,13},{10,... | collective-permute-start | bytes 307208 | tf_op jit(solution)/shard_map/ppermute | solution.py:378
  43.6 1.5 %collective-permute-start.4 = (bf16[1,400,128]{2,1,0:T(8,128)(2,1)S(1)}, bf16[1,400,128]{2,1,0:T(8,128)(2,1)S(1)}, u32[]{:S(2)}, u32[]{:S(2)}) collective-permute-start(bf16[1,400,128]{2,1,0:T(8,128)(2,1)S(1)} %get-tuple-element.47), channel_id=1, source_target_pairs={{0,5},{1,4},{2,7},{3,6},{4,1},{5,0},{6,3},{7,2},{8,13},{9,12},{10,... | collective-permute-start | bytes 307208 | tf_op jit(solution)/shard_map/ppermute | solution.py:378
  45.1 2.2 %collective-permute-start.5 = (bf16[1,400,128]{2,1,0:T(8,128)(2,1)S(1)}, bf16[1,400,128]{2,1,0:T(8,128)(2,1)S(1)}, u32[]{:S(2)}, u32[]{:S(2)}) collective-permute-start(bf16[1,400,128]{2,1,0:T(8,128)(2,1)S(1)} %get-tuple-element.48), channel_id=1, source_target_pairs={{0,6},{1,7},{2,4},{3,5},{4,2},{5,3},{6,0},{7,1},{8,14},{9,15},{10,... | collective-permute-start | bytes 307208 | tf_op jit(solution)/shard_map/ppermute | solution.py:378
  47.3 2.1 %collective-permute-start.6 = (bf16[1,400,128]{2,1,0:T(8,128)(2,1)S(1)}, bf16[1,400,128]{2,1,0:T(8,128)(2,1)S(1)}, u32[]{:S(2)}, u32[]{:S(2)}) collective-permute-start(bf16[1,400,128]{2,1,0:T(8,128)(2,1)S(1)} %get-tuple-element.49), channel_id=1, source_target_pairs={{0,7},{1,6},{2,5},{3,4},{4,3},{5,2},{6,1},{7,0},{8,15},{9,14},{10,... | collective-permute-start | bytes 307208 | tf_op jit(solution)/shard_map/ppermute | solution.py:378
  49.4 1.1 %collective-permute-done.7.refs_0_ = bf16[2,400,128]{2,1,0:T(8,128)(2,1)S(1)} collective-permute-done((bf16[2,400,128]{2,1,0:T(8,128)(2,1)S(1)}, bf16[2,400,128]{2,1,0:T(8,128)(2,1)S(1)}, u32[]{:S(2)}, u32[]{:S(2)}) %collective-permute-start.7) | collective-permute-done | bytes 204832 | tf_op jit(solution)/shard_map/ppermute | solution.py:378
  50.6 1.9 %collective-permute-start.8 = (bf16[2,400,128]{2,1,0:T(8,128)(2,1)S(1)}, bf16[2,400,128]{2,1,0:T(8,128)(2,1)S(1)}, u32[]{:S(2)}, u32[]{:S(2)}) collective-permute-start(bf16[2,400,128]{2,1,0:T(8,128)(2,1)S(1)} %pad_maximum_fusion), channel_id=1, source_target_pairs={{0,1},{1,0},{2,3},{3,2},{4,5},{5,4},{6,7},{7,6},{8,9},{9,8},{10,11... | collective-permute-start | bytes 614408 | tf_op jit(solution)/shard_map/ppermute | solution.py:378
  52.5 6.5 %local.1 = (bf16[512,768]{1,0:T(8,128)(2,1)S(1)}, f32[512,128]{1,0:T(8,128)S(1)}) custom-call(s32[4]{0:T(128)S(1)} %copy-done.3, bf16[128,768]{1,0:T(8,128)(2,1)S(1)} %bitcast.6, bf16[128,768]{1,0:T(8,128)(2,1)S(1)} %bitcast.7, bf16[128,768]{1,0:T(8,128)(2,1)S(1)} %bitcast.8, bf16[128,768]{1,0:T(8,128)(2,1)S(1)} %bitcast.9, ...), custom_call_target="tpu_custom_call" | custom-call | flops 8000000000 | bytes 10000000 | tf_op jit(solution)/shard_map/local/pallas_call | solution.py:188
  58.9 0.2 collective-permute-done.8.refs_2_
  59.1 1.8 %merge.2.refs_4_ = bf16[512,768]{1,0:T(8,128)(2,1)S(1)} custom-call(s32[4]{0:T(128)S(1)} %copy-done.3, bf16[512,768]{1,0:T(8,128)(2,1)S(1)} %get-tuple-element.44.out_ref, f32[512,128]{1,0:T(8,128)S(1)} %get-tuple-element.45.log_ref, bf16[768,768]{1,0:T(8,128)(2,1)S(1)} %copy-done, bf16[2,400,128]{2,1,0:T(8,128)(2,1)S(1)} %collective-permute-done.7.refs_0_, ...), custom_call_target="tpu_custom_call" | custom-call | flops 1000000 | bytes 10000 | tf_op jit(solution)/shard_map/merge/pallas_call | solution.py:359
  60.9 2.7 %merge.3 = bf16[1,512,768]{2,1,0:T(8,128)(2,1)} custom-call(s32[4]{0:T(128)S(1)} %copy-done.3, bf16[512,768]{1,0:T(8,128)(2,1)S(1)} %get-tuple-element.44.out_ref, f32[512,128]{1,0:T(8,128)S(1)} %get-tuple-element.45.log_ref, bf16[768,768]{1,0:T(8,128)(2,1)S(1)} %copy-done, bf16[1,400,128]{2,1,0:T(8,128)(2,1)S(1)} %collective-permute-done.3.refs_0_, ...), custom_call_target="tpu_custom_call" | custom-call | flops 1000000 | bytes 10000 | tf_op jit(solution)/shard_map/merge/pallas_call | solution.py:359
  (24 shorter events, 0.1 us)
Async XLA Ops:
  5.0 28.0 %all-to-all-start = ((bf16[32,16,768]{2,1,0:T(8,128)(2,1)}), bf16[32,16,768]{2,1,0:T(8,128)(2,1)}, u32[]{:S(2)}, u32[]{:S(2)}) async-start(bf16[32,16,768]{2,1,0:T(8,128)(2,1)} %bitcast.10), calls=%async_computation | async-start | bytes 1572864 | tf_op jit(solution)/shard_map/all_to_all | solution.py:396
  12.4 4.9 %collective-permute-start = (bf16[8,16,768]{2,1,0:T(8,128)(2,1)}, bf16[8,16,768]{2,1,0:T(8,128)(2,1)S(1)}, u32[]{:S(2)}, u32[]{:S(2)}) collective-permute-start(bf16[8,16,768]{2,1,0:T(8,128)(2,1)} %get-tuple-element.31), channel_id=1, source_target_pairs={{0,8},{8,0},{16,24},{24,16},{1,9},{9,1},{17,25},{25,17},{2,10},{10... | collective-permute-start | bytes 589832 | tf_op jit(solution)/shard_map/ppermute | solution.py:378
  12.7 14.3 %collective-permute-start.1 = (bf16[8,16,768]{2,1,0:T(8,128)(2,1)}, bf16[8,16,768]{2,1,0:T(8,128)(2,1)S(1)}, u32[]{:S(2)}, u32[]{:S(2)}) collective-permute-start(bf16[8,16,768]{2,1,0:T(8,128)(2,1)} %get-tuple-element.32), channel_id=1, source_target_pairs={{0,16},{8,24},{16,0},{24,8},{1,17},{9,25},{17,1},{25,9},{2,18},{10... | collective-permute-start | bytes 589832 | tf_op jit(solution)/shard_map/ppermute | solution.py:378
  14.4 16.1 %collective-permute-start.2 = (bf16[8,16,768]{2,1,0:T(8,128)(2,1)}, bf16[8,16,768]{2,1,0:T(8,128)(2,1)S(1)}, u32[]{:S(2)}, u32[]{:S(2)}) collective-permute-start(bf16[8,16,768]{2,1,0:T(8,128)(2,1)} %get-tuple-element.33), channel_id=1, source_target_pairs={{0,24},{8,16},{16,8},{24,0},{1,25},{9,17},{17,9},{25,1},{2,26},{10... | collective-permute-start | bytes 589832 | tf_op jit(solution)/shard_map/ppermute | solution.py:378
  14.4 0.9 %copy-start.1 = (bf16[8,16,768]{2,1,0:T(8,128)(2,1)S(1)}, bf16[8,16,768]{2,1,0:T(8,128)(2,1)}, u32[]{:S(2)}) copy-start(bf16[8,16,768]{2,1,0:T(8,128)(2,1)} %get-tuple-element.30.after) | copy-start | bytes 589828
  15.3 17.7 %copy-start.3 = (s32[4]{0:T(128)S(1)}, s32[4]{0:T(128)}, u32[]{:S(2)}) copy-start(s32[4]{0:T(128)} %counts_ref.7) | copy-start | bytes 52
  17.4 0.7 %copy-start.4 = (bf16[8,16,768]{2,1,0:T(8,128)(2,1)}, bf16[8,16,768]{2,1,0:T(8,128)(2,1)S(1)}, u32[]{:S(2)}) copy-start(bf16[8,16,768]{2,1,0:T(8,128)(2,1)S(1)} %collective-permute-done) | copy-start | bytes 589828
  27.0 0.7 %copy-start.6 = (bf16[8,16,768]{2,1,0:T(8,128)(2,1)}, bf16[8,16,768]{2,1,0:T(8,128)(2,1)S(1)}, u32[]{:S(2)}) copy-start(bf16[8,16,768]{2,1,0:T(8,128)(2,1)S(1)} %collective-permute-done.1) | copy-start | bytes 589828
  30.5 0.7 %copy-start.8 = (bf16[8,16,768]{2,1,0:T(8,128)(2,1)}, bf16[8,16,768]{2,1,0:T(8,128)(2,1)S(1)}, u32[]{:S(2)}) copy-start(bf16[8,16,768]{2,1,0:T(8,128)(2,1)S(1)} %collective-permute-done.2) | copy-start | bytes 589828
  33.1 19.4 %copy-start.2 = (bf16[8,16,768]{2,1,0:T(8,128)(2,1)S(1)}, bf16[8,16,768]{2,1,0:T(8,128)(2,1)}, u32[]{:S(2)}) copy-start(bf16[8,16,768]{2,1,0:T(8,128)(2,1)} %get-tuple-element.30.after) | copy-start | bytes 589828
  33.1 19.4 %copy-start.5 = (bf16[8,16,768]{2,1,0:T(8,128)(2,1)S(1)}, bf16[8,16,768]{2,1,0:T(8,128)(2,1)}, u32[]{:S(2)}) copy-start(bf16[8,16,768]{2,1,0:T(8,128)(2,1)} %copy-done.4) | copy-start | bytes 589828
  33.1 19.4 %copy-start.7 = (bf16[8,16,768]{2,1,0:T(8,128)(2,1)S(1)}, bf16[8,16,768]{2,1,0:T(8,128)(2,1)}, u32[]{:S(2)}) copy-start(bf16[8,16,768]{2,1,0:T(8,128)(2,1)} %copy-done.6) | copy-start | bytes 589828
  33.1 19.4 %copy-start.9 = (bf16[8,16,768]{2,1,0:T(8,128)(2,1)S(1)}, bf16[8,16,768]{2,1,0:T(8,128)(2,1)}, u32[]{:S(2)}) copy-start(bf16[8,16,768]{2,1,0:T(8,128)(2,1)} %copy-done.8) | copy-start | bytes 589828
  40.3 10.2 %collective-permute-start.7 = (bf16[2,400,128]{2,1,0:T(8,128)(2,1)S(1)}, bf16[2,400,128]{2,1,0:T(8,128)(2,1)S(1)}, u32[]{:S(2)}, u32[]{:S(2)}) collective-permute-start(bf16[2,400,128]{2,1,0:T(8,128)(2,1)S(1)} %get-tuple-element.50), channel_id=1, source_target_pairs={{0,2},{1,3},{2,0},{3,1},{4,6},{5,7},{6,4},{7,5},{8,10},{9,11},{10,... | collective-permute-start | bytes 614408 | tf_op jit(solution)/shard_map/ppermute | solution.py:378
  41.8 19.1 %collective-permute-start.3 = (bf16[1,400,128]{2,1,0:T(8,128)(2,1)S(1)}, bf16[1,400,128]{2,1,0:T(8,128)(2,1)S(1)}, u32[]{:S(2)}, u32[]{:S(2)}) collective-permute-start(bf16[1,400,128]{2,1,0:T(8,128)(2,1)S(1)} %get-tuple-element.46), channel_id=1, source_target_pairs={{0,4},{1,5},{2,6},{3,7},{4,0},{5,1},{6,2},{7,3},{8,12},{9,13},{10,... | collective-permute-start | bytes 307208 | tf_op jit(solution)/shard_map/ppermute | solution.py:378
  43.6 17.3 %collective-permute-start.4 = (bf16[1,400,128]{2,1,0:T(8,128)(2,1)S(1)}, bf16[1,400,128]{2,1,0:T(8,128)(2,1)S(1)}, u32[]{:S(2)}, u32[]{:S(2)}) collective-permute-start(bf16[1,400,128]{2,1,0:T(8,128)(2,1)S(1)} %get-tuple-element.47), channel_id=1, source_target_pairs={{0,5},{1,4},{2,7},{3,6},{4,1},{5,0},{6,3},{7,2},{8,13},{9,12},{10,... | collective-permute-start | bytes 307208 | tf_op jit(solution)/shard_map/ppermute | solution.py:378
  45.1 15.8 %collective-permute-start.5 = (bf16[1,400,128]{2,1,0:T(8,128)(2,1)S(1)}, bf16[1,400,128]{2,1,0:T(8,128)(2,1)S(1)}, u32[]{:S(2)}, u32[]{:S(2)}) collective-permute-start(bf16[1,400,128]{2,1,0:T(8,128)(2,1)S(1)} %get-tuple-element.48), channel_id=1, source_target_pairs={{0,6},{1,7},{2,4},{3,5},{4,2},{5,3},{6,0},{7,1},{8,14},{9,15},{10,... | collective-permute-start | bytes 307208 | tf_op jit(solution)/shard_map/ppermute | solution.py:378
  47.3 13.7 %collective-permute-start.6 = (bf16[1,400,128]{2,1,0:T(8,128)(2,1)S(1)}, bf16[1,400,128]{2,1,0:T(8,128)(2,1)S(1)}, u32[]{:S(2)}, u32[]{:S(2)}) collective-permute-start(bf16[1,400,128]{2,1,0:T(8,128)(2,1)S(1)} %get-tuple-element.49), channel_id=1, source_target_pairs={{0,7},{1,6},{2,5},{3,4},{4,3},{5,2},{6,1},{7,0},{8,15},{9,14},{10,... | collective-permute-start | bytes 307208 | tf_op jit(solution)/shard_map/ppermute | solution.py:378
  50.6 8.6 %copy-start = (bf16[768,768]{1,0:T(8,128)(2,1)S(1)}, bf16[768,768]{1,0:T(8,128)(2,1)}, u32[]{:S(2)}) copy-start(bf16[768,768]{1,0:T(8,128)(2,1)} %weight_ref.3) | copy-start | bytes 3538948
  50.6 8.5 %collective-permute-start.8 = (bf16[2,400,128]{2,1,0:T(8,128)(2,1)S(1)}, bf16[2,400,128]{2,1,0:T(8,128)(2,1)S(1)}, u32[]{:S(2)}, u32[]{:S(2)}) collective-permute-start(bf16[2,400,128]{2,1,0:T(8,128)(2,1)S(1)} %pad_maximum_fusion), channel_id=1, source_target_pairs={{0,1},{1,0},{2,3},{3,2},{4,5},{5,4},{6,7},{7,6},{8,9},{9,8},{10,11... | collective-permute-start | bytes 614408 | tf_op jit(solution)/shard_map/ppermute | solution.py:378

commit v6 on v5

--- a/solution.py
+++ b/solution.py
@@ -27,32 +27,38 @@
 def embed_kernel(ctx, steps, split, x_hbm, w_hbm, *refs):
     slides, _, sub, width = x_hbm.shape
     outs = refs[: slides + split]
-    x_parts, w_parts, made, arrived, sent = refs[slides + split :]
+    early, late, weight, made, arrived, sent = refs[slides + split :]
     part = width // steps
+    half = slides // 2
     loads = []
     for step in range(steps):
         columns = pl.ds(step * part, part)
         loads.append(
             (
-                pltpu.make_async_copy(w_hbm.at[columns], w_parts.at[step], arrived.at[0, step]),
-                pltpu.make_async_copy(x_hbm.at[:, 0, :, columns], x_parts.at[step], arrived.at[1, step]),
+                pltpu.make_async_copy(w_hbm.at[columns], weight.at[columns], arrived.at[0, step]),
+                pltpu.make_async_copy(x_hbm.at[pl.ds(0, half), 0, :, columns], early.at[step], arrived.at[1, step]),
             )
         )
         for load in loads[-1]:
             load.start()
+    last = pltpu.make_async_copy(x_hbm.at[pl.ds(half, slides - half), 0], late, arrived.at[0, steps])
+    last.start()
     total = None
     for step in range(steps):
         for load in loads[step]:
             load.wait()
-        product = dot(x_parts[step].reshape(slides * sub, part), w_parts[step])
+        product = dot(early[step].reshape(half * sub, part), weight[step * part : (step + 1) * part, :])
         total = product if total is None else total + product
+    last.wait()
+    totals = (total, dot(late[...].reshape((slides - half) * sub, width), weight[...]))
     me = lax.axis_index("dp")
     each = sub // ctx
     target, source = iota((sub, sub), 0), iota((sub, sub), 1)
     order = (source == target % each * ctx + target // each).astype(BF16)
     stores = []
     for slide in range(slides):
-        hidden = total[slide * sub : (slide + 1) * sub].astype(BF16).astype(F32)
+        start = slide % half * sub
+        hidden = totals[slide // half][start : start + sub].astype(BF16).astype(F32)
         centered = hidden - jnp.mean(hidden, axis=-1, keepdims=True)
         variance = jnp.mean(centered * centered, axis=-1, keepdims=True)
         normed = (centered * lax.rsqrt(variance + EPSILON)).astype(BF16)
@@ -83,10 +89,11 @@
         in_specs=[hbm] * 2,
         out_specs=[hbm] * len(outs),
         scratch_shapes=[
-            pltpu.VMEM((steps, slides, sub, part), BF16),
-            pltpu.VMEM((steps, part, features), BF16),
+            pltpu.VMEM((steps, slides // 2, sub, part), BF16),
+            pltpu.VMEM((slides - slides // 2, sub, width), BF16),
+            pltpu.VMEM((width, features), BF16),
             pltpu.VMEM((slides,) + shape, BF16),
-            pltpu.SemaphoreType.DMA((2, steps)),
+            pltpu.SemaphoreType.DMA((2, steps + 1)),
             pltpu.SemaphoreType.DMA((2, slides)),
         ],
         compiler_params=pltpu.CompilerParams(vmem_limit_bytes=60 * MIB),
@@ -311,7 +318,7 @@
     pieces, refs = refs[: len(sends)], refs[len(sends) :]
     pieces = [(other, ref.at[place]) for ref, group in zip(pieces, sends) for place, other in enumerate(group)]
     sends = [other for other, _ in pieces]
-    mixed_ref, (dilated, own, own_logs) = refs[-4], refs[-3:]
+    mixed_ref, (dilated, own, own_logs, ready, sent) = refs[-6], refs[-5:]
     me, mine = lax.axis_index("dp"), lax.axis_index("ctx")
     count, features = out_ref.shape
     sub = count // dp
@@ -341,14 +348,18 @@
     mixed = jnp.where(position < counts_ref[me], mixed, 0.0).astype(BF16)
     target, source = iota((sub, span), 0), iota((sub, span), 1)
     order = (target == source % each * ctx + first + source // each).astype(BF16)
+    stores = []
     for part in range(dp):
         made = dot(order, mixed[part * span : (part + 1) * span])
         rows = slice(part * sub, (part + 1) * sub)
         if with_others:
-            made = made + refs[0][rows, :].astype(F32)
-            mixed_ref[0, rows, :] = made.astype(BF16)
+            ready[rows, :] = (made + refs[0][rows, :].astype(F32)).astype(BF16)
+            stores.append(pltpu.make_async_copy(ready.at[rows], mixed_ref.at[0, rows], sent.at[part]))
+            stores[-1].start()
         else:
             mixed_ref[rows, :] = made.astype(BF16)
+    for store in stores:
+        store.wait()
 
 
 def merge_part(tile_counts, out, logs, w_out, received, dp, ctx, sends, others=()):
@@ -360,11 +371,13 @@
         functools.partial(merge_part_kernel, dp, ctx, sends, len(others)),
         out_shape=jax.ShapeDtypeStruct(shape, BF16),
         in_specs=[pl.BlockSpec(memory_space=pltpu.SMEM)] + [vmem] * (3 + len(received) + len(others)),
-        out_specs=vmem,
+        out_specs=pl.BlockSpec(memory_space=pltpu.HBM) if others else vmem,
         scratch_shapes=[
             pltpu.VMEM((rows, features + 128), BF16),
             pltpu.VMEM((rows, features), BF16),
             pltpu.VMEM((rows, 128), F32),
+            pltpu.VMEM((count if others else 16, features), BF16),
+            pltpu.SemaphoreType.DMA((dp,)),
         ],
         compiler_params=pltpu.CompilerParams(vmem_limit_bytes=24 * MIB),
         cost_estimate=pl.CostEstimate(flops=10**6, bytes_accessed=10**4, transcendentals=0),

time: 63.9 us -> 63.8 us (level)
  no operation moved by 1% of the time
where the time goes in v6:
time: 63.8 us; the launch traced here: 63.5 us
  Pallas kernels  25.1 us (39%)
  starting transfers between devices  20.3 us (32%)
  waiting for transfers between devices  14.9 us (23%)
  local copies, waits for them, and re-layouts  2.98 us (5%)
    ppermute x9, waiting for transfers between devices, exchange(): lax.ppermute(value, axis, [(i, i ^ other) for i in range(lax.axis_size(ax...  13.1 us
    ppermute x9, starting transfers between devices, exchange(): lax.ppermute(value, axis, [(i, i ^ other) for i in range(lax.axis_size(ax...  12.9 us
    all_to_all x1, starting transfers between devices, body(): lax.all_to_all(by_residue.reshape(ctx * dp, each, features), ('ctx', 'dp'...  7.42 us
    pallas_call x1, Pallas kernels, dilated_attention(): pl.pallas_call(functools.partial(dilated_kernel, dp, ctx, min(256, count)...  7.24 us
    pallas_call x1, Pallas kernels, local_attention(): pl.pallas_call(functools.partial(local_kernel, dp, ctx, min(256, count)),...  6.48 us
    pallas_call x1, Pallas kernels, embed(): pl.pallas_call(functools.partial(embed_kernel, ctx, steps, int(split)), o...  4.96 us
    pallas_call x2, Pallas kernels, merge_part(): pl.pallas_call(functools.partial(merge_part_kernel, dp, ctx, sends, len(o...  4.36 us
    unnamed x20, local copies, waits for them, and re-layouts  2.97 us
  transfers between devices with their start and end apart: 10, of which 5 were waited for; matrix products, arithmetic and copies ran while one was open for 0% of the time, Pallas kernels for 16%

profile of v6, /device:TPU:0, one launch (start us, length us, event | category | flops | bytes accessed | tf_op | source)
XLA Modules:
  0.0 63.5 jit_solution(5365051401160404772)
XLA Ops:
  0.0 5.0 %embed.1 = (bf16[8,4,16,768]{3,2,1,0:T(8,128)(2,1)}, bf16[8,16,768]{2,1,0:T(8,128)(2,1)}, bf16[8,16,768]{2,1,0:T(8,128)(2,1)}, bf16[8,16,768]{2,1,0:T(8,128)(2,1)}, bf16[8,16,768]{2,1,0:T(8,128)(2,1)}) custom-call(bf16[4,1,128,1536]{3,2,1,0:T(8,128)(2,1)} %x_hbm.1, bf16[1536,768]{1,0:T(8,128)(2,1)} %w_hbm.1), custom_call_target="tpu_custom_call" | custom-call | tf_op jit(solution)/shard_map/embed/pallas_call | solution.py:86
  5.0 7.4 %all-to-all-start = ((bf16[32,16,768]{2,1,0:T(8,128)(2,1)}), bf16[32,16,768]{2,1,0:T(8,128)(2,1)}, u32[]{:S(2)}, u32[]{:S(2)}) async-start(bf16[32,16,768]{2,1,0:T(8,128)(2,1)} %bitcast.10), calls=%async_computation | async-start | bytes 1572864 | tf_op jit(solution)/shard_map/all_to_all | solution.py:409
  12.4 0.3 collective-permute-start
  12.6 1.7 %collective-permute-start.1 = (bf16[8,16,768]{2,1,0:T(8,128)(2,1)}, bf16[8,16,768]{2,1,0:T(8,128)(2,1)S(1)}, u32[]{:S(2)}, u32[]{:S(2)}) collective-permute-start(bf16[8,16,768]{2,1,0:T(8,128)(2,1)} %get-tuple-element.32), channel_id=1, source_target_pairs={{0,16},{8,24},{16,0},{24,8},{1,17},{9,25},{17,1},{25,9},{2,18},{10... | collective-permute-start | bytes 589832 | tf_op jit(solution)/shard_map/ppermute | solution.py:391
  14.3 0.9 %copy-done.1 = bf16[8,16,768]{2,1,0:T(8,128)(2,1)S(1)} copy-done((bf16[8,16,768]{2,1,0:T(8,128)(2,1)S(1)}, bf16[8,16,768]{2,1,0:T(8,128)(2,1)}, u32[]{:S(2)}) %copy-start.1) | copy-done | bytes 196632
  15.3 2.0 %fetch.1.weight_ref.refs_4_ = bf16[768,2304]{1,0:T(8,128)(2,1)S(1)} custom-call(bf16[768,2304]{1,0:T(8,128)(2,1)} %source.1, bf16[8,16,768]{2,1,0:T(8,128)(2,1)S(1)} %copy-done.1), custom_call_target="tpu_custom_call" | custom-call | bytes 8000000 | tf_op jit(solution)/shard_map/fetch/pallas_call | solution.py:112
  17.3 0.7 %copy-done.4 = bf16[8,16,768]{2,1,0:T(8,128)(2,1)} copy-done((bf16[8,16,768]{2,1,0:T(8,128)(2,1)}, bf16[8,16,768]{2,1,0:T(8,128)(2,1)S(1)}, u32[]{:S(2)}) %copy-start.4) | copy-done | bytes 196632
  18.0 8.9 %collective-permute-done.1 = bf16[8,16,768]{2,1,0:T(8,128)(2,1)S(1)} collective-permute-done((bf16[8,16,768]{2,1,0:T(8,128)(2,1)}, bf16[8,16,768]{2,1,0:T(8,128)(2,1)S(1)}, u32[]{:S(2)}, u32[]{:S(2)}) %collective-permute-start.1) | collective-permute-done | bytes 196640 | tf_op jit(solution)/shard_map/ppermute | solution.py:391
  26.9 0.7 %copy-done.6 = bf16[8,16,768]{2,1,0:T(8,128)(2,1)} copy-done((bf16[8,16,768]{2,1,0:T(8,128)(2,1)}, bf16[8,16,768]{2,1,0:T(8,128)(2,1)S(1)}, u32[]{:S(2)}) %copy-start.6) | copy-done | bytes 196632
  27.6 2.9 %collective-permute-done.2 = bf16[8,16,768]{2,1,0:T(8,128)(2,1)S(1)} collective-permute-done((bf16[8,16,768]{2,1,0:T(8,128)(2,1)}, bf16[8,16,768]{2,1,0:T(8,128)(2,1)S(1)}, u32[]{:S(2)}, u32[]{:S(2)}) %collective-permute-start.2) | collective-permute-done | bytes 196640 | tf_op jit(solution)/shard_map/ppermute | solution.py:391
  30.5 0.7 %copy-done.8 = bf16[8,16,768]{2,1,0:T(8,128)(2,1)} copy-done((bf16[8,16,768]{2,1,0:T(8,128)(2,1)}, bf16[8,16,768]{2,1,0:T(8,128)(2,1)S(1)}, u32[]{:S(2)}) %copy-start.8) | copy-done | bytes 196632
  31.1 1.9 %all-to-all-done = bf16[32,16,768]{2,1,0:T(8,128)(2,1)} async-done(((bf16[32,16,768]{2,1,0:T(8,128)(2,1)}), bf16[32,16,768]{2,1,0:T(8,128)(2,1)}, u32[]{:S(2)}, u32[]{:S(2)}) %all-to-all-start) | async-done | bytes 786464 | tf_op jit(solution)/shard_map/all_to_all | solution.py:409
  33.0 7.2 %dilated.1 = (bf16[1,400,128]{2,1,0:T(8,128)(2,1)S(1)}, bf16[1,400,128]{2,1,0:T(8,128)(2,1)S(1)}, bf16[1,400,128]{2,1,0:T(8,128)(2,1)S(1)}, bf16[1,400,128]{2,1,...) custom-call(s32[4]{0:T(128)S(1)} %copy-done.3, ...), custom_call_target="tpu_custom_call" | custom-call | flops 1000000 | bytes 10000 | tf_op jit(solution)/shard_map/dilated/pallas_call | solution.py:258
  40.3 1.5 %collective-permute-start.7 = (bf16[2,400,128]{2,1,0:T(8,128)(2,1)S(1)}, bf16[2,400,128]{2,1,0:T(8,128)(2,1)S(1)}, u32[]{:S(2)}, u32[]{:S(2)}) collective-permute-start(bf16[2,400,128]{2,1,0:T(8,128)(2,1)S(1)} %get-tuple-element.50), channel_id=1, source_target_pairs={{0,2},{1,3},{2,0},{3,1},{4,6},{5,7},{6,4},{7,5},{8,10},{9,11},{10,... | collective-permute-start | bytes 614408 | tf_op jit(solution)/shard_map/ppermute | solution.py:391
  41.7 1.8 %collective-permute-start.3 = (bf16[1,400,128]{2,1,0:T(8,128)(2,1)S(1)}, bf16[1,400,128]{2,1,0:T(8,128)(2,1)S(1)}, u32[]{:S(2)}, u32[]{:S(2)}) collective-permute-start(bf16[1,400,128]{2,1,0:T(8,128)(2,1)S(1)} %get-tuple-element.46), channel_id=1, source_target_pairs={{0,4},{1,5},{2,6},{3,7},{4,0},{5,1},{6,2},{7,3},{8,12},{9,13},{10,... | collective-permute-start | bytes 307208 | tf_op jit(solution)/shard_map/ppermute | solution.py:391
  43.5 1.5 %collective-permute-start.4 = (bf16[1,400,128]{2,1,0:T(8,128)(2,1)S(1)}, bf16[1,400,128]{2,1,0:T(8,128)(2,1)S(1)}, u32[]{:S(2)}, u32[]{:S(2)}) collective-permute-start(bf16[1,400,128]{2,1,0:T(8,128)(2,1)S(1)} %get-tuple-element.47), channel_id=1, source_target_pairs={{0,5},{1,4},{2,7},{3,6},{4,1},{5,0},{6,3},{7,2},{8,13},{9,12},{10,... | collective-permute-start | bytes 307208 | tf_op jit(solution)/shard_map/ppermute | solution.py:391
  45.0 2.2 %collective-permute-start.5 = (bf16[1,400,128]{2,1,0:T(8,128)(2,1)S(1)}, bf16[1,400,128]{2,1,0:T(8,128)(2,1)S(1)}, u32[]{:S(2)}, u32[]{:S(2)}) collective-permute-start(bf16[1,400,128]{2,1,0:T(8,128)(2,1)S(1)} %get-tuple-element.48), channel_id=1, source_target_pairs={{0,6},{1,7},{2,4},{3,5},{4,2},{5,3},{6,0},{7,1},{8,14},{9,15},{10,... | collective-permute-start | bytes 307208 | tf_op jit(solution)/shard_map/ppermute | solution.py:391
  47.2 2.1 %collective-permute-start.6 = (bf16[1,400,128]{2,1,0:T(8,128)(2,1)S(1)}, bf16[1,400,128]{2,1,0:T(8,128)(2,1)S(1)}, u32[]{:S(2)}, u32[]{:S(2)}) collective-permute-start(bf16[1,400,128]{2,1,0:T(8,128)(2,1)S(1)} %get-tuple-element.49), channel_id=1, source_target_pairs={{0,7},{1,6},{2,5},{3,4},{4,3},{5,2},{6,1},{7,0},{8,15},{9,14},{10,... | collective-permute-start | bytes 307208 | tf_op jit(solution)/shard_map/ppermute | solution.py:391
  49.4 1.1 %collective-permute-done.7.refs_0_ = bf16[2,400,128]{2,1,0:T(8,128)(2,1)S(1)} collective-permute-done((bf16[2,400,128]{2,1,0:T(8,128)(2,1)S(1)}, bf16[2,400,128]{2,1,0:T(8,128)(2,1)S(1)}, u32[]{:S(2)}, u32[]{:S(2)}) %collective-permute-start.7) | collective-permute-done | bytes 204832 | tf_op jit(solution)/shard_map/ppermute | solution.py:391
  50.5 1.9 %collective-permute-start.8 = (bf16[2,400,128]{2,1,0:T(8,128)(2,1)S(1)}, bf16[2,400,128]{2,1,0:T(8,128)(2,1)S(1)}, u32[]{:S(2)}, u32[]{:S(2)}) collective-permute-start(bf16[2,400,128]{2,1,0:T(8,128)(2,1)S(1)} %pad_maximum_fusion), channel_id=1, source_target_pairs={{0,1},{1,0},{2,3},{3,2},{4,5},{5,4},{6,7},{7,6},{8,9},{9,8},{10,11... | collective-permute-start | bytes 614408 | tf_op jit(solution)/shard_map/ppermute | solution.py:391
  52.4 6.5 %local.1 = (bf16[512,768]{1,0:T(8,128)(2,1)S(1)}, f32[512,128]{1,0:T(8,128)S(1)}) custom-call(s32[4]{0:T(128)S(1)} %copy-done.3, bf16[128,768]{1,0:T(8,128)(2,1)S(1)} %bitcast.6, bf16[128,768]{1,0:T(8,128)(2,1)S(1)} %bitcast.7, bf16[128,768]{1,0:T(8,128)(2,1)S(1)} %bitcast.8, bf16[128,768]{1,0:T(8,128)(2,1)S(1)} %bitcast.9, ...), custom_call_target="tpu_custom_call" | custom-call | flops 8000000000 | bytes 10000000 | tf_op jit(solution)/shard_map/local/pallas_call | solution.py:195
  58.9 0.2 collective-permute-done.8.refs_2_
  59.1 1.8 %merge.2.refs_4_ = bf16[512,768]{1,0:T(8,128)(2,1)S(1)} custom-call(s32[4]{0:T(128)S(1)} %copy-done.3, bf16[512,768]{1,0:T(8,128)(2,1)S(1)} %get-tuple-element.44.out_ref, f32[512,128]{1,0:T(8,128)S(1)} %get-tuple-element.45.log_ref, bf16[768,768]{1,0:T(8,128)(2,1)S(1)} %copy-done, bf16[2,400,128]{2,1,0:T(8,128)(2,1)S(1)} %collective-permute-done.7.refs_0_, ...), custom_call_target="tpu_custom_call" | custom-call | flops 1000000 | bytes 10000 | tf_op jit(solution)/shard_map/merge/pallas_call | solution.py:370
  60.9 2.5 %merge.3 = bf16[1,512,768]{2,1,0:T(8,128)(2,1)} custom-call(s32[4]{0:T(128)S(1)} %copy-done.3, bf16[512,768]{1,0:T(8,128)(2,1)S(1)} %get-tuple-element.44.out_ref, f32[512,128]{1,0:T(8,128)S(1)} %get-tuple-element.45.log_ref, bf16[768,768]{1,0:T(8,128)(2,1)S(1)} %copy-done, bf16[1,400,128]{2,1,0:T(8,128)(2,1)S(1)} %collective-permute-done.3.refs_0_, ...), custom_call_target="tpu_custom_call" | custom-call | flops 1000000 | bytes 10000 | tf_op jit(solution)/shard_map/merge/pallas_call | solution.py:370
  (24 shorter events, 0.1 us)
Async XLA Ops:
  5.0 28.0 %all-to-all-start = ((bf16[32,16,768]{2,1,0:T(8,128)(2,1)}), bf16[32,16,768]{2,1,0:T(8,128)(2,1)}, u32[]{:S(2)}, u32[]{:S(2)}) async-start(bf16[32,16,768]{2,1,0:T(8,128)(2,1)} %bitcast.10), calls=%async_computation | async-start | bytes 1572864 | tf_op jit(solution)/shard_map/all_to_all | solution.py:409
  12.4 4.9 %collective-permute-start = (bf16[8,16,768]{2,1,0:T(8,128)(2,1)}, bf16[8,16,768]{2,1,0:T(8,128)(2,1)S(1)}, u32[]{:S(2)}, u32[]{:S(2)}) collective-permute-start(bf16[8,16,768]{2,1,0:T(8,128)(2,1)} %get-tuple-element.31), channel_id=1, source_target_pairs={{0,8},{8,0},{16,24},{24,16},{1,9},{9,1},{17,25},{25,17},{2,10},{10... | collective-permute-start | bytes 589832 | tf_op jit(solution)/shard_map/ppermute | solution.py:391
  12.6 14.3 %collective-permute-start.1 = (bf16[8,16,768]{2,1,0:T(8,128)(2,1)}, bf16[8,16,768]{2,1,0:T(8,128)(2,1)S(1)}, u32[]{:S(2)}, u32[]{:S(2)}) collective-permute-start(bf16[8,16,768]{2,1,0:T(8,128)(2,1)} %get-tuple-element.32), channel_id=1, source_target_pairs={{0,16},{8,24},{16,0},{24,8},{1,17},{9,25},{17,1},{25,9},{2,18},{10... | collective-permute-start | bytes 589832 | tf_op jit(solution)/shard_map/ppermute | solution.py:391
  14.3 16.1 %collective-permute-start.2 = (bf16[8,16,768]{2,1,0:T(8,128)(2,1)}, bf16[8,16,768]{2,1,0:T(8,128)(2,1)S(1)}, u32[]{:S(2)}, u32[]{:S(2)}) collective-permute-start(bf16[8,16,768]{2,1,0:T(8,128)(2,1)} %get-tuple-element.33), channel_id=1, source_target_pairs={{0,24},{8,16},{16,8},{24,0},{1,25},{9,17},{17,9},{25,1},{2,26},{10... | collective-permute-start | bytes 589832 | tf_op jit(solution)/shard_map/ppermute | solution.py:391
  14.3 0.9 %copy-start.1 = (bf16[8,16,768]{2,1,0:T(8,128)(2,1)S(1)}, bf16[8,16,768]{2,1,0:T(8,128)(2,1)}, u32[]{:S(2)}) copy-start(bf16[8,16,768]{2,1,0:T(8,128)(2,1)} %get-tuple-element.30.after) | copy-start | bytes 589828
  15.3 17.7 %copy-start.3 = (s32[4]{0:T(128)S(1)}, s32[4]{0:T(128)}, u32[]{:S(2)}) copy-start(s32[4]{0:T(128)} %counts_ref.7) | copy-start | bytes 52
  17.3 0.7 %copy-start.4 = (bf16[8,16,768]{2,1,0:T(8,128)(2,1)}, bf16[8,16,768]{2,1,0:T(8,128)(2,1)S(1)}, u32[]{:S(2)}) copy-start(bf16[8,16,768]{2,1,0:T(8,128)(2,1)S(1)} %collective-permute-done) | copy-start | bytes 589828
  26.9 0.7 %copy-start.6 = (bf16[8,16,768]{2,1,0:T(8,128)(2,1)}, bf16[8,16,768]{2,1,0:T(8,128)(2,1)S(1)}, u32[]{:S(2)}) copy-start(bf16[8,16,768]{2,1,0:T(8,128)(2,1)S(1)} %collective-permute-done.1) | copy-start | bytes 589828
  30.5 0.7 %copy-start.8 = (bf16[8,16,768]{2,1,0:T(8,128)(2,1)}, bf16[8,16,768]{2,1,0:T(8,128)(2,1)S(1)}, u32[]{:S(2)}) copy-start(bf16[8,16,768]{2,1,0:T(8,128)(2,1)S(1)} %collective-permute-done.2) | copy-start | bytes 589828
  33.0 19.4 %copy-start.2 = (bf16[8,16,768]{2,1,0:T(8,128)(2,1)S(1)}, bf16[8,16,768]{2,1,0:T(8,128)(2,1)}, u32[]{:S(2)}) copy-start(bf16[8,16,768]{2,1,0:T(8,128)(2,1)} %get-tuple-element.30.after) | copy-start | bytes 589828
  33.0 19.4 %copy-start.5 = (bf16[8,16,768]{2,1,0:T(8,128)(2,1)S(1)}, bf16[8,16,768]{2,1,0:T(8,128)(2,1)}, u32[]{:S(2)}) copy-start(bf16[8,16,768]{2,1,0:T(8,128)(2,1)} %copy-done.4) | copy-start | bytes 589828
  33.0 19.4 %copy-start.7 = (bf16[8,16,768]{2,1,0:T(8,128)(2,1)S(1)}, bf16[8,16,768]{2,1,0:T(8,128)(2,1)}, u32[]{:S(2)}) copy-start(bf16[8,16,768]{2,1,0:T(8,128)(2,1)} %copy-done.6) | copy-start | bytes 589828
  33.0 19.4 %copy-start.9 = (bf16[8,16,768]{2,1,0:T(8,128)(2,1)S(1)}, bf16[8,16,768]{2,1,0:T(8,128)(2,1)}, u32[]{:S(2)}) copy-start(bf16[8,16,768]{2,1,0:T(8,128)(2,1)} %copy-done.8) | copy-start | bytes 589828
  40.3 10.2 %collective-permute-start.7 = (bf16[2,400,128]{2,1,0:T(8,128)(2,1)S(1)}, bf16[2,400,128]{2,1,0:T(8,128)(2,1)S(1)}, u32[]{:S(2)}, u32[]{:S(2)}) collective-permute-start(bf16[2,400,128]{2,1,0:T(8,128)(2,1)S(1)} %get-tuple-element.50), channel_id=1, source_target_pairs={{0,2},{1,3},{2,0},{3,1},{4,6},{5,7},{6,4},{7,5},{8,10},{9,11},{10,... | collective-permute-start | bytes 614408 | tf_op jit(solution)/shard_map/ppermute | solution.py:391
  41.7 19.2 %collective-permute-start.3 = (bf16[1,400,128]{2,1,0:T(8,128)(2,1)S(1)}, bf16[1,400,128]{2,1,0:T(8,128)(2,1)S(1)}, u32[]{:S(2)}, u32[]{:S(2)}) collective-permute-start(bf16[1,400,128]{2,1,0:T(8,128)(2,1)S(1)} %get-tuple-element.46), channel_id=1, source_target_pairs={{0,4},{1,5},{2,6},{3,7},{4,0},{5,1},{6,2},{7,3},{8,12},{9,13},{10,... | collective-permute-start | bytes 307208 | tf_op jit(solution)/shard_map/ppermute | solution.py:391
  43.5 17.4 %collective-permute-start.4 = (bf16[1,400,128]{2,1,0:T(8,128)(2,1)S(1)}, bf16[1,400,128]{2,1,0:T(8,128)(2,1)S(1)}, u32[]{:S(2)}, u32[]{:S(2)}) collective-permute-start(bf16[1,400,128]{2,1,0:T(8,128)(2,1)S(1)} %get-tuple-element.47), channel_id=1, source_target_pairs={{0,5},{1,4},{2,7},{3,6},{4,1},{5,0},{6,3},{7,2},{8,13},{9,12},{10,... | collective-permute-start | bytes 307208 | tf_op jit(solution)/shard_map/ppermute | solution.py:391
  45.0 15.9 %collective-permute-start.5 = (bf16[1,400,128]{2,1,0:T(8,128)(2,1)S(1)}, bf16[1,400,128]{2,1,0:T(8,128)(2,1)S(1)}, u32[]{:S(2)}, u32[]{:S(2)}) collective-permute-start(bf16[1,400,128]{2,1,0:T(8,128)(2,1)S(1)} %get-tuple-element.48), channel_id=1, source_target_pairs={{0,6},{1,7},{2,4},{3,5},{4,2},{5,3},{6,0},{7,1},{8,14},{9,15},{10,... | collective-permute-start | bytes 307208 | tf_op jit(solution)/shard_map/ppermute | solution.py:391
  47.2 13.7 %collective-permute-start.6 = (bf16[1,400,128]{2,1,0:T(8,128)(2,1)S(1)}, bf16[1,400,128]{2,1,0:T(8,128)(2,1)S(1)}, u32[]{:S(2)}, u32[]{:S(2)}) collective-permute-start(bf16[1,400,128]{2,1,0:T(8,128)(2,1)S(1)} %get-tuple-element.49), channel_id=1, source_target_pairs={{0,7},{1,6},{2,5},{3,4},{4,3},{5,2},{6,1},{7,0},{8,15},{9,14},{10,... | collective-permute-start | bytes 307208 | tf_op jit(solution)/shard_map/ppermute | solution.py:391
  50.5 8.6 %copy-start = (bf16[768,768]{1,0:T(8,128)(2,1)S(1)}, bf16[768,768]{1,0:T(8,128)(2,1)}, u32[]{:S(2)}) copy-start(bf16[768,768]{1,0:T(8,128)(2,1)} %weight_ref.3) | copy-start | bytes 3538948
  50.5 8.5 %collective-permute-start.8 = (bf16[2,400,128]{2,1,0:T(8,128)(2,1)S(1)}, bf16[2,400,128]{2,1,0:T(8,128)(2,1)S(1)}, u32[]{:S(2)}, u32[]{:S(2)}) collective-permute-start(bf16[2,400,128]{2,1,0:T(8,128)(2,1)S(1)} %pad_maximum_fusion), channel_id=1, source_target_pairs={{0,1},{1,0},{2,3},{3,2},{4,5},{5,4},{6,7},{7,6},{8,9},{9,8},{10,11... | collective-permute-start | bytes 614408 | tf_op jit(solution)/shard_map/ppermute | solution.py:391

commit v7 on v6

--- a/solution.py
+++ b/solution.py
@@ -26,8 +26,7 @@
 
 def embed_kernel(ctx, steps, split, x_hbm, w_hbm, *refs):
     slides, _, sub, width = x_hbm.shape
-    outs = refs[: slides + split]
-    early, late, weight, made, arrived, sent = refs[slides + split :]
+    outs, (early, late, weight, made, arrived, sent) = refs[:-6], refs[-6:]
     part = width // steps
     half = slides // 2
     loads = []
@@ -66,11 +65,32 @@
         if split:
             stores.append(pltpu.make_async_copy(made.at[slide], outs[0].at[:, slide], sent.at[1, slide]))
             stores[-1].start()
-    for other in range(slides):
-        stores.append(pltpu.make_async_copy(made.at[me ^ other], outs[split + other], sent.at[0, other]))
-        stores[-1].start()
+    if not split:
+        for other in range(slides):
+            stores.append(pltpu.make_async_copy(made.at[me ^ other], outs[other], sent.at[0, other]))
+            stores[-1].start()
     for store in stores:
         store.wait()
+
+
+def part_kernel(by_residue, *outs):
+    me = lax.axis_index("dp")
+    for other, out in enumerate(outs):
+        out[...] = by_residue[:, me ^ other]
+
+
+def part_slides(by_residue):
+    ctx, slides, each, features = by_residue.shape
+    vmem = pl.BlockSpec(memory_space=pltpu.VMEM)
+    return pl.pallas_call(
+        part_kernel,
+        out_shape=[jax.ShapeDtypeStruct((ctx, each, features), BF16)] * slides,
+        in_specs=[vmem],
+        out_specs=[vmem] * slides,
+        compiler_params=pltpu.CompilerParams(vmem_limit_bytes=16 * MIB),
+        cost_estimate=pl.CostEstimate(flops=10**6, bytes_accessed=10**4, transcendentals=0),
+        name="part",
+    )(by_residue)
 
 
 def embed(tile_embed, w_in, ctx, split):
@@ -79,9 +99,10 @@
     steps = 6
     part = width // steps
     shape = (ctx, sub // ctx, features) if split else (sub, features)
-    outs = [jax.ShapeDtypeStruct(shape, BF16)] * slides
     if split:
-        outs = [jax.ShapeDtypeStruct((ctx, slides, sub // ctx, features), BF16)] + outs
+        outs = [jax.ShapeDtypeStruct((ctx, slides, sub // ctx, features), BF16)]
+    else:
+        outs = [jax.ShapeDtypeStruct(shape, BF16)] * slides
     hbm = pl.BlockSpec(memory_space=pltpu.HBM)
     return pl.pallas_call(
         functools.partial(embed_kernel, ctx, steps, int(split)),
@@ -400,7 +421,7 @@
     aligned = each % 16 == 0 and ctx <= 8
     made = embed(tile_embed, w_in, ctx, aligned)
     if aligned:
-        by_residue, made = made[0], made[1:]
+        by_residue, made = made[0], part_slides(made[0])
     else:
         slide_of = [lax.axis_index("dp") ^ other for other in range(dp)]
         stacked = jnp.stack(made)[jnp.stack(slide_of)]

time: 63.8 us -> 63.5 us (level)
    unnamed x20 -> x22, local copies, waits for them, and re-layouts: 2.97 us -> 3.24 us
where the time goes in v7:
time: 63.5 us; the launch traced here: 63.2 us
  Pallas kernels  24.8 us (39%)
  starting transfers between devices  20.3 us (32%)
  waiting for transfers between devices  14.6 us (23%)
  local copies, waits for them, and re-layouts  3.25 us (5%)
    ppermute x9, starting transfers between devices, exchange(): lax.ppermute(value, axis, [(i, i ^ other) for i in range(lax.axis_size(ax...  12.9 us
    ppermute x9, waiting for transfers between devices, exchange(): lax.ppermute(value, axis, [(i, i ^ other) for i in range(lax.axis_size(ax...  12.7 us
    all_to_all x1, starting transfers between devices, body(): lax.all_to_all(by_residue.reshape(ctx * dp, each, features), ('ctx', 'dp'...  7.42 us
    pallas_call x1, Pallas kernels, dilated_attention(): pl.pallas_call(functools.partial(dilated_kernel, dp, ctx, min(256, count)...  7.24 us
    pallas_call x1, Pallas kernels, local_attention(): pl.pallas_call(functools.partial(local_kernel, dp, ctx, min(256, count)),...  6.48 us
    pallas_call x1, Pallas kernels, embed(): pl.pallas_call(functools.partial(embed_kernel, ctx, steps, int(split)), o...  4.69 us
    pallas_call x2, Pallas kernels, merge_part(): pl.pallas_call(functools.partial(merge_part_kernel, dp, ctx, sends, len(o...  4.35 us
    unnamed x22, local copies, waits for them, and re-layouts  3.24 us
  transfers between devices with their start and end apart: 10, of which 5 were waited for; matrix products, arithmetic and copies ran while one was open for 0% of the time, Pallas kernels for 16%

profile of v7, /device:TPU:0, one launch (start us, length us, event | category | flops | bytes accessed | tf_op | source)
XLA Modules:
  0.0 63.2 jit_solution(8686854784478545917)
XLA Ops:
  0.0 4.7 %embed.1.by_residue = bf16[8,4,16,768]{3,2,1,0:T(8,128)(2,1)} custom-call(bf16[4,1,128,1536]{3,2,1,0:T(8,128)(2,1)} %x_hbm.1, bf16[1536,768]{1,0:T(8,128)(2,1)} %w_hbm.1), custom_call_target="tpu_custom_call" | custom-call | tf_op jit(solution)/shard_map/embed/pallas_call | solution.py:107
  4.7 7.4 %all-to-all-start = ((bf16[32,16,768]{2,1,0:T(8,128)(2,1)}), bf16[32,16,768]{2,1,0:T(8,128)(2,1)}, u32[]{:S(2)}, u32[]{:S(2)}) async-start(bf16[32,16,768]{2,1,0:T(8,128)(2,1)} %bitcast.6), calls=%async_computation | async-start | bytes 1572864 | tf_op jit(solution)/shard_map/all_to_all | solution.py:430
  12.1 1.2 %copy-done = bf16[8,4,16,768]{3,2,1,0:T(8,128)(2,1)S(1)} copy-done((bf16[8,4,16,768]{3,2,1,0:T(8,128)(2,1)S(1)}, bf16[8,4,16,768]{3,2,1,0:T(8,128)(2,1)}, u32[]{:S(2)}) %copy-start) | copy-done | bytes 786456
  13.4 0.3 collective-permute-start
  13.6 1.7 %collective-permute-start.1 = (bf16[8,16,768]{2,1,0:T(8,128)(2,1)S(1)}, bf16[8,16,768]{2,1,0:T(8,128)(2,1)S(1)}, u32[]{:S(2)}, u32[]{:S(2)}) collective-permute-start(bf16[8,16,768]{2,1,0:T(8,128)(2,1)S(1)} %get-tuple-element.30), channel_id=1, source_target_pairs={{0,16},{8,24},{16,0},{24,8},{1,17},{9,25},{17,1},{25,9},{2,18},{10... | collective-permute-start | bytes 589832 | tf_op jit(solution)/shard_map/ppermute | solution.py:412
  15.3 2.0 %fetch.1.weight_ref.refs_4_ = bf16[768,2304]{1,0:T(8,128)(2,1)S(1)} custom-call(bf16[768,2304]{1,0:T(8,128)(2,1)} %source.1, bf16[8,16,768]{2,1,0:T(8,128)(2,1)S(1)} %get-tuple-element.28.after), custom_call_target="tpu_custom_call" | custom-call | bytes 8000000 | tf_op jit(solution)/shard_map/fetch/pallas_call | solution.py:133
  17.4 0.7 %copy-done.5 = bf16[8,16,768]{2,1,0:T(8,128)(2,1)} copy-done((bf16[8,16,768]{2,1,0:T(8,128)(2,1)}, bf16[8,16,768]{2,1,0:T(8,128)(2,1)S(1)}, u32[]{:S(2)}) %copy-start.5) | copy-done | bytes 196632
  18.1 8.6 %collective-permute-done.1 = bf16[8,16,768]{2,1,0:T(8,128)(2,1)S(1)} collective-permute-done((bf16[8,16,768]{2,1,0:T(8,128)(2,1)S(1)}, bf16[8,16,768]{2,1,0:T(8,128)(2,1)S(1)}, u32[]{:S(2)}, u32[]{:S(2)}) %collective-permute-start.1) | collective-permute-done | bytes 196640 | tf_op jit(solution)/shard_map/ppermute | solution.py:412
  26.6 0.7 %copy-done.7 = bf16[8,16,768]{2,1,0:T(8,128)(2,1)} copy-done((bf16[8,16,768]{2,1,0:T(8,128)(2,1)}, bf16[8,16,768]{2,1,0:T(8,128)(2,1)S(1)}, u32[]{:S(2)}) %copy-start.7) | copy-done | bytes 196632
  27.3 2.9 %collective-permute-done.2 = bf16[8,16,768]{2,1,0:T(8,128)(2,1)S(1)} collective-permute-done((bf16[8,16,768]{2,1,0:T(8,128)(2,1)S(1)}, bf16[8,16,768]{2,1,0:T(8,128)(2,1)S(1)}, u32[]{:S(2)}, u32[]{:S(2)}) %collective-permute-start.2) | collective-permute-done | bytes 196640 | tf_op jit(solution)/shard_map/ppermute | solution.py:412
  30.2 0.7 %copy-done.9 = bf16[8,16,768]{2,1,0:T(8,128)(2,1)} copy-done((bf16[8,16,768]{2,1,0:T(8,128)(2,1)}, bf16[8,16,768]{2,1,0:T(8,128)(2,1)S(1)}, u32[]{:S(2)}) %copy-start.9) | copy-done | bytes 196632
  30.9 1.9 %all-to-all-done = bf16[32,16,768]{2,1,0:T(8,128)(2,1)} async-done(((bf16[32,16,768]{2,1,0:T(8,128)(2,1)}), bf16[32,16,768]{2,1,0:T(8,128)(2,1)}, u32[]{:S(2)}, u32[]{:S(2)}) %all-to-all-start) | async-done | bytes 786464 | tf_op jit(solution)/shard_map/all_to_all | solution.py:430
  32.8 7.2 %dilated.1 = (bf16[1,400,128]{2,1,0:T(8,128)(2,1)S(1)}, bf16[1,400,128]{2,1,0:T(8,128)(2,1)S(1)}, bf16[1,400,128]{2,1,0:T(8,128)(2,1)S(1)}, bf16[1,400,128]{2,1,...) custom-call(s32[4]{0:T(128)S(1)} %copy-done.4, ...), custom_call_target="tpu_custom_call" | custom-call | flops 1000000 | bytes 10000 | tf_op jit(solution)/shard_map/dilated/pallas_call | solution.py:279
  40.0 1.5 %collective-permute-start.7 = (bf16[2,400,128]{2,1,0:T(8,128)(2,1)S(1)}, bf16[2,400,128]{2,1,0:T(8,128)(2,1)S(1)}, u32[]{:S(2)}, u32[]{:S(2)}) collective-permute-start(bf16[2,400,128]{2,1,0:T(8,128)(2,1)S(1)} %get-tuple-element.48), channel_id=1, source_target_pairs={{0,2},{1,3},{2,0},{3,1},{4,6},{5,7},{6,4},{7,5},{8,10},{9,11},{10,... | collective-permute-start | bytes 614408 | tf_op jit(solution)/shard_map/ppermute | solution.py:412
  41.4 1.8 %collective-permute-start.3 = (bf16[1,400,128]{2,1,0:T(8,128)(2,1)S(1)}, bf16[1,400,128]{2,1,0:T(8,128)(2,1)S(1)}, u32[]{:S(2)}, u32[]{:S(2)}) collective-permute-start(bf16[1,400,128]{2,1,0:T(8,128)(2,1)S(1)} %get-tuple-element.44), channel_id=1, source_target_pairs={{0,4},{1,5},{2,6},{3,7},{4,0},{5,1},{6,2},{7,3},{8,12},{9,13},{10,... | collective-permute-start | bytes 307208 | tf_op jit(solution)/shard_map/ppermute | solution.py:412
  43.2 1.5 %collective-permute-start.4 = (bf16[1,400,128]{2,1,0:T(8,128)(2,1)S(1)}, bf16[1,400,128]{2,1,0:T(8,128)(2,1)S(1)}, u32[]{:S(2)}, u32[]{:S(2)}) collective-permute-start(bf16[1,400,128]{2,1,0:T(8,128)(2,1)S(1)} %get-tuple-element.45), channel_id=1, source_target_pairs={{0,5},{1,4},{2,7},{3,6},{4,1},{5,0},{6,3},{7,2},{8,13},{9,12},{10,... | collective-permute-start | bytes 307208 | tf_op jit(solution)/shard_map/ppermute | solution.py:412
  44.8 2.2 %collective-permute-start.5 = (bf16[1,400,128]{2,1,0:T(8,128)(2,1)S(1)}, bf16[1,400,128]{2,1,0:T(8,128)(2,1)S(1)}, u32[]{:S(2)}, u32[]{:S(2)}) collective-permute-start(bf16[1,400,128]{2,1,0:T(8,128)(2,1)S(1)} %get-tuple-element.46), channel_id=1, source_target_pairs={{0,6},{1,7},{2,4},{3,5},{4,2},{5,3},{6,0},{7,1},{8,14},{9,15},{10,... | collective-permute-start | bytes 307208 | tf_op jit(solution)/shard_map/ppermute | solution.py:412
  46.9 2.2 %collective-permute-start.6 = (bf16[1,400,128]{2,1,0:T(8,128)(2,1)S(1)}, bf16[1,400,128]{2,1,0:T(8,128)(2,1)S(1)}, u32[]{:S(2)}, u32[]{:S(2)}) collective-permute-start(bf16[1,400,128]{2,1,0:T(8,128)(2,1)S(1)} %get-tuple-element.47), channel_id=1, source_target_pairs={{0,7},{1,6},{2,5},{3,4},{4,3},{5,2},{6,1},{7,0},{8,15},{9,14},{10,... | collective-permute-start | bytes 307208 | tf_op jit(solution)/shard_map/ppermute | solution.py:412
  49.1 1.1 %collective-permute-done.7.refs_0_ = bf16[2,400,128]{2,1,0:T(8,128)(2,1)S(1)} collective-permute-done((bf16[2,400,128]{2,1,0:T(8,128)(2,1)S(1)}, bf16[2,400,128]{2,1,0:T(8,128)(2,1)S(1)}, u32[]{:S(2)}, u32[]{:S(2)}) %collective-permute-start.7) | collective-permute-done | bytes 204832 | tf_op jit(solution)/shard_map/ppermute | solution.py:412
  50.2 1.9 %collective-permute-start.8 = (bf16[2,400,128]{2,1,0:T(8,128)(2,1)S(1)}, bf16[2,400,128]{2,1,0:T(8,128)(2,1)S(1)}, u32[]{:S(2)}, u32[]{:S(2)}) collective-permute-start(bf16[2,400,128]{2,1,0:T(8,128)(2,1)S(1)} %pad_maximum_fusion), channel_id=1, source_target_pairs={{0,1},{1,0},{2,3},{3,2},{4,5},{5,4},{6,7},{7,6},{8,9},{9,8},{10,11... | collective-permute-start | bytes 614408 | tf_op jit(solution)/shard_map/ppermute | solution.py:412
  52.1 6.5 %local.1 = (bf16[512,768]{1,0:T(8,128)(2,1)S(1)}, f32[512,128]{1,0:T(8,128)S(1)}) custom-call(s32[4]{0:T(128)S(1)} %copy-done.4, bf16[128,768]{1,0:T(8,128)(2,1)S(1)} %bitcast.7, bf16[128,768]{1,0:T(8,128)(2,1)S(1)} %bitcast.8, bf16[128,768]{1,0:T(8,128)(2,1)S(1)} %bitcast.9, bf16[128,768]{1,0:T(8,128)(2,1)S(1)} %bitcast.10, ...), custom_call_target="tpu_custom_call" | custom-call | flops 8000000000 | bytes 10000000 | tf_op jit(solution)/shard_map/local/pallas_call | solution.py:216
  58.6 0.2 collective-permute-done.8.refs_2_
  58.8 1.8 %merge.2.refs_4_ = bf16[512,768]{1,0:T(8,128)(2,1)S(1)} custom-call(s32[4]{0:T(128)S(1)} %copy-done.4, bf16[512,768]{1,0:T(8,128)(2,1)S(1)} %get-tuple-element.42.out_ref, f32[512,128]{1,0:T(8,128)S(1)} %get-tuple-element.43.log_ref, bf16[768,768]{1,0:T(8,128)(2,1)S(1)} %copy-done.1, bf16[2,400,128]{2,1,0:T(8,128)(2,1)S(1)} %collective-permute-done.7.refs_0_, ...), custom_call_target="tpu_custom_call" | custom-call | flops 1000000 | bytes 10000 | tf_op jit(solution)/shard_map/merge/pallas_call | solution.py:391
  60.7 2.5 %merge.3 = bf16[1,512,768]{2,1,0:T(8,128)(2,1)} custom-call(s32[4]{0:T(128)S(1)} %copy-done.4, bf16[512,768]{1,0:T(8,128)(2,1)S(1)} %get-tuple-element.42.out_ref, f32[512,128]{1,0:T(8,128)S(1)} %get-tuple-element.43.log_ref, bf16[768,768]{1,0:T(8,128)(2,1)S(1)} %copy-done.1, bf16[1,400,128]{2,1,0:T(8,128)(2,1)S(1)} %collective-permute-done.3.refs_0_, ...), custom_call_target="tpu_custom_call" | custom-call | flops 1000000 | bytes 10000 | tf_op jit(solution)/shard_map/merge/pallas_call | solution.py:391
  (27 shorter events, 0.2 us)
Async XLA Ops:
  4.7 28.0 %all-to-all-start = ((bf16[32,16,768]{2,1,0:T(8,128)(2,1)}), bf16[32,16,768]{2,1,0:T(8,128)(2,1)}, u32[]{:S(2)}, u32[]{:S(2)}) async-start(bf16[32,16,768]{2,1,0:T(8,128)(2,1)} %bitcast.6), calls=%async_computation | async-start | bytes 1572864 | tf_op jit(solution)/shard_map/all_to_all | solution.py:430
  12.1 1.2 %copy-start = (bf16[8,4,16,768]{3,2,1,0:T(8,128)(2,1)S(1)}, bf16[8,4,16,768]{3,2,1,0:T(8,128)(2,1)}, u32[]{:S(2)}) copy-start(bf16[8,4,16,768]{3,2,1,0:T(8,128)(2,1)} %embed.1.by_residue) | copy-start | bytes 2359300
  13.3 4.0 %copy-start.2 = (bf16[8,16,768]{2,1,0:T(8,128)(2,1)}, bf16[8,16,768]{2,1,0:T(8,128)(2,1)S(1)}, u32[]{:S(2)}) copy-start(bf16[8,16,768]{2,1,0:T(8,128)(2,1)S(1)} %get-tuple-element.28.after) | copy-start | bytes 589828
  13.4 4.0 %collective-permute-start = (bf16[8,16,768]{2,1,0:T(8,128)(2,1)S(1)}, bf16[8,16,768]{2,1,0:T(8,128)(2,1)S(1)}, u32[]{:S(2)}, u32[]{:S(2)}) collective-permute-start(bf16[8,16,768]{2,1,0:T(8,128)(2,1)S(1)} %get-tuple-element.29), channel_id=1, source_target_pairs={{0,8},{8,0},{16,24},{24,16},{1,9},{9,1},{17,25},{25,17},{2,10},{10... | collective-permute-start | bytes 589832 | tf_op jit(solution)/shard_map/ppermute | solution.py:412
  13.6 13.0 %collective-permute-start.1 = (bf16[8,16,768]{2,1,0:T(8,128)(2,1)S(1)}, bf16[8,16,768]{2,1,0:T(8,128)(2,1)S(1)}, u32[]{:S(2)}, u32[]{:S(2)}) collective-permute-start(bf16[8,16,768]{2,1,0:T(8,128)(2,1)S(1)} %get-tuple-element.30), channel_id=1, source_target_pairs={{0,16},{8,24},{16,0},{24,8},{1,17},{9,25},{17,1},{25,9},{2,18},{10... | collective-permute-start | bytes 589832 | tf_op jit(solution)/shard_map/ppermute | solution.py:412
  15.3 14.9 %collective-permute-start.2 = (bf16[8,16,768]{2,1,0:T(8,128)(2,1)S(1)}, bf16[8,16,768]{2,1,0:T(8,128)(2,1)S(1)}, u32[]{:S(2)}, u32[]{:S(2)}) collective-permute-start(bf16[8,16,768]{2,1,0:T(8,128)(2,1)S(1)} %get-tuple-element.31), channel_id=1, source_target_pairs={{0,24},{8,16},{16,8},{24,0},{1,25},{9,17},{17,9},{25,1},{2,26},{10... | collective-permute-start | bytes 589832 | tf_op jit(solution)/shard_map/ppermute | solution.py:412
  15.3 17.4 %copy-start.4 = (s32[4]{0:T(128)S(1)}, s32[4]{0:T(128)}, u32[]{:S(2)}) copy-start(s32[4]{0:T(128)} %counts_ref.7) | copy-start | bytes 52
  17.4 0.7 %copy-start.5 = (bf16[8,16,768]{2,1,0:T(8,128)(2,1)}, bf16[8,16,768]{2,1,0:T(8,128)(2,1)S(1)}, u32[]{:S(2)}) copy-start(bf16[8,16,768]{2,1,0:T(8,128)(2,1)S(1)} %collective-permute-done) | copy-start | bytes 589828
  26.6 0.7 %copy-start.7 = (bf16[8,16,768]{2,1,0:T(8,128)(2,1)}, bf16[8,16,768]{2,1,0:T(8,128)(2,1)S(1)}, u32[]{:S(2)}) copy-start(bf16[8,16,768]{2,1,0:T(8,128)(2,1)S(1)} %collective-permute-done.1) | copy-start | bytes 589828
  30.2 0.7 %copy-start.9 = (bf16[8,16,768]{2,1,0:T(8,128)(2,1)}, bf16[8,16,768]{2,1,0:T(8,128)(2,1)S(1)}, u32[]{:S(2)}) copy-start(bf16[8,16,768]{2,1,0:T(8,128)(2,1)S(1)} %collective-permute-done.2) | copy-start | bytes 589828
  32.7 19.4 %copy-start.3 = (bf16[8,16,768]{2,1,0:T(8,128)(2,1)S(1)}, bf16[8,16,768]{2,1,0:T(8,128)(2,1)}, u32[]{:S(2)}) copy-start(bf16[8,16,768]{2,1,0:T(8,128)(2,1)} %copy-done.2) | copy-start | bytes 589828
  32.7 19.4 %copy-start.6 = (bf16[8,16,768]{2,1,0:T(8,128)(2,1)S(1)}, bf16[8,16,768]{2,1,0:T(8,128)(2,1)}, u32[]{:S(2)}) copy-start(bf16[8,16,768]{2,1,0:T(8,128)(2,1)} %copy-done.5) | copy-start | bytes 589828
  32.7 19.4 %copy-start.8 = (bf16[8,16,768]{2,1,0:T(8,128)(2,1)S(1)}, bf16[8,16,768]{2,1,0:T(8,128)(2,1)}, u32[]{:S(2)}) copy-start(bf16[8,16,768]{2,1,0:T(8,128)(2,1)} %copy-done.7) | copy-start | bytes 589828
  32.7 19.4 %copy-start.10 = (bf16[8,16,768]{2,1,0:T(8,128)(2,1)S(1)}, bf16[8,16,768]{2,1,0:T(8,128)(2,1)}, u32[]{:S(2)}) copy-start(bf16[8,16,768]{2,1,0:T(8,128)(2,1)} %copy-done.9) | copy-start | bytes 589828
  40.0 10.2 %collective-permute-start.7 = (bf16[2,400,128]{2,1,0:T(8,128)(2,1)S(1)}, bf16[2,400,128]{2,1,0:T(8,128)(2,1)S(1)}, u32[]{:S(2)}, u32[]{:S(2)}) collective-permute-start(bf16[2,400,128]{2,1,0:T(8,128)(2,1)S(1)} %get-tuple-element.48), channel_id=1, source_target_pairs={{0,2},{1,3},{2,0},{3,1},{4,6},{5,7},{6,4},{7,5},{8,10},{9,11},{10,... | collective-permute-start | bytes 614408 | tf_op jit(solution)/shard_map/ppermute | solution.py:412
  41.4 19.2 %collective-permute-start.3 = (bf16[1,400,128]{2,1,0:T(8,128)(2,1)S(1)}, bf16[1,400,128]{2,1,0:T(8,128)(2,1)S(1)}, u32[]{:S(2)}, u32[]{:S(2)}) collective-permute-start(bf16[1,400,128]{2,1,0:T(8,128)(2,1)S(1)} %get-tuple-element.44), channel_id=1, source_target_pairs={{0,4},{1,5},{2,6},{3,7},{4,0},{5,1},{6,2},{7,3},{8,12},{9,13},{10,... | collective-permute-start | bytes 307208 | tf_op jit(solution)/shard_map/ppermute | solution.py:412
  43.2 17.4 %collective-permute-start.4 = (bf16[1,400,128]{2,1,0:T(8,128)(2,1)S(1)}, bf16[1,400,128]{2,1,0:T(8,128)(2,1)S(1)}, u32[]{:S(2)}, u32[]{:S(2)}) collective-permute-start(bf16[1,400,128]{2,1,0:T(8,128)(2,1)S(1)} %get-tuple-element.45), channel_id=1, source_target_pairs={{0,5},{1,4},{2,7},{3,6},{4,1},{5,0},{6,3},{7,2},{8,13},{9,12},{10,... | collective-permute-start | bytes 307208 | tf_op jit(solution)/shard_map/ppermute | solution.py:412
  44.8 15.9 %collective-permute-start.5 = (bf16[1,400,128]{2,1,0:T(8,128)(2,1)S(1)}, bf16[1,400,128]{2,1,0:T(8,128)(2,1)S(1)}, u32[]{:S(2)}, u32[]{:S(2)}) collective-permute-start(bf16[1,400,128]{2,1,0:T(8,128)(2,1)S(1)} %get-tuple-element.46), channel_id=1, source_target_pairs={{0,6},{1,7},{2,4},{3,5},{4,2},{5,3},{6,0},{7,1},{8,14},{9,15},{10,... | collective-permute-start | bytes 307208 | tf_op jit(solution)/shard_map/ppermute | solution.py:412
  46.9 13.7 %collective-permute-start.6 = (bf16[1,400,128]{2,1,0:T(8,128)(2,1)S(1)}, bf16[1,400,128]{2,1,0:T(8,128)(2,1)S(1)}, u32[]{:S(2)}, u32[]{:S(2)}) collective-permute-start(bf16[1,400,128]{2,1,0:T(8,128)(2,1)S(1)} %get-tuple-element.47), channel_id=1, source_target_pairs={{0,7},{1,6},{2,5},{3,4},{4,3},{5,2},{6,1},{7,0},{8,15},{9,14},{10,... | collective-permute-start | bytes 307208 | tf_op jit(solution)/shard_map/ppermute | solution.py:412
  50.2 8.6 %copy-start.1 = (bf16[768,768]{1,0:T(8,128)(2,1)S(1)}, bf16[768,768]{1,0:T(8,128)(2,1)}, u32[]{:S(2)}) copy-start(bf16[768,768]{1,0:T(8,128)(2,1)} %weight_ref.3) | copy-start | bytes 3538948
  50.2 8.6 %collective-permute-start.8 = (bf16[2,400,128]{2,1,0:T(8,128)(2,1)S(1)}, bf16[2,400,128]{2,1,0:T(8,128)(2,1)S(1)}, u32[]{:S(2)}, u32[]{:S(2)}) collective-permute-start(bf16[2,400,128]{2,1,0:T(8,128)(2,1)S(1)} %pad_maximum_fusion), channel_id=1, source_target_pairs={{0,1},{1,0},{2,3},{3,2},{4,5},{5,4},{6,7},{7,6},{8,9},{9,8},{10,11... | collective-permute-start | bytes 614408 | tf_op jit(solution)/shard_map/ppermute | solution.py:412

commit v8 on v7

--- a/solution.py
+++ b/solution.py
@@ -291,16 +291,16 @@
 def merge_rows(own, own_logs, features_of, logs, heads, weight):
     lane = iota((1, 128), 1)
     share = jnp.where(lane < HEAD_TOTAL, 1.0 / (1.0 + jnp.exp2(own_logs - logs)), 0.0)
-    high = share.astype(BF16)
-    low = (share - high.astype(F32)).astype(BF16)
-    wide = dot(high, heads) + dot(low, heads)
+    high = share.astype(BF16).astype(F32)
+    wide = dot((high + pltpu.roll(share - high, 16, 1)).astype(BF16), heads)
     own = own.astype(F32)
     merged = own + wide * (features_of.astype(F32) - own)
     return dot(merged.astype(BF16), weight)
 
 
 def heads_of(features):
-    return (iota((128, features), 0) == iota((128, features), 1) // (features // HEAD_TOTAL)).astype(BF16)
+    lane = iota((128, features), 0)
+    return ((lane % 16 == iota((128, features), 1) // (features // HEAD_TOTAL)) & (lane < 32)).astype(BF16)
 
 
 def merge_kernel(dp, ctx, counts_ref, out_ref, log_ref, weight_ref, dilated, mixed_ref):

time: 63.5 us -> 63.6 us (level)
  no operation moved by 1% of the time
where the time goes in v8:
time: 63.6 us; the launch traced here: 63.4 us
  Pallas kernels  25 us (39%)
  starting transfers between devices  20.3 us (32%)
  waiting for transfers between devices  14.6 us (23%)
  local copies, waits for them, and re-layouts  3.25 us (5%)
    ppermute x9, starting transfers between devices, exchange(): lax.ppermute(value, axis, [(i, i ^ other) for i in range(lax.axis_size(ax...  12.9 us
    ppermute x9, waiting for transfers between devices, exchange(): lax.ppermute(value, axis, [(i, i ^ other) for i in range(lax.axis_size(ax...  12.7 us
    all_to_all x1, starting transfers between devices, body(): lax.all_to_all(by_residue.reshape(ctx * dp, each, features), ('ctx', 'dp'...  7.42 us
    pallas_call x1, Pallas kernels, dilated_attention(): pl.pallas_call(functools.partial(dilated_kernel, dp, ctx, min(256, count)...  7.24 us
    pallas_call x1, Pallas kernels, local_attention(): pl.pallas_call(functools.partial(local_kernel, dp, ctx, min(256, count)),...  6.48 us
    pallas_call x1, Pallas kernels, embed(): pl.pallas_call(functools.partial(embed_kernel, ctx, steps, int(split)), o...  4.69 us
    pallas_call x2, Pallas kernels, merge_part(): pl.pallas_call(functools.partial(merge_part_kernel, dp, ctx, sends, len(o...  4.51 us
    unnamed x22, local copies, waits for them, and re-layouts  3.24 us
  transfers between devices with their start and end apart: 10, of which 5 were waited for; matrix products, arithmetic and copies ran while one was open for 0% of the time, Pallas kernels for 16%

profile of v8, /device:TPU:0, one launch (start us, length us, event | category | flops | bytes accessed | tf_op | source)
XLA Modules:
  0.0 63.4 jit_solution(1979191522053524006)
XLA Ops:
  0.0 4.7 %embed.1.by_residue = bf16[8,4,16,768]{3,2,1,0:T(8,128)(2,1)} custom-call(bf16[4,1,128,1536]{3,2,1,0:T(8,128)(2,1)} %x_hbm.1, bf16[1536,768]{1,0:T(8,128)(2,1)} %w_hbm.1), custom_call_target="tpu_custom_call" | custom-call | tf_op jit(solution)/shard_map/embed/pallas_call | solution.py:107
  4.7 7.4 %all-to-all-start = ((bf16[32,16,768]{2,1,0:T(8,128)(2,1)}), bf16[32,16,768]{2,1,0:T(8,128)(2,1)}, u32[]{:S(2)}, u32[]{:S(2)}) async-start(bf16[32,16,768]{2,1,0:T(8,128)(2,1)} %bitcast.6), calls=%async_computation | async-start | bytes 1572864 | tf_op jit(solution)/shard_map/all_to_all | solution.py:430
  12.1 1.2 %copy-done = bf16[8,4,16,768]{3,2,1,0:T(8,128)(2,1)S(1)} copy-done((bf16[8,4,16,768]{3,2,1,0:T(8,128)(2,1)S(1)}, bf16[8,4,16,768]{3,2,1,0:T(8,128)(2,1)}, u32[]{:S(2)}) %copy-start) | copy-done | bytes 786456
  13.4 0.3 collective-permute-start
  13.6 1.7 %collective-permute-start.1 = (bf16[8,16,768]{2,1,0:T(8,128)(2,1)S(1)}, bf16[8,16,768]{2,1,0:T(8,128)(2,1)S(1)}, u32[]{:S(2)}, u32[]{:S(2)}) collective-permute-start(bf16[8,16,768]{2,1,0:T(8,128)(2,1)S(1)} %get-tuple-element.30), channel_id=1, source_target_pairs={{0,16},{8,24},{16,0},{24,8},{1,17},{9,25},{17,1},{25,9},{2,18},{10... | collective-permute-start | bytes 589832 | tf_op jit(solution)/shard_map/ppermute | solution.py:412
  15.3 2.0 %fetch.1.weight_ref.refs_4_ = bf16[768,2304]{1,0:T(8,128)(2,1)S(1)} custom-call(bf16[768,2304]{1,0:T(8,128)(2,1)} %source.1, bf16[8,16,768]{2,1,0:T(8,128)(2,1)S(1)} %get-tuple-element.28.after), custom_call_target="tpu_custom_call" | custom-call | bytes 8000000 | tf_op jit(solution)/shard_map/fetch/pallas_call | solution.py:133
  17.4 0.7 %copy-done.5 = bf16[8,16,768]{2,1,0:T(8,128)(2,1)} copy-done((bf16[8,16,768]{2,1,0:T(8,128)(2,1)}, bf16[8,16,768]{2,1,0:T(8,128)(2,1)S(1)}, u32[]{:S(2)}) %copy-start.5) | copy-done | bytes 196632
  18.1 8.6 %collective-permute-done.1 = bf16[8,16,768]{2,1,0:T(8,128)(2,1)S(1)} collective-permute-done((bf16[8,16,768]{2,1,0:T(8,128)(2,1)S(1)}, bf16[8,16,768]{2,1,0:T(8,128)(2,1)S(1)}, u32[]{:S(2)}, u32[]{:S(2)}) %collective-permute-start.1) | collective-permute-done | bytes 196640 | tf_op jit(solution)/shard_map/ppermute | solution.py:412
  26.6 0.7 %copy-done.7 = bf16[8,16,768]{2,1,0:T(8,128)(2,1)} copy-done((bf16[8,16,768]{2,1,0:T(8,128)(2,1)}, bf16[8,16,768]{2,1,0:T(8,128)(2,1)S(1)}, u32[]{:S(2)}) %copy-start.7) | copy-done | bytes 196632
  27.3 2.9 %collective-permute-done.2 = bf16[8,16,768]{2,1,0:T(8,128)(2,1)S(1)} collective-permute-done((bf16[8,16,768]{2,1,0:T(8,128)(2,1)S(1)}, bf16[8,16,768]{2,1,0:T(8,128)(2,1)S(1)}, u32[]{:S(2)}, u32[]{:S(2)}) %collective-permute-start.2) | collective-permute-done | bytes 196640 | tf_op jit(solution)/shard_map/ppermute | solution.py:412
  30.2 0.7 %copy-done.9 = bf16[8,16,768]{2,1,0:T(8,128)(2,1)} copy-done((bf16[8,16,768]{2,1,0:T(8,128)(2,1)}, bf16[8,16,768]{2,1,0:T(8,128)(2,1)S(1)}, u32[]{:S(2)}) %copy-start.9) | copy-done | bytes 196632
  30.9 1.9 %all-to-all-done = bf16[32,16,768]{2,1,0:T(8,128)(2,1)} async-done(((bf16[32,16,768]{2,1,0:T(8,128)(2,1)}), bf16[32,16,768]{2,1,0:T(8,128)(2,1)}, u32[]{:S(2)}, u32[]{:S(2)}) %all-to-all-start) | async-done | bytes 786464 | tf_op jit(solution)/shard_map/all_to_all | solution.py:430
  32.8 7.2 %dilated.1 = (bf16[1,400,128]{2,1,0:T(8,128)(2,1)S(1)}, bf16[1,400,128]{2,1,0:T(8,128)(2,1)S(1)}, bf16[1,400,128]{2,1,0:T(8,128)(2,1)S(1)}, bf16[1,400,128]{2,1,...) custom-call(s32[4]{0:T(128)S(1)} %copy-done.4, ...), custom_call_target="tpu_custom_call" | custom-call | flops 1000000 | bytes 10000 | tf_op jit(solution)/shard_map/dilated/pallas_call | solution.py:279
  40.0 1.5 %collective-permute-start.7 = (bf16[2,400,128]{2,1,0:T(8,128)(2,1)S(1)}, bf16[2,400,128]{2,1,0:T(8,128)(2,1)S(1)}, u32[]{:S(2)}, u32[]{:S(2)}) collective-permute-start(bf16[2,400,128]{2,1,0:T(8,128)(2,1)S(1)} %get-tuple-element.48), channel_id=1, source_target_pairs={{0,2},{1,3},{2,0},{3,1},{4,6},{5,7},{6,4},{7,5},{8,10},{9,11},{10,... | collective-permute-start | bytes 614408 | tf_op jit(solution)/shard_map/ppermute | solution.py:412
  41.4 1.8 %collective-permute-start.3 = (bf16[1,400,128]{2,1,0:T(8,128)(2,1)S(1)}, bf16[1,400,128]{2,1,0:T(8,128)(2,1)S(1)}, u32[]{:S(2)}, u32[]{:S(2)}) collective-permute-start(bf16[1,400,128]{2,1,0:T(8,128)(2,1)S(1)} %get-tuple-element.44), channel_id=1, source_target_pairs={{0,4},{1,5},{2,6},{3,7},{4,0},{5,1},{6,2},{7,3},{8,12},{9,13},{10,... | collective-permute-start | bytes 307208 | tf_op jit(solution)/shard_map/ppermute | solution.py:412
  43.2 1.5 %collective-permute-start.4 = (bf16[1,400,128]{2,1,0:T(8,128)(2,1)S(1)}, bf16[1,400,128]{2,1,0:T(8,128)(2,1)S(1)}, u32[]{:S(2)}, u32[]{:S(2)}) collective-permute-start(bf16[1,400,128]{2,1,0:T(8,128)(2,1)S(1)} %get-tuple-element.45), channel_id=1, source_target_pairs={{0,5},{1,4},{2,7},{3,6},{4,1},{5,0},{6,3},{7,2},{8,13},{9,12},{10,... | collective-permute-start | bytes 307208 | tf_op jit(solution)/shard_map/ppermute | solution.py:412
  44.8 2.2 %collective-permute-start.5 = (bf16[1,400,128]{2,1,0:T(8,128)(2,1)S(1)}, bf16[1,400,128]{2,1,0:T(8,128)(2,1)S(1)}, u32[]{:S(2)}, u32[]{:S(2)}) collective-permute-start(bf16[1,400,128]{2,1,0:T(8,128)(2,1)S(1)} %get-tuple-element.46), channel_id=1, source_target_pairs={{0,6},{1,7},{2,4},{3,5},{4,2},{5,3},{6,0},{7,1},{8,14},{9,15},{10,... | collective-permute-start | bytes 307208 | tf_op jit(solution)/shard_map/ppermute | solution.py:412
  46.9 2.2 %collective-permute-start.6 = (bf16[1,400,128]{2,1,0:T(8,128)(2,1)S(1)}, bf16[1,400,128]{2,1,0:T(8,128)(2,1)S(1)}, u32[]{:S(2)}, u32[]{:S(2)}) collective-permute-start(bf16[1,400,128]{2,1,0:T(8,128)(2,1)S(1)} %get-tuple-element.47), channel_id=1, source_target_pairs={{0,7},{1,6},{2,5},{3,4},{4,3},{5,2},{6,1},{7,0},{8,15},{9,14},{10,... | collective-permute-start | bytes 307208 | tf_op jit(solution)/shard_map/ppermute | solution.py:412
  49.1 1.1 %collective-permute-done.7.refs_0_ = bf16[2,400,128]{2,1,0:T(8,128)(2,1)S(1)} collective-permute-done((bf16[2,400,128]{2,1,0:T(8,128)(2,1)S(1)}, bf16[2,400,128]{2,1,0:T(8,128)(2,1)S(1)}, u32[]{:S(2)}, u32[]{:S(2)}) %collective-permute-start.7) | collective-permute-done | bytes 204832 | tf_op jit(solution)/shard_map/ppermute | solution.py:412
  50.2 1.9 %collective-permute-start.8 = (bf16[2,400,128]{2,1,0:T(8,128)(2,1)S(1)}, bf16[2,400,128]{2,1,0:T(8,128)(2,1)S(1)}, u32[]{:S(2)}, u32[]{:S(2)}) collective-permute-start(bf16[2,400,128]{2,1,0:T(8,128)(2,1)S(1)} %pad_maximum_fusion), channel_id=1, source_target_pairs={{0,1},{1,0},{2,3},{3,2},{4,5},{5,4},{6,7},{7,6},{8,9},{9,8},{10,11... | collective-permute-start | bytes 614408 | tf_op jit(solution)/shard_map/ppermute | solution.py:412
  52.1 6.5 %local.1 = (bf16[512,768]{1,0:T(8,128)(2,1)S(1)}, f32[512,128]{1,0:T(8,128)S(1)}) custom-call(s32[4]{0:T(128)S(1)} %copy-done.4, bf16[128,768]{1,0:T(8,128)(2,1)S(1)} %bitcast.7, bf16[128,768]{1,0:T(8,128)(2,1)S(1)} %bitcast.8, bf16[128,768]{1,0:T(8,128)(2,1)S(1)} %bitcast.9, bf16[128,768]{1,0:T(8,128)(2,1)S(1)} %bitcast.10, ...), custom_call_target="tpu_custom_call" | custom-call | flops 8000000000 | bytes 10000000 | tf_op jit(solution)/shard_map/local/pallas_call | solution.py:216
  58.6 0.2 collective-permute-done.8.refs_2_
  58.8 1.9 %merge.2.refs_4_ = bf16[512,768]{1,0:T(8,128)(2,1)S(1)} custom-call(s32[4]{0:T(128)S(1)} %copy-done.4, bf16[512,768]{1,0:T(8,128)(2,1)S(1)} %get-tuple-element.42.out_ref, f32[512,128]{1,0:T(8,128)S(1)} %get-tuple-element.43.log_ref, bf16[768,768]{1,0:T(8,128)(2,1)S(1)} %copy-done.1, bf16[2,400,128]{2,1,0:T(8,128)(2,1)S(1)} %collective-permute-done.7.refs_0_, ...), custom_call_target="tpu_custom_call" | custom-call | flops 1000000 | bytes 10000 | tf_op jit(solution)/shard_map/merge/pallas_call | solution.py:391
  60.8 2.6 %merge.3 = bf16[1,512,768]{2,1,0:T(8,128)(2,1)} custom-call(s32[4]{0:T(128)S(1)} %copy-done.4, bf16[512,768]{1,0:T(8,128)(2,1)S(1)} %get-tuple-element.42.out_ref, f32[512,128]{1,0:T(8,128)S(1)} %get-tuple-element.43.log_ref, bf16[768,768]{1,0:T(8,128)(2,1)S(1)} %copy-done.1, bf16[1,400,128]{2,1,0:T(8,128)(2,1)S(1)} %collective-permute-done.3.refs_0_, ...), custom_call_target="tpu_custom_call" | custom-call | flops 1000000 | bytes 10000 | tf_op jit(solution)/shard_map/merge/pallas_call | solution.py:391
  (27 shorter events, 0.2 us)
Async XLA Ops:
  4.7 28.0 %all-to-all-start = ((bf16[32,16,768]{2,1,0:T(8,128)(2,1)}), bf16[32,16,768]{2,1,0:T(8,128)(2,1)}, u32[]{:S(2)}, u32[]{:S(2)}) async-start(bf16[32,16,768]{2,1,0:T(8,128)(2,1)} %bitcast.6), calls=%async_computation | async-start | bytes 1572864 | tf_op jit(solution)/shard_map/all_to_all | solution.py:430
  12.1 1.2 %copy-start = (bf16[8,4,16,768]{3,2,1,0:T(8,128)(2,1)S(1)}, bf16[8,4,16,768]{3,2,1,0:T(8,128)(2,1)}, u32[]{:S(2)}) copy-start(bf16[8,4,16,768]{3,2,1,0:T(8,128)(2,1)} %embed.1.by_residue) | copy-start | bytes 2359300
  13.3 4.0 %copy-start.2 = (bf16[8,16,768]{2,1,0:T(8,128)(2,1)}, bf16[8,16,768]{2,1,0:T(8,128)(2,1)S(1)}, u32[]{:S(2)}) copy-start(bf16[8,16,768]{2,1,0:T(8,128)(2,1)S(1)} %get-tuple-element.28.after) | copy-start | bytes 589828
  13.4 4.0 %collective-permute-start = (bf16[8,16,768]{2,1,0:T(8,128)(2,1)S(1)}, bf16[8,16,768]{2,1,0:T(8,128)(2,1)S(1)}, u32[]{:S(2)}, u32[]{:S(2)}) collective-permute-start(bf16[8,16,768]{2,1,0:T(8,128)(2,1)S(1)} %get-tuple-element.29), channel_id=1, source_target_pairs={{0,8},{8,0},{16,24},{24,16},{1,9},{9,1},{17,25},{25,17},{2,10},{10... | collective-permute-start | bytes 589832 | tf_op jit(solution)/shard_map/ppermute | solution.py:412
  13.6 13.0 %collective-permute-start.1 = (bf16[8,16,768]{2,1,0:T(8,128)(2,1)S(1)}, bf16[8,16,768]{2,1,0:T(8,128)(2,1)S(1)}, u32[]{:S(2)}, u32[]{:S(2)}) collective-permute-start(bf16[8,16,768]{2,1,0:T(8,128)(2,1)S(1)} %get-tuple-element.30), channel_id=1, source_target_pairs={{0,16},{8,24},{16,0},{24,8},{1,17},{9,25},{17,1},{25,9},{2,18},{10... | collective-permute-start | bytes 589832 | tf_op jit(solution)/shard_map/ppermute | solution.py:412
  15.3 14.9 %collective-permute-start.2 = (bf16[8,16,768]{2,1,0:T(8,128)(2,1)S(1)}, bf16[8,16,768]{2,1,0:T(8,128)(2,1)S(1)}, u32[]{:S(2)}, u32[]{:S(2)}) collective-permute-start(bf16[8,16,768]{2,1,0:T(8,128)(2,1)S(1)} %get-tuple-element.31), channel_id=1, source_target_pairs={{0,24},{8,16},{16,8},{24,0},{1,25},{9,17},{17,9},{25,1},{2,26},{10... | collective-permute-start | bytes 589832 | tf_op jit(solution)/shard_map/ppermute | solution.py:412
  15.3 17.4 %copy-start.4 = (s32[4]{0:T(128)S(1)}, s32[4]{0:T(128)}, u32[]{:S(2)}) copy-start(s32[4]{0:T(128)} %counts_ref.7) | copy-start | bytes 52
  17.4 0.7 %copy-start.5 = (bf16[8,16,768]{2,1,0:T(8,128)(2,1)}, bf16[8,16,768]{2,1,0:T(8,128)(2,1)S(1)}, u32[]{:S(2)}) copy-start(bf16[8,16,768]{2,1,0:T(8,128)(2,1)S(1)} %collective-permute-done) | copy-start | bytes 589828
  26.6 0.7 %copy-start.7 = (bf16[8,16,768]{2,1,0:T(8,128)(2,1)}, bf16[8,16,768]{2,1,0:T(8,128)(2,1)S(1)}, u32[]{:S(2)}) copy-start(bf16[8,16,768]{2,1,0:T(8,128)(2,1)S(1)} %collective-permute-done.1) | copy-start | bytes 589828
  30.2 0.7 %copy-start.9 = (bf16[8,16,768]{2,1,0:T(8,128)(2,1)}, bf16[8,16,768]{2,1,0:T(8,128)(2,1)S(1)}, u32[]{:S(2)}) copy-start(bf16[8,16,768]{2,1,0:T(8,128)(2,1)S(1)} %collective-permute-done.2) | copy-start | bytes 589828
  32.7 19.4 %copy-start.3 = (bf16[8,16,768]{2,1,0:T(8,128)(2,1)S(1)}, bf16[8,16,768]{2,1,0:T(8,128)(2,1)}, u32[]{:S(2)}) copy-start(bf16[8,16,768]{2,1,0:T(8,128)(2,1)} %copy-done.2) | copy-start | bytes 589828
  32.7 19.4 %copy-start.6 = (bf16[8,16,768]{2,1,0:T(8,128)(2,1)S(1)}, bf16[8,16,768]{2,1,0:T(8,128)(2,1)}, u32[]{:S(2)}) copy-start(bf16[8,16,768]{2,1,0:T(8,128)(2,1)} %copy-done.5) | copy-start | bytes 589828
  32.7 19.4 %copy-start.8 = (bf16[8,16,768]{2,1,0:T(8,128)(2,1)S(1)}, bf16[8,16,768]{2,1,0:T(8,128)(2,1)}, u32[]{:S(2)}) copy-start(bf16[8,16,768]{2,1,0:T(8,128)(2,1)} %copy-done.7) | copy-start | bytes 589828
  32.7 19.4 %copy-start.10 = (bf16[8,16,768]{2,1,0:T(8,128)(2,1)S(1)}, bf16[8,16,768]{2,1,0:T(8,128)(2,1)}, u32[]{:S(2)}) copy-start(bf16[8,16,768]{2,1,0:T(8,128)(2,1)} %copy-done.9) | copy-start | bytes 589828
  40.0 10.2 %collective-permute-start.7 = (bf16[2,400,128]{2,1,0:T(8,128)(2,1)S(1)}, bf16[2,400,128]{2,1,0:T(8,128)(2,1)S(1)}, u32[]{:S(2)}, u32[]{:S(2)}) collective-permute-start(bf16[2,400,128]{2,1,0:T(8,128)(2,1)S(1)} %get-tuple-element.48), channel_id=1, source_target_pairs={{0,2},{1,3},{2,0},{3,1},{4,6},{5,7},{6,4},{7,5},{8,10},{9,11},{10,... | collective-permute-start | bytes 614408 | tf_op jit(solution)/shard_map/ppermute | solution.py:412
  41.4 19.3 %collective-permute-start.3 = (bf16[1,400,128]{2,1,0:T(8,128)(2,1)S(1)}, bf16[1,400,128]{2,1,0:T(8,128)(2,1)S(1)}, u32[]{:S(2)}, u32[]{:S(2)}) collective-permute-start(bf16[1,400,128]{2,1,0:T(8,128)(2,1)S(1)} %get-tuple-element.44), channel_id=1, source_target_pairs={{0,4},{1,5},{2,6},{3,7},{4,0},{5,1},{6,2},{7,3},{8,12},{9,13},{10,... | collective-permute-start | bytes 307208 | tf_op jit(solution)/shard_map/ppermute | solution.py:412
  43.2 17.5 %collective-permute-start.4 = (bf16[1,400,128]{2,1,0:T(8,128)(2,1)S(1)}, bf16[1,400,128]{2,1,0:T(8,128)(2,1)S(1)}, u32[]{:S(2)}, u32[]{:S(2)}) collective-permute-start(bf16[1,400,128]{2,1,0:T(8,128)(2,1)S(1)} %get-tuple-element.45), channel_id=1, source_target_pairs={{0,5},{1,4},{2,7},{3,6},{4,1},{5,0},{6,3},{7,2},{8,13},{9,12},{10,... | collective-permute-start | bytes 307208 | tf_op jit(solution)/shard_map/ppermute | solution.py:412
  44.8 16.0 %collective-permute-start.5 = (bf16[1,400,128]{2,1,0:T(8,128)(2,1)S(1)}, bf16[1,400,128]{2,1,0:T(8,128)(2,1)S(1)}, u32[]{:S(2)}, u32[]{:S(2)}) collective-permute-start(bf16[1,400,128]{2,1,0:T(8,128)(2,1)S(1)} %get-tuple-element.46), channel_id=1, source_target_pairs={{0,6},{1,7},{2,4},{3,5},{4,2},{5,3},{6,0},{7,1},{8,14},{9,15},{10,... | collective-permute-start | bytes 307208 | tf_op jit(solution)/shard_map/ppermute | solution.py:412
  46.9 13.8 %collective-permute-start.6 = (bf16[1,400,128]{2,1,0:T(8,128)(2,1)S(1)}, bf16[1,400,128]{2,1,0:T(8,128)(2,1)S(1)}, u32[]{:S(2)}, u32[]{:S(2)}) collective-permute-start(bf16[1,400,128]{2,1,0:T(8,128)(2,1)S(1)} %get-tuple-element.47), channel_id=1, source_target_pairs={{0,7},{1,6},{2,5},{3,4},{4,3},{5,2},{6,1},{7,0},{8,15},{9,14},{10,... | collective-permute-start | bytes 307208 | tf_op jit(solution)/shard_map/ppermute | solution.py:412
  50.2 8.6 %copy-start.1 = (bf16[768,768]{1,0:T(8,128)(2,1)S(1)}, bf16[768,768]{1,0:T(8,128)(2,1)}, u32[]{:S(2)}) copy-start(bf16[768,768]{1,0:T(8,128)(2,1)} %weight_ref.3) | copy-start | bytes 3538948
  50.2 8.6 %collective-permute-start.8 = (bf16[2,400,128]{2,1,0:T(8,128)(2,1)S(1)}, bf16[2,400,128]{2,1,0:T(8,128)(2,1)S(1)}, u32[]{:S(2)}, u32[]{:S(2)}) collective-permute-start(bf16[2,400,128]{2,1,0:T(8,128)(2,1)S(1)} %pad_maximum_fusion), channel_id=1, source_target_pairs={{0,1},{1,0},{2,3},{3,2},{4,5},{5,4},{6,7},{7,6},{8,9},{9,8},{10,11... | collective-permute-start | bytes 614408 | tf_op jit(solution)/shard_map/ppermute | solution.py:412

commit v9 on v7

--- a/solution.py
+++ b/solution.py
@@ -435,7 +435,7 @@
     portion = count // ctx
     if aligned:
         if ctx == 8:
-            far, sends = ((4,), (5,), (6,), (7,)), ((2, 3), (1,), (0,))
+            far, sends = ((5,), (4,), (7,), (6,)), ((2, 3), (1,), (0,))
             *across, two_three, one, own = dilated_attention(tile_counts, regrouped, w_near, dp, ctx, far + sends)
             across = [exchange(piece, "ctx", other) for piece, (other,) in zip(across, far)]
             two_three = exchange(two_three, "ctx", 2)

time: 63.5 us -> 63.5 us (level)
  waiting for transfers between devices: 14.6 us -> 13.9 us
    ppermute x9, waiting for transfers between devices: 12.7 us -> 12 us  [exchange(): lax.ppermute(value, axis, [(i, i ^ other) for i in range(lax.axis_size(ax...]
  transfers between devices with their start and end apart: 10 -> 10, of which waited for: 5 -> 4; matrix products, arithmetic and copies ran while one was open for 0% -> 0% of each run, Pallas kernels for 16% -> 16%
where the time goes in v9:
time: 63.5 us; the launch traced here: 63.1 us
  Pallas kernels  24.8 us (39%)
  starting transfers between devices  20.9 us (33%)
  waiting for transfers between devices  13.9 us (22%)
  local copies, waits for them, and re-layouts  3.25 us (5%)
    ppermute x9, starting transfers between devices, exchange(): lax.ppermute(value, axis, [(i, i ^ other) for i in range(lax.axis_size(ax...  13.4 us
    ppermute x9, waiting for transfers between devices, exchange(): lax.ppermute(value, axis, [(i, i ^ other) for i in range(lax.axis_size(ax...  12 us
    all_to_all x1, starting transfers between devices, body(): lax.all_to_all(by_residue.reshape(ctx * dp, each, features), ('ctx', 'dp'...  7.42 us
    pallas_call x1, Pallas kernels, dilated_attention(): pl.pallas_call(functools.partial(dilated_kernel, dp, ctx, min(256, count)...  7.24 us
    pallas_call x1, Pallas kernels, local_attention(): pl.pallas_call(functools.partial(local_kernel, dp, ctx, min(256, count)),...  6.48 us
    pallas_call x1, Pallas kernels, embed(): pl.pallas_call(functools.partial(embed_kernel, ctx, steps, int(split)), o...  4.69 us
    pallas_call x2, Pallas kernels, merge_part(): pl.pallas_call(functools.partial(merge_part_kernel, dp, ctx, sends, len(o...  4.35 us
    unnamed x22, local copies, waits for them, and re-layouts  3.24 us
  transfers between devices with their start and end apart: 10, of which 4 were waited for; matrix products, arithmetic and copies ran while one was open for 0% of the time, Pallas kernels for 16%

profile of v9, /device:TPU:0, one launch (start us, length us, event | category | flops | bytes accessed | tf_op | source)
XLA Modules:
  0.0 63.1 jit_solution(10115192957182914304)
XLA Ops:
  0.0 4.7 %embed.1.by_residue = bf16[8,4,16,768]{3,2,1,0:T(8,128)(2,1)} custom-call(bf16[4,1,128,1536]{3,2,1,0:T(8,128)(2,1)} %x_hbm.1, bf16[1536,768]{1,0:T(8,128)(2,1)} %w_hbm.1), custom_call_target="tpu_custom_call" | custom-call | tf_op jit(solution)/shard_map/embed/pallas_call | solution.py:107
  4.7 7.4 %all-to-all-start = ((bf16[32,16,768]{2,1,0:T(8,128)(2,1)}), bf16[32,16,768]{2,1,0:T(8,128)(2,1)}, u32[]{:S(2)}, u32[]{:S(2)}) async-start(bf16[32,16,768]{2,1,0:T(8,128)(2,1)} %bitcast.6), calls=%async_computation | async-start | bytes 1572864 | tf_op jit(solution)/shard_map/all_to_all | solution.py:430
  12.1 1.2 %copy-done = bf16[8,4,16,768]{3,2,1,0:T(8,128)(2,1)S(1)} copy-done((bf16[8,4,16,768]{3,2,1,0:T(8,128)(2,1)S(1)}, bf16[8,4,16,768]{3,2,1,0:T(8,128)(2,1)}, u32[]{:S(2)}) %copy-start) | copy-done | bytes 786456
  13.3 0.1 part.1
  13.4 0.3 collective-permute-start
  13.6 1.7 %collective-permute-start.1 = (bf16[8,16,768]{2,1,0:T(8,128)(2,1)S(1)}, bf16[8,16,768]{2,1,0:T(8,128)(2,1)S(1)}, u32[]{:S(2)}, u32[]{:S(2)}) collective-permute-start(bf16[8,16,768]{2,1,0:T(8,128)(2,1)S(1)} %get-tuple-element.30), channel_id=1, source_target_pairs={{0,16},{8,24},{16,0},{24,8},{1,17},{9,25},{17,1},{25,9},{2,18},{10... | collective-permute-start | bytes 589832 | tf_op jit(solution)/shard_map/ppermute | solution.py:412
  15.3 2.0 %fetch.1.weight_ref.refs_4_ = bf16[768,2304]{1,0:T(8,128)(2,1)S(1)} custom-call(bf16[768,2304]{1,0:T(8,128)(2,1)} %source.1, bf16[8,16,768]{2,1,0:T(8,128)(2,1)S(1)} %get-tuple-element.28.after), custom_call_target="tpu_custom_call" | custom-call | bytes 8000000 | tf_op jit(solution)/shard_map/fetch/pallas_call | solution.py:133
  17.4 0.7 %copy-done.5 = bf16[8,16,768]{2,1,0:T(8,128)(2,1)} copy-done((bf16[8,16,768]{2,1,0:T(8,128)(2,1)}, bf16[8,16,768]{2,1,0:T(8,128)(2,1)S(1)}, u32[]{:S(2)}) %copy-start.5) | copy-done | bytes 196632
  18.1 8.6 %collective-permute-done.1 = bf16[8,16,768]{2,1,0:T(8,128)(2,1)S(1)} collective-permute-done((bf16[8,16,768]{2,1,0:T(8,128)(2,1)S(1)}, bf16[8,16,768]{2,1,0:T(8,128)(2,1)S(1)}, u32[]{:S(2)}, u32[]{:S(2)}) %collective-permute-start.1) | collective-permute-done | bytes 196640 | tf_op jit(solution)/shard_map/ppermute | solution.py:412
  26.6 0.7 %copy-done.7 = bf16[8,16,768]{2,1,0:T(8,128)(2,1)} copy-done((bf16[8,16,768]{2,1,0:T(8,128)(2,1)}, bf16[8,16,768]{2,1,0:T(8,128)(2,1)S(1)}, u32[]{:S(2)}) %copy-start.7) | copy-done | bytes 196632
  27.3 2.9 %collective-permute-done.2 = bf16[8,16,768]{2,1,0:T(8,128)(2,1)S(1)} collective-permute-done((bf16[8,16,768]{2,1,0:T(8,128)(2,1)S(1)}, bf16[8,16,768]{2,1,0:T(8,128)(2,1)S(1)}, u32[]{:S(2)}, u32[]{:S(2)}) %collective-permute-start.2) | collective-permute-done | bytes 196640 | tf_op jit(solution)/shard_map/ppermute | solution.py:412
  30.2 0.7 %copy-done.9 = bf16[8,16,768]{2,1,0:T(8,128)(2,1)} copy-done((bf16[8,16,768]{2,1,0:T(8,128)(2,1)}, bf16[8,16,768]{2,1,0:T(8,128)(2,1)S(1)}, u32[]{:S(2)}) %copy-start.9) | copy-done | bytes 196632
  30.9 1.9 %all-to-all-done = bf16[32,16,768]{2,1,0:T(8,128)(2,1)} async-done(((bf16[32,16,768]{2,1,0:T(8,128)(2,1)}), bf16[32,16,768]{2,1,0:T(8,128)(2,1)}, u32[]{:S(2)}, u32[]{:S(2)}) %all-to-all-start) | async-done | bytes 786464 | tf_op jit(solution)/shard_map/all_to_all | solution.py:430
  32.8 7.2 %dilated.1 = (bf16[1,400,128]{2,1,0:T(8,128)(2,1)S(1)}, bf16[1,400,128]{2,1,0:T(8,128)(2,1)S(1)}, bf16[1,400,128]{2,1,0:T(8,128)(2,1)S(1)}, bf16[1,400,128]{2,1,...) custom-call(s32[4]{0:T(128)S(1)} %copy-done.4, ...), custom_call_target="tpu_custom_call" | custom-call | flops 1000000 | bytes 10000 | tf_op jit(solution)/shard_map/dilated/pallas_call | solution.py:279
  40.0 1.5 %collective-permute-start.7 = (bf16[2,400,128]{2,1,0:T(8,128)(2,1)S(1)}, bf16[2,400,128]{2,1,0:T(8,128)(2,1)S(1)}, u32[]{:S(2)}, u32[]{:S(2)}) collective-permute-start(bf16[2,400,128]{2,1,0:T(8,128)(2,1)S(1)} %get-tuple-element.48), channel_id=1, source_target_pairs={{0,2},{1,3},{2,0},{3,1},{4,6},{5,7},{6,4},{7,5},{8,10},{9,11},{10,... | collective-permute-start | bytes 614408 | tf_op jit(solution)/shard_map/ppermute | solution.py:412
  41.4 2.8 %collective-permute-start.3 = (bf16[1,400,128]{2,1,0:T(8,128)(2,1)S(1)}, bf16[1,400,128]{2,1,0:T(8,128)(2,1)S(1)}, u32[]{:S(2)}, u32[]{:S(2)}) collective-permute-start(bf16[1,400,128]{2,1,0:T(8,128)(2,1)S(1)} %get-tuple-element.44), channel_id=1, source_target_pairs={{0,5},{1,4},{2,7},{3,6},{4,1},{5,0},{6,3},{7,2},{8,13},{9,12},{10,... | collective-permute-start | bytes 307208 | tf_op jit(solution)/shard_map/ppermute | solution.py:412
  44.2 0.5 collective-permute-start.4
  44.8 2.2 %collective-permute-start.5 = (bf16[1,400,128]{2,1,0:T(8,128)(2,1)S(1)}, bf16[1,400,128]{2,1,0:T(8,128)(2,1)S(1)}, u32[]{:S(2)}, u32[]{:S(2)}) collective-permute-start(bf16[1,400,128]{2,1,0:T(8,128)(2,1)S(1)} %get-tuple-element.46), channel_id=1, source_target_pairs={{0,7},{1,6},{2,5},{3,4},{4,3},{5,2},{6,1},{7,0},{8,15},{9,14},{10,... | collective-permute-start | bytes 307208 | tf_op jit(solution)/shard_map/ppermute | solution.py:412
  47.0 2.1 %collective-permute-start.6 = (bf16[1,400,128]{2,1,0:T(8,128)(2,1)S(1)}, bf16[1,400,128]{2,1,0:T(8,128)(2,1)S(1)}, u32[]{:S(2)}, u32[]{:S(2)}) collective-permute-start(bf16[1,400,128]{2,1,0:T(8,128)(2,1)S(1)} %get-tuple-element.47), channel_id=1, source_target_pairs={{0,6},{1,7},{2,4},{3,5},{4,2},{5,3},{6,0},{7,1},{8,14},{9,15},{10,... | collective-permute-start | bytes 307208 | tf_op jit(solution)/shard_map/ppermute | solution.py:412
  49.1 0.6 collective-permute-done.7.refs_0_
  49.7 2.4 %collective-permute-start.8 = (bf16[2,400,128]{2,1,0:T(8,128)(2,1)S(1)}, bf16[2,400,128]{2,1,0:T(8,128)(2,1)S(1)}, u32[]{:S(2)}, u32[]{:S(2)}) collective-permute-start(bf16[2,400,128]{2,1,0:T(8,128)(2,1)S(1)} %pad_maximum_fusion), channel_id=1, source_target_pairs={{0,1},{1,0},{2,3},{3,2},{4,5},{5,4},{6,7},{7,6},{8,9},{9,8},{10,11... | collective-permute-start | bytes 614408 | tf_op jit(solution)/shard_map/ppermute | solution.py:412
  52.1 6.5 %local.1 = (bf16[512,768]{1,0:T(8,128)(2,1)S(1)}, f32[512,128]{1,0:T(8,128)S(1)}) custom-call(s32[4]{0:T(128)S(1)} %copy-done.4, bf16[128,768]{1,0:T(8,128)(2,1)S(1)} %bitcast.7, bf16[128,768]{1,0:T(8,128)(2,1)S(1)} %bitcast.8, bf16[128,768]{1,0:T(8,128)(2,1)S(1)} %bitcast.9, bf16[128,768]{1,0:T(8,128)(2,1)S(1)} %bitcast.10, ...), custom_call_target="tpu_custom_call" | custom-call | flops 8000000000 | bytes 10000000 | tf_op jit(solution)/shard_map/local/pallas_call | solution.py:216
  58.7 1.8 %merge.2.refs_4_ = bf16[512,768]{1,0:T(8,128)(2,1)S(1)} custom-call(s32[4]{0:T(128)S(1)} %copy-done.4, bf16[512,768]{1,0:T(8,128)(2,1)S(1)} %get-tuple-element.42.out_ref, f32[512,128]{1,0:T(8,128)S(1)} %get-tuple-element.43.log_ref, bf16[768,768]{1,0:T(8,128)(2,1)S(1)} %copy-done.1, bf16[2,400,128]{2,1,0:T(8,128)(2,1)S(1)} %collective-permute-done.7.refs_0_, ...), custom_call_target="tpu_custom_call" | custom-call | flops 1000000 | bytes 10000 | tf_op jit(solution)/shard_map/merge/pallas_call | solution.py:391
  60.5 2.5 %merge.3 = bf16[1,512,768]{2,1,0:T(8,128)(2,1)} custom-call(s32[4]{0:T(128)S(1)} %copy-done.4, bf16[512,768]{1,0:T(8,128)(2,1)S(1)} %get-tuple-element.42.out_ref, f32[512,128]{1,0:T(8,128)S(1)} %get-tuple-element.43.log_ref, bf16[768,768]{1,0:T(8,128)(2,1)S(1)} %copy-done.1, bf16[1,400,128]{2,1,0:T(8,128)(2,1)S(1)} %collective-permute-done.3.refs_0_, ...), custom_call_target="tpu_custom_call" | custom-call | flops 1000000 | bytes 10000 | tf_op jit(solution)/shard_map/merge/pallas_call | solution.py:391
  (27 shorter events, 0.1 us)
Async XLA Ops:
  4.7 28.0 %all-to-all-start = ((bf16[32,16,768]{2,1,0:T(8,128)(2,1)}), bf16[32,16,768]{2,1,0:T(8,128)(2,1)}, u32[]{:S(2)}, u32[]{:S(2)}) async-start(bf16[32,16,768]{2,1,0:T(8,128)(2,1)} %bitcast.6), calls=%async_computation | async-start | bytes 1572864 | tf_op jit(solution)/shard_map/all_to_all | solution.py:430
  12.1 1.2 %copy-start = (bf16[8,4,16,768]{3,2,1,0:T(8,128)(2,1)S(1)}, bf16[8,4,16,768]{3,2,1,0:T(8,128)(2,1)}, u32[]{:S(2)}) copy-start(bf16[8,4,16,768]{3,2,1,0:T(8,128)(2,1)} %embed.1.by_residue) | copy-start | bytes 2359300
  13.3 4.0 %copy-start.2 = (bf16[8,16,768]{2,1,0:T(8,128)(2,1)}, bf16[8,16,768]{2,1,0:T(8,128)(2,1)S(1)}, u32[]{:S(2)}) copy-start(bf16[8,16,768]{2,1,0:T(8,128)(2,1)S(1)} %get-tuple-element.28.after) | copy-start | bytes 589828
  13.4 4.0 %collective-permute-start = (bf16[8,16,768]{2,1,0:T(8,128)(2,1)S(1)}, bf16[8,16,768]{2,1,0:T(8,128)(2,1)S(1)}, u32[]{:S(2)}, u32[]{:S(2)}) collective-permute-start(bf16[8,16,768]{2,1,0:T(8,128)(2,1)S(1)} %get-tuple-element.29), channel_id=1, source_target_pairs={{0,8},{8,0},{16,24},{24,16},{1,9},{9,1},{17,25},{25,17},{2,10},{10... | collective-permute-start | bytes 589832 | tf_op jit(solution)/shard_map/ppermute | solution.py:412
  13.6 13.0 %collective-permute-start.1 = (bf16[8,16,768]{2,1,0:T(8,128)(2,1)S(1)}, bf16[8,16,768]{2,1,0:T(8,128)(2,1)S(1)}, u32[]{:S(2)}, u32[]{:S(2)}) collective-permute-start(bf16[8,16,768]{2,1,0:T(8,128)(2,1)S(1)} %get-tuple-element.30), channel_id=1, source_target_pairs={{0,16},{8,24},{16,0},{24,8},{1,17},{9,25},{17,1},{25,9},{2,18},{10... | collective-permute-start | bytes 589832 | tf_op jit(solution)/shard_map/ppermute | solution.py:412
  15.3 14.9 %collective-permute-start.2 = (bf16[8,16,768]{2,1,0:T(8,128)(2,1)S(1)}, bf16[8,16,768]{2,1,0:T(8,128)(2,1)S(1)}, u32[]{:S(2)}, u32[]{:S(2)}) collective-permute-start(bf16[8,16,768]{2,1,0:T(8,128)(2,1)S(1)} %get-tuple-element.31), channel_id=1, source_target_pairs={{0,24},{8,16},{16,8},{24,0},{1,25},{9,17},{17,9},{25,1},{2,26},{10... | collective-permute-start | bytes 589832 | tf_op jit(solution)/shard_map/ppermute | solution.py:412
  15.3 17.4 %copy-start.4 = (s32[4]{0:T(128)S(1)}, s32[4]{0:T(128)}, u32[]{:S(2)}) copy-start(s32[4]{0:T(128)} %counts_ref.7) | copy-start | bytes 52
  17.4 0.7 %copy-start.5 = (bf16[8,16,768]{2,1,0:T(8,128)(2,1)}, bf16[8,16,768]{2,1,0:T(8,128)(2,1)S(1)}, u32[]{:S(2)}) copy-start(bf16[8,16,768]{2,1,0:T(8,128)(2,1)S(1)} %collective-permute-done) | copy-start | bytes 589828
  26.6 0.7 %copy-start.7 = (bf16[8,16,768]{2,1,0:T(8,128)(2,1)}, bf16[8,16,768]{2,1,0:T(8,128)(2,1)S(1)}, u32[]{:S(2)}) copy-start(bf16[8,16,768]{2,1,0:T(8,128)(2,1)S(1)} %collective-permute-done.1) | copy-start | bytes 589828
  30.2 0.7 %copy-start.9 = (bf16[8,16,768]{2,1,0:T(8,128)(2,1)}, bf16[8,16,768]{2,1,0:T(8,128)(2,1)S(1)}, u32[]{:S(2)}) copy-start(bf16[8,16,768]{2,1,0:T(8,128)(2,1)S(1)} %collective-permute-done.2) | copy-start | bytes 589828
  32.7 19.4 %copy-start.3 = (bf16[8,16,768]{2,1,0:T(8,128)(2,1)S(1)}, bf16[8,16,768]{2,1,0:T(8,128)(2,1)}, u32[]{:S(2)}) copy-start(bf16[8,16,768]{2,1,0:T(8,128)(2,1)} %copy-done.2) | copy-start | bytes 589828
  32.7 19.4 %copy-start.6 = (bf16[8,16,768]{2,1,0:T(8,128)(2,1)S(1)}, bf16[8,16,768]{2,1,0:T(8,128)(2,1)}, u32[]{:S(2)}) copy-start(bf16[8,16,768]{2,1,0:T(8,128)(2,1)} %copy-done.5) | copy-start | bytes 589828
  32.7 19.4 %copy-start.8 = (bf16[8,16,768]{2,1,0:T(8,128)(2,1)S(1)}, bf16[8,16,768]{2,1,0:T(8,128)(2,1)}, u32[]{:S(2)}) copy-start(bf16[8,16,768]{2,1,0:T(8,128)(2,1)} %copy-done.7) | copy-start | bytes 589828
  32.7 19.4 %copy-start.10 = (bf16[8,16,768]{2,1,0:T(8,128)(2,1)S(1)}, bf16[8,16,768]{2,1,0:T(8,128)(2,1)}, u32[]{:S(2)}) copy-start(bf16[8,16,768]{2,1,0:T(8,128)(2,1)} %copy-done.9) | copy-start | bytes 589828
  40.0 9.7 %collective-permute-start.7 = (bf16[2,400,128]{2,1,0:T(8,128)(2,1)S(1)}, bf16[2,400,128]{2,1,0:T(8,128)(2,1)S(1)}, u32[]{:S(2)}, u32[]{:S(2)}) collective-permute-start(bf16[2,400,128]{2,1,0:T(8,128)(2,1)S(1)} %get-tuple-element.48), channel_id=1, source_target_pairs={{0,2},{1,3},{2,0},{3,1},{4,6},{5,7},{6,4},{7,5},{8,10},{9,11},{10,... | collective-permute-start | bytes 614408 | tf_op jit(solution)/shard_map/ppermute | solution.py:412
  41.4 19.0 %collective-permute-start.3 = (bf16[1,400,128]{2,1,0:T(8,128)(2,1)S(1)}, bf16[1,400,128]{2,1,0:T(8,128)(2,1)S(1)}, u32[]{:S(2)}, u32[]{:S(2)}) collective-permute-start(bf16[1,400,128]{2,1,0:T(8,128)(2,1)S(1)} %get-tuple-element.44), channel_id=1, source_target_pairs={{0,5},{1,4},{2,7},{3,6},{4,1},{5,0},{6,3},{7,2},{8,13},{9,12},{10,... | collective-permute-start | bytes 307208 | tf_op jit(solution)/shard_map/ppermute | solution.py:412
  44.2 16.3 %collective-permute-start.4 = (bf16[1,400,128]{2,1,0:T(8,128)(2,1)S(1)}, bf16[1,400,128]{2,1,0:T(8,128)(2,1)S(1)}, u32[]{:S(2)}, u32[]{:S(2)}) collective-permute-start(bf16[1,400,128]{2,1,0:T(8,128)(2,1)S(1)} %get-tuple-element.45), channel_id=1, source_target_pairs={{0,4},{1,5},{2,6},{3,7},{4,0},{5,1},{6,2},{7,3},{8,12},{9,13},{10,... | collective-permute-start | bytes 307208 | tf_op jit(solution)/shard_map/ppermute | solution.py:412
  44.8 15.7 %collective-permute-start.5 = (bf16[1,400,128]{2,1,0:T(8,128)(2,1)S(1)}, bf16[1,400,128]{2,1,0:T(8,128)(2,1)S(1)}, u32[]{:S(2)}, u32[]{:S(2)}) collective-permute-start(bf16[1,400,128]{2,1,0:T(8,128)(2,1)S(1)} %get-tuple-element.46), channel_id=1, source_target_pairs={{0,7},{1,6},{2,5},{3,4},{4,3},{5,2},{6,1},{7,0},{8,15},{9,14},{10,... | collective-permute-start | bytes 307208 | tf_op jit(solution)/shard_map/ppermute | solution.py:412
  47.0 13.5 %collective-permute-start.6 = (bf16[1,400,128]{2,1,0:T(8,128)(2,1)S(1)}, bf16[1,400,128]{2,1,0:T(8,128)(2,1)S(1)}, u32[]{:S(2)}, u32[]{:S(2)}) collective-permute-start(bf16[1,400,128]{2,1,0:T(8,128)(2,1)S(1)} %get-tuple-element.47), channel_id=1, source_target_pairs={{0,6},{1,7},{2,4},{3,5},{4,2},{5,3},{6,0},{7,1},{8,14},{9,15},{10,... | collective-permute-start | bytes 307208 | tf_op jit(solution)/shard_map/ppermute | solution.py:412
  49.7 8.9 %copy-start.1 = (bf16[768,768]{1,0:T(8,128)(2,1)S(1)}, bf16[768,768]{1,0:T(8,128)(2,1)}, u32[]{:S(2)}) copy-start(bf16[768,768]{1,0:T(8,128)(2,1)} %weight_ref.3) | copy-start | bytes 3538948
  49.7 8.9 %collective-permute-start.8 = (bf16[2,400,128]{2,1,0:T(8,128)(2,1)S(1)}, bf16[2,400,128]{2,1,0:T(8,128)(2,1)S(1)}, u32[]{:S(2)}, u32[]{:S(2)}) collective-permute-start(bf16[2,400,128]{2,1,0:T(8,128)(2,1)S(1)} %pad_maximum_fusion), channel_id=1, source_target_pairs={{0,1},{1,0},{2,3},{3,2},{4,5},{5,4},{6,7},{7,6},{8,9},{9,8},{10,11... | collective-permute-start | bytes 614408 | tf_op jit(solution)/shard_map/ppermute | solution.py:412
